TPU v7x, 128 devices: a whole 4x4x4 slice. The times are simulated.
128 devices in a mesh: section: 4 (over z), ctx: 16 (over x_hi, y, core), mirror: 2 (over x_lo).
Axes of the slice: x: 4 (x_hi: 2, x_lo: 2; x = x_hi * 2 + x_lo), y: 4, z: 4, core: 2. Of those that a mesh axis runs over, the one named last changes fastest.
Arguments:
- queries: bfloat16 [4, 2, 4096, 2048], P('section', 'mirror', 'ctx'), may hold values from -480 to 480
- saved_keys: bfloat16 [4, 2, 4096, 1024], P('section', 'mirror', 'ctx'), may hold values from -6 to 6
- saved_values: bfloat16 [4, 2, 4096, 1024], P('section', 'mirror', 'ctx'), may hold values from -6 to 6
- output_gradient: bfloat16 [4, 2, 4096, 2048], P('section', 'mirror', 'ctx'), may hold values from -96 to 96
- layer_input: bfloat16 [4, 2, 4096, 4608], P('section', 'mirror', 'ctx'), may hold values from -0.375 to 0.375
- hadamard_signs: int32 [4, 1024], replicated, may hold values from -1 to 1, as said below
Outputs:
- query_gradient: bfloat16 [4, 2, 4096, 2048], P('section', 'mirror', 'ctx')
- key_gradient: bfloat16 [4, 2, 4096, 1024], P('section', 'mirror', 'ctx')
- value_gradient: bfloat16 [4, 2, 4096, 1024], P('section', 'mirror', 'ctx')
- rotated_grad: float32 [4, 4608, 1024], P('section', ('ctx', 'mirror'))
Inputs may be any that keep to these rules, and one draw needn't show every extreme that they name: `hadamard_signs`: every entry is -1 or +1.
All inputs are finite; a program needn't handle non-finite values.
Results may differ from a plain program's by a relative error of at most 0.022.
Values may be sent and summed in bfloat16 or wider, within the bound.
No kernel may reach another device: no remote copies, remote signals or barrier semaphores. Data moves between devices by JAX's collectives and lax.ppermute only.
A program may use at most 192 MiB of HBM per device.

v0:
```python
import math

import jax
import jax.numpy as jnp
from jax import lax
from jax.sharding import PartitionSpec as P

QUERY_HEADS = 16
KEY_VALUE_HEADS = 8
HEAD_SIZE = 128
WINDOW = 2048


score_scale = 144.0 ** (-0.5)
softcap = 50.0


def passed_along(block, axis, distance):
    devices = range(lax.axis_size(axis))
    route = [(i - distance, i) for i in devices if i - distance in devices]
    return lax.ppermute(block, axis, route)


def partner(array, axis, distance):
    return lax.ppermute(array, axis, [(i, i ^ 1 << distance) for i in range(lax.axis_size(axis))])


def hadamard(order_size):
    positions = jnp.arange(order_size, dtype=jnp.int32)
    parity = jnp.zeros((order_size, order_size), jnp.int32)
    for bit_level in range(order_size.bit_length() - 1):
        digit_row = positions // 2**bit_level % 2
        parity = parity + digit_row[:, None] * digit_row[None, :]
    return (1 - 2 * (parity % 2)).astype(jnp.float32)


def group_grads(queries, saved_keys, saved_values, output_gradient, first_key):
    row_number = queries.shape[0]
    key_number = saved_keys.shape[0]
    window_rows = key_number - row_number
    query_place = jnp.arange(row_number, dtype=jnp.int32)[:, None]
    key_place = jnp.arange(key_number, dtype=jnp.int32)[None, :]
    distance = query_place + window_rows - key_place
    allowed = (distance >= 0) & (distance < window_rows) & (key_place >= first_key)
    raw_score = (
        jnp.einsum("rgd,ld->grl", queries, saved_keys, preferred_element_type=jnp.float32)
        * score_scale
    )
    capped = jnp.tanh(raw_score / softcap)
    weights = jnp.where(allowed[None], jnp.exp(softcap * capped), 0.0)
    probability = weights / jnp.sum(weights, axis=2, keepdims=True)
    prob_low = probability.astype(jnp.bfloat16)
    attended = jnp.einsum("grl,ld->rgd", prob_low, saved_values, preferred_element_type=jnp.float32)
    row_delta = jnp.sum(output_gradient.astype(jnp.float32) * attended, axis=2)
    prob_grad = jnp.einsum(
        "rgd,ld->grl", output_gradient, saved_values, preferred_element_type=jnp.float32
    )
    score_grad = (
        probability
        * (prob_grad - jnp.transpose(row_delta)[:, :, None])
        * (1.0 - capped * capped)
        * score_scale
    )
    score_low = score_grad.astype(jnp.bfloat16)
    query_gradient = jnp.einsum(
        "grl,ld->rgd", score_low, saved_keys, preferred_element_type=jnp.float32
    )
    key_gradient = jnp.einsum("grl,rgd->ld", score_low, queries, preferred_element_type=jnp.float32)
    value_gradient = jnp.einsum(
        "grl,rgd->ld", prob_low, output_gradient, preferred_element_type=jnp.float32
    )
    return (query_gradient, key_gradient, value_gradient)


def layer_grads(queries, saved_keys, saved_values, output_gradient, first_key):
    row_number = queries.shape[0]
    key_number = saved_keys.shape[0]
    query_heads = queries.reshape(
        row_number, KEY_VALUE_HEADS, QUERY_HEADS // KEY_VALUE_HEADS, HEAD_SIZE
    ).transpose(1, 0, 2, 3)
    gradient_heads = output_gradient.reshape(
        row_number, KEY_VALUE_HEADS, QUERY_HEADS // KEY_VALUE_HEADS, HEAD_SIZE
    ).transpose(1, 0, 2, 3)
    key_heads = saved_keys.reshape(key_number, KEY_VALUE_HEADS, HEAD_SIZE).transpose(1, 0, 2)
    value_heads = saved_values.reshape(key_number, KEY_VALUE_HEADS, HEAD_SIZE).transpose(1, 0, 2)

    def one_group(members):
        return group_grads(members[0], members[1], members[2], members[3], first_key)

    query_gradient, key_gradient, value_gradient = lax.map(
        one_group, (query_heads, key_heads, value_heads, gradient_heads)
    )
    return (
        query_gradient.transpose(1, 0, 2, 3).reshape(row_number, QUERY_HEADS * HEAD_SIZE),
        key_gradient.transpose(1, 0, 2).reshape(key_number, KEY_VALUE_HEADS * HEAD_SIZE),
        value_gradient.transpose(1, 0, 2).reshape(key_number, KEY_VALUE_HEADS * HEAD_SIZE),
    )


def turn_block(input_rows, grad_rows, sign_row):
    key_value_width = grad_rows.shape[1]
    outer_size = 2 ** ((key_value_width.bit_length() - 1) // 2)
    inner_size = key_value_width // outer_size
    partial_t = lax.dot_general(
        grad_rows, input_rows, (((0,), (0,)), ((), ())), preferred_element_type=jnp.float32
    )
    signed = (partial_t * sign_row[:, None]).reshape(outer_size, inner_size, input_rows.shape[1])
    inner_turn = jnp.einsum(
        "abd,bc->acd", signed, hadamard(inner_size), precision=lax.Precision.HIGHEST
    )
    outer_turn = jnp.einsum(
        "acd,ae->ecd", inner_turn, hadamard(outer_size), precision=lax.Precision.HIGHEST
    )
    return (
        outer_turn.reshape(key_value_width, input_rows.shape[1])
        * (1.0 / math.sqrt(key_value_width))
    ).astype(jnp.bfloat16)


def body(queries, saved_keys, saved_values, output_gradient, layer_input, hadamard_signs):
    own_query = queries[0, 0]
    own_grad_out = output_gradient[0, 0]
    own_input = layer_input[0, 0]
    row_number = own_query.shape[0]
    span_blocks = WINDOW // row_number
    reach_blocks = min(span_blocks, lax.axis_size("ctx") - 1)
    ctx_index = lax.axis_index("ctx")
    kv_own = jnp.stack([saved_keys[0, 0], saved_values[0, 0]])
    blocks = []
    for distance in range(1, reach_blocks + 1):
        blocks.append(passed_along(kv_own, "ctx", distance))
    zero_block = jnp.zeros_like(kv_own)
    blocks = blocks + [zero_block] * (span_blocks - reach_blocks)
    ordered = blocks[::-1] + [kv_own]
    kv_all = jnp.concatenate(ordered, axis=1)
    first_key = (span_blocks - ctx_index) * row_number
    query_gradient, key_gradient, value_gradient = layer_grads(
        own_query, kv_all[0], kv_all[1], own_grad_out, first_key
    )
    grad_all = jnp.stack([key_gradient, value_gradient])

    def piece_at(distance):
        begin_row = (span_blocks - distance) * row_number
        return grad_all[:, begin_row : begin_row + row_number]

    own_total = piece_at(0)
    for distance in range(1, reach_blocks + 1):
        own_total = own_total + passed_along(
            piece_at(distance).astype(jnp.bfloat16), "ctx", -distance
        ).astype(jnp.float32)
    key_low = own_total[0].astype(jnp.bfloat16)
    value_low = own_total[1].astype(jnp.bfloat16)
    section_index = lax.axis_index("section")
    mirror_index = lax.axis_index("mirror")
    section_count = lax.axis_size("section")
    flip_bits = section_count.bit_length() - 1
    layer_index = jnp.where(mirror_index == 0, section_index, section_count - 1 - section_index)
    sign_row = lax.dynamic_index_in_dim(hadamard_signs, layer_index, 0, keepdims=False).astype(
        jnp.float32
    )
    turned = turn_block(own_input, value_low, sign_row)
    summed = lax.psum_scatter(turned, "ctx", scatter_dimension=1, tiled=True).astype(jnp.float32)
    flipped = summed
    for bit_index in range(flip_bits):
        flipped = partner(flipped.astype(jnp.bfloat16), "section", bit_index).astype(flipped.dtype)
    paired = jnp.where(mirror_index == 0, summed, flipped)
    result = lax.psum_scatter(
        paired.astype(jnp.bfloat16), "mirror", scatter_dimension=1, tiled=True
    ).astype(jnp.float32)
    return (
        query_gradient.astype(jnp.bfloat16)[None, None],
        key_low[None, None],
        value_low[None, None],
        jnp.transpose(result)[None],
    )


def solution(mesh):
    return jax.shard_map(
        body,
        mesh=mesh,
        in_specs=(
            P("section", "mirror", "ctx", None),
            P("section", "mirror", "ctx", None),
            P("section", "mirror", "ctx", None),
            P("section", "mirror", "ctx", None),
            P("section", "mirror", "ctx", None),
            P(),
        ),
        out_specs=(
            P("section", "mirror", "ctx", None),
            P("section", "mirror", "ctx", None),
            P("section", "mirror", "ctx", None),
            P("section", ("ctx", "mirror"), None),
        ),
        check_vma=False,
    )
```

profile of v0, /device:TPU:2, one launch (start us, length us, event | category | flops | bytes accessed | tf_op | source)
XLA Modules:
  0.0 906.0 jit_solution(12042865112919276453)
XLA Ops:
  28.9 9.9 %collective-permute-done = bf16[2,256,1024]{1,2,0:T(8,128)(2,1)} collective-permute-done((bf16[2,256,1024]{1,2,0:T(8,128)(2,1)}, bf16[2,256,1024]{1,2,0:T(8,128)(2,1)}, u32[]{:S(2)}, u32[]{:S(2)}) %collective-permute-start) | collective-permute-done | bytes 1048608 | tf_op jit(solution)/shard_map/ppermute | solution.py:21
  41.1 46.3 %collective-permute-done.1 = bf16[2,256,1024]{1,2,0:T(8,128)(2,1)} collective-permute-done((bf16[2,256,1024]{1,2,0:T(8,128)(2,1)}, bf16[2,256,1024]{1,2,0:T(8,128)(2,1)}, u32[]{:S(2)}, u32[]{:S(2)}) %collective-permute-start.1) | collective-permute-done | bytes 1048608 | tf_op jit(solution)/shard_map/ppermute | solution.py:21
  89.7 20.1 %collective-permute-done.2 = bf16[2,256,1024]{1,2,0:T(8,128)(2,1)} collective-permute-done((bf16[2,256,1024]{1,2,0:T(8,128)(2,1)}, bf16[2,256,1024]{1,2,0:T(8,128)(2,1)}, u32[]{:S(2)}, u32[]{:S(2)}) %collective-permute-start.2) | collective-permute-done | bytes 1048608 | tf_op jit(solution)/shard_map/ppermute | solution.py:21
  144.9 199.9 %while.16 = (s32[]{:T(128)}, bf16[8,256,2,128]{1,3,2,0:T(8,128)(2,1)}, f32[8,2304,128]{2,1,0:T(8,128)}, f32[8,2304,128]{2,1,0:T(8,128)}, bf16[8,2304,128]{1,2,0:...) while((s32[]{:T(128)}, ...), condition=%wide.region_3.4_spmd, body=%wide.region_0.3_spmd.sunk | while | flops 1836320256 | bytes 65165476 | solution.py:90
  344.9 14.7 %copy.50 = f32[2304,8,128]{2,1,0:T(8,128)} copy(f32[2304,8,128]{2,0,1:T(8,128)} %bitcast.190) | data formatting | bytes 18874368 | tf_op jit(solution)/shard_map/transpose | solution.py:95
  359.5 11.1 %stack_reshape.6 = f32[1,2304,1024]{2,1,0:T(8,128)} reshape(f32[2304,8,128]{2,1,0:T(8,128)} %copy.50) | data formatting | bytes 18874368 | tf_op jit(solution)/shard_map/stack;reshape | solution.py:140
  370.7 9.3 %constant_dynamic-update-slice_fusion.10 = f32[2,2304,1024]{2,1,0:T(8,128)} fusion(f32[1,2304,1024]{2,1,0:T(8,128)} %stack_reshape.6), kind=kLoop, calls=%fused_computation.83 | loop fusion | bytes 18874368
  380.0 14.6 %copy.51 = f32[2304,8,128]{2,1,0:T(8,128)} copy(f32[2304,8,128]{2,0,1:T(8,128)} %bitcast.191) | data formatting | bytes 18874368 | tf_op jit(solution)/shard_map/transpose | solution.py:96
  394.6 11.1 %stack_reshape.7 = f32[1,2304,1024]{2,1,0:T(8,128)} reshape(f32[2304,8,128]{2,1,0:T(8,128)} %copy.51) | data formatting | bytes 18874368 | tf_op jit(solution)/shard_map/stack;reshape | solution.py:140
  405.7 9.3 %constant_dynamic-update-slice_fusion.9 = f32[2,2304,1024]{2,1,0:T(8,128)} fusion(f32[2,2304,1024]{2,1,0:T(8,128)} %constant_dynamic-update-slice_fusion.10, f32[1,2304,1024]{2,1,0:T(8,128)} %stack_reshape.7), kind=kLoop, calls=%fused_computation.82 | loop fusion | bytes 18874368 | tf_op jit(solution)/shard_map/stack | solution.py:140
  431.3 9.6 %collective-permute-done.10 = bf16[2,256,1024]{2,1,0:T(8,128)(2,1)S(1)} collective-permute-done((bf16[2,256,1024]{2,1,0:T(8,128)(2,1)S(1)}, bf16[2,256,1024]{2,1,0:T(8,128)(2,1)S(1)}, u32[]{:S(2)}, u32[]{:S(2)}) %collective-permute-start.10) | collective-permute-done | bytes 1048608 | tf_op jit(solution)/shard_map/ppermute | solution.py:21
  442.2 23.5 %collective-permute-done.11 = bf16[2,256,1024]{2,1,0:T(8,128)(2,1)S(1)} collective-permute-done((bf16[2,256,1024]{2,1,0:T(8,128)(2,1)S(1)}, bf16[2,256,1024]{2,1,0:T(8,128)(2,1)S(1)}, u32[]{:S(2)}, u32[]{:S(2)}) %collective-permute-start.11) | collective-permute-done | bytes 1048608 | tf_op jit(solution)/shard_map/ppermute | solution.py:21
  467.0 12.1 %collective-permute-done.12 = bf16[2,256,1024]{2,1,0:T(8,128)(2,1)S(1)} collective-permute-done((bf16[2,256,1024]{2,1,0:T(8,128)(2,1)S(1)}, bf16[2,256,1024]{2,1,0:T(8,128)(2,1)S(1)}, u32[]{:S(2)}, u32[]{:S(2)}) %collective-permute-start.12) | collective-permute-done | bytes 1048608 | tf_op jit(solution)/shard_map/ppermute | solution.py:21
  482.4 33.3 %collective-permute-done.13 = bf16[2,256,1024]{2,1,0:T(8,128)(2,1)} collective-permute-done((bf16[2,256,1024]{2,1,0:T(8,128)(2,1)}, bf16[2,256,1024]{2,1,0:T(8,128)(2,1)}, u32[]{:S(2)}, u32[]{:S(2)}) %collective-permute-start.13) | collective-permute-done | bytes 1048608 | tf_op jit(solution)/shard_map/ppermute | solution.py:21
  515.7 8.4 collective-permute-done.14
  524.1 97.2 %collective-permute-done.15 = bf16[2,256,1024]{2,1,0:T(8,128)(2,1)} collective-permute-done((bf16[2,256,1024]{2,1,0:T(8,128)(2,1)}, bf16[2,256,1024]{2,1,0:T(8,128)(2,1)}, u32[]{:S(2)}, u32[]{:S(2)}) %collective-permute-start.15) | collective-permute-done | bytes 1048608 | tf_op jit(solution)/shard_map/ppermute | solution.py:21
  630.2 19.5 %convolution_bitcast_fusion.5 = f32[32,32,4608]{2,1,0:T(8,128)} fusion(f32[32,32,4608]{2,1,0:T(8,128)S(1)} %bitcast.185, s32[32]{0:T(128)S(1)} %get-tuple-element.180, s32[32]{0:T(128)S(1)} %get-tuple-element.181, s32[32]{0:T(128)S(1)} %get-tuple-element.182, s32[32]{0:T(128)S(1)} %get-tuple-element.183, s32[32]{0:T(128)S(1)} %and_select_fusion.8), kind=kOutput, calls=%fused_computation.52 | convolution fusion | flops 1811962880 | bytes 37749376 | tf_op jit(solution)/shard_map/abd,bc->acd/dot_general | solution.py:108
  649.7 35.2 %multiply_convert_fusion = bf16[32,32,4608]{2,0,1:T(8,128)(2,1)} fusion(f32[32,32,4608]{2,1,0:T(8,128)} %convolution_bitcast_fusion.5, s32[32]{0:T(128)S(1)} %get-tuple-element.180, s32[32]{0:T(128)S(1)} %get-tuple-element.181, s32[32]{0:T(128)S(1)} %get-tuple-element.182, s32[32]{0:T(128)S(1)} %get-tuple-element.183, s32[32]{0:T(128)S(1)} %and_select_fusion.8), kind=kOutput, calls=%fused_computation.50 | convolution fusion | flops 1821400064 | bytes 28312192 | tf_op jit(solution)/shard_map/acd,ae->ecd/dot_general | solution.py:111
  684.9 12.6 %copy.53 = bf16[32,32,4608]{2,1,0:T(8,128)(2,1)} copy(bf16[32,32,4608]{2,0,1:T(8,128)(2,1)} %multiply_convert_fusion) | data formatting | bytes 18874368 | tf_op jit(solution)/shard_map/convert_element_type | solution.py:117
  697.5 12.6 %copy.65 = bf16[1024,4608]{0,1:T(8,128)(2,1)} copy(bf16[1024,4608]{1,0:T(8,128)(2,1)} %bitcast.187) | data formatting | bytes 18874368
  710.1 132.9 %reduce-scatter.7.cloned.1.call-done = bf16[288,1024]{1,0:T(8,128)(2,1)} async-done(((bf16[4608,1024]{1,0:T(8,128)(2,1)}), bf16[288,1024]{1,0:T(8,128)(2,1)}) %reduce-scatter.7.cloned.1.call-update) | async-done | bytes 589840
  844.6 12.8 %collective-permute-done.16 = bf16[1024,288]{0,1:T(8,128)(2,1)} collective-permute-done((bf16[1024,288]{0,1:T(8,128)(2,1)}, bf16[1024,288]{0,1:T(8,128)(2,1)}, u32[]{:S(2)}, u32[]{:S(2)}) %collective-permute-start.16) | collective-permute-done | bytes 589856 | tf_op jit(solution)/shard_map/ppermute | solution.py:25
  862.6 9.8 %collective-permute-done.17 = bf16[1024,288]{0,1:T(8,128)(2,1)} collective-permute-done((bf16[1024,288]{0,1:T(8,128)(2,1)}, bf16[1024,288]{0,1:T(8,128)(2,1)}, u32[]{:S(2)}, u32[]{:S(2)}) %collective-permute-start.17) | collective-permute-done | bytes 589856 | tf_op jit(solution)/shard_map/ppermute | solution.py:25
  882.6 12.2 %reduce-scatter.9.cloned.1.call-done = bf16[144,1024]{1,0:T(8,128)(2,1)} async-done(((bf16[288,1024]{1,0:T(8,128)(2,1)}), bf16[144,1024]{1,0:T(8,128)(2,1)}) %reduce-scatter.9.cloned.1.call-update) | async-done | bytes 294928
  (200 shorter events, 313.1 us)
Async XLA Ops:
  7.2 620.4 %copy-start = (bf16[1,1,256,4608]{3,2,1,0:T(8,128)(2,1)S(1)}, bf16[1,1,256,4608]{3,2,1,0:T(8,128)(2,1)}, u32[]{:S(2)}) copy-start(bf16[1,1,256,4608]{3,2,1,0:T(8,128)(2,1)} %param.12) | copy-start | bytes 7077892
  7.2 835.8 %reduce-scatter.7.cloned.1.call-start = ((), (), s32[]{:S(2)}) async-start(), calls=%async_computation.2 | async-start | bytes 10027008
  10.9 27.9 %collective-permute-start = (bf16[2,256,1024]{1,2,0:T(8,128)(2,1)}, bf16[2,256,1024]{1,2,0:T(8,128)(2,1)}, u32[]{:S(2)}, u32[]{:S(2)}) collective-permute-start(bf16[2,256,1024]{1,2,0:T(8,128)(2,1)} %pad_maximum_fusion), channel_id=1, source_target_pairs={{0,16},{2,18},{4,20},{6,22},{8,24},{10,26},{12,28},{14,30},{1,17},... | collective-permute-start | bytes 3145736 | tf_op jit(solution)/shard_map/ppermute | solution.py:21
  15.9 71.5 %collective-permute-start.1 = (bf16[2,256,1024]{1,2,0:T(8,128)(2,1)}, bf16[2,256,1024]{1,2,0:T(8,128)(2,1)}, u32[]{:S(2)}, u32[]{:S(2)}) collective-permute-start(bf16[2,256,1024]{1,2,0:T(8,128)(2,1)} %pad_maximum_fusion), channel_id=1, source_target_pairs={{0,14},{2,16},{4,18},{6,20},{8,22},{10,24},{12,26},{14,28},{16,30}... | collective-permute-start | bytes 3145736 | tf_op jit(solution)/shard_map/ppermute | solution.py:21
  21.0 88.9 %collective-permute-start.2 = (bf16[2,256,1024]{1,2,0:T(8,128)(2,1)}, bf16[2,256,1024]{1,2,0:T(8,128)(2,1)}, u32[]{:S(2)}, u32[]{:S(2)}) collective-permute-start(bf16[2,256,1024]{1,2,0:T(8,128)(2,1)} %pad_maximum_fusion), channel_id=1, source_target_pairs={{0,12},{2,14},{4,16},{6,18},{8,20},{10,22},{12,24},{14,26},{16,28}... | collective-permute-start | bytes 3145736 | tf_op jit(solution)/shard_map/ppermute | solution.py:21
  24.1 99.7 %collective-permute-start.3 = (bf16[2,256,1024]{1,2,0:T(8,128)(2,1)}, bf16[2,256,1024]{1,2,0:T(8,128)(2,1)}, u32[]{:S(2)}, u32[]{:S(2)}) collective-permute-start(bf16[2,256,1024]{1,2,0:T(8,128)(2,1)} %pad_maximum_fusion), channel_id=1, source_target_pairs={{0,10},{2,12},{4,14},{6,16},{8,18},{10,20},{12,22},{14,24},{16,26}... | collective-permute-start | bytes 3145736 | tf_op jit(solution)/shard_map/ppermute | solution.py:21
  26.4 99.7 %collective-permute-start.4 = (bf16[2,256,1024]{1,2,0:T(8,128)(2,1)}, bf16[2,256,1024]{1,2,0:T(8,128)(2,1)}, u32[]{:S(2)}, u32[]{:S(2)}) collective-permute-start(bf16[2,256,1024]{1,2,0:T(8,128)(2,1)} %pad_maximum_fusion), channel_id=1, source_target_pairs={{0,8},{2,10},{4,12},{6,14},{8,16},{10,18},{12,20},{14,22},{16,24},... | collective-permute-start | bytes 3145736 | tf_op jit(solution)/shard_map/ppermute | solution.py:21
  38.8 89.7 %collective-permute-start.5 = (bf16[2,256,1024]{1,2,0:T(8,128)(2,1)}, bf16[2,256,1024]{1,2,0:T(8,128)(2,1)}, u32[]{:S(2)}, u32[]{:S(2)}) collective-permute-start(bf16[2,256,1024]{1,2,0:T(8,128)(2,1)} %pad_maximum_fusion), channel_id=1, source_target_pairs={{0,6},{2,8},{4,10},{6,12},{8,14},{10,16},{12,18},{14,20},{16,22},{... | collective-permute-start | bytes 3145736 | tf_op jit(solution)/shard_map/ppermute | solution.py:21
  87.4 43.5 %collective-permute-start.6 = (bf16[2,256,1024]{1,2,0:T(8,128)(2,1)}, bf16[2,256,1024]{1,2,0:T(8,128)(2,1)}, u32[]{:S(2)}, u32[]{:S(2)}) collective-permute-start(bf16[2,256,1024]{1,2,0:T(8,128)(2,1)} %pad_maximum_fusion), channel_id=1, source_target_pairs={{0,4},{2,6},{4,8},{6,10},{8,12},{10,14},{12,16},{14,18},{16,20},{1... | collective-permute-start | bytes 3145736 | tf_op jit(solution)/shard_map/ppermute | solution.py:21
  109.9 23.4 %collective-permute-start.7 = (bf16[2,256,1024]{1,2,0:T(8,128)(2,1)}, bf16[2,256,1024]{1,2,0:T(8,128)(2,1)}, u32[]{:S(2)}, u32[]{:S(2)}) collective-permute-start(bf16[2,256,1024]{1,2,0:T(8,128)(2,1)} %pad_maximum_fusion), channel_id=1, source_target_pairs={{0,2},{2,4},{4,6},{6,8},{8,10},{10,12},{12,14},{14,16},{16,18},{18... | collective-permute-start | bytes 3145736 | tf_op jit(solution)/shard_map/ppermute | solution.py:21
  337.0 3.0 copy-start.1
  424.8 16.1 %collective-permute-start.10 = (bf16[2,256,1024]{2,1,0:T(8,128)(2,1)S(1)}, bf16[2,256,1024]{2,1,0:T(8,128)(2,1)S(1)}, u32[]{:S(2)}, u32[]{:S(2)}) collective-permute-start(bf16[2,256,1024]{2,1,0:T(8,128)(2,1)S(1)} %get-tuple-element.174), channel_id=1, source_target_pairs={{6,0},{8,2},{10,4},{12,6},{14,8},{16,10},{18,12},{20,14},{22,16},{... | collective-permute-start | bytes 3145736 | tf_op jit(solution)/shard_map/ppermute | solution.py:21
  426.1 39.6 %collective-permute-start.11 = (bf16[2,256,1024]{2,1,0:T(8,128)(2,1)S(1)}, bf16[2,256,1024]{2,1,0:T(8,128)(2,1)S(1)}, u32[]{:S(2)}, u32[]{:S(2)}) collective-permute-start(bf16[2,256,1024]{2,1,0:T(8,128)(2,1)S(1)} %get-tuple-element.173), channel_id=1, source_target_pairs={{8,0},{10,2},{12,4},{14,6},{16,8},{18,10},{20,12},{22,14},{24,16},... | collective-permute-start | bytes 3145736 | tf_op jit(solution)/shard_map/ppermute | solution.py:21
  427.4 51.7 %collective-permute-start.12 = (bf16[2,256,1024]{2,1,0:T(8,128)(2,1)S(1)}, bf16[2,256,1024]{2,1,0:T(8,128)(2,1)S(1)}, u32[]{:S(2)}, u32[]{:S(2)}) collective-permute-start(bf16[2,256,1024]{2,1,0:T(8,128)(2,1)S(1)} %get-tuple-element.172), channel_id=1, source_target_pairs={{10,0},{12,2},{14,4},{16,6},{18,8},{20,10},{22,12},{24,14},{26,16}... | collective-permute-start | bytes 3145736 | tf_op jit(solution)/shard_map/ppermute | solution.py:21
  428.7 86.9 %collective-permute-start.13 = (bf16[2,256,1024]{2,1,0:T(8,128)(2,1)}, bf16[2,256,1024]{2,1,0:T(8,128)(2,1)}, u32[]{:S(2)}, u32[]{:S(2)}) collective-permute-start(bf16[2,256,1024]{2,1,0:T(8,128)(2,1)} %get-tuple-element.171), channel_id=1, source_target_pairs={{12,0},{14,2},{16,4},{18,6},{20,8},{22,10},{24,12},{26,14},{28,16}... | collective-permute-start | bytes 3145736 | tf_op jit(solution)/shard_map/ppermute | solution.py:21
  430.0 94.0 %collective-permute-start.14 = (bf16[2,256,1024]{2,1,0:T(8,128)(2,1)}, bf16[2,256,1024]{2,1,0:T(8,128)(2,1)}, u32[]{:S(2)}, u32[]{:S(2)}) collective-permute-start(bf16[2,256,1024]{2,1,0:T(8,128)(2,1)} %get-tuple-element.170), channel_id=1, source_target_pairs={{14,0},{16,2},{18,4},{20,6},{22,8},{24,10},{26,12},{28,14},{30,16}... | collective-permute-start | bytes 3145736 | tf_op jit(solution)/shard_map/ppermute | solution.py:21
  440.9 38.2 %copy-start.3 = (bf16[2,256,1024]{2,1,0:T(8,128)(2,1)}, bf16[2,256,1024]{2,1,0:T(8,128)(2,1)S(1)}, u32[]{:S(2)}) copy-start(bf16[2,256,1024]{2,1,0:T(8,128)(2,1)S(1)} %collective-permute-done.10) | copy-start | bytes 3145732
  440.9 180.4 %collective-permute-start.15 = (bf16[2,256,1024]{2,1,0:T(8,128)(2,1)}, bf16[2,256,1024]{2,1,0:T(8,128)(2,1)}, u32[]{:S(2)}, u32[]{:S(2)}) collective-permute-start(bf16[2,256,1024]{2,1,0:T(8,128)(2,1)} %get-tuple-element.169), channel_id=1, source_target_pairs={{16,0},{18,2},{20,4},{22,6},{24,8},{26,10},{28,12},{30,14},{17,1},... | collective-permute-start | bytes 3145736 | tf_op jit(solution)/shard_map/ppermute | solution.py:21
  465.7 13.4 %copy-start.4 = (bf16[2,256,1024]{2,1,0:T(8,128)(2,1)}, bf16[2,256,1024]{2,1,0:T(8,128)(2,1)S(1)}, u32[]{:S(2)}) copy-start(bf16[2,256,1024]{2,1,0:T(8,128)(2,1)S(1)} %collective-permute-done.11) | copy-start | bytes 3145732
  465.7 155.6 %collective-permute-start.8 = (bf16[2,256,1024]{2,1,0:T(8,128)(2,1)}, bf16[2,256,1024]{2,1,0:T(8,128)(2,1)}, u32[]{:S(2)}, u32[]{:S(2)}) collective-permute-start(bf16[2,256,1024]{2,1,0:T(8,128)(2,1)} %get-tuple-element.168), channel_id=1, source_target_pairs={{2,0},{4,2},{6,4},{8,6},{10,8},{12,10},{14,12},{16,14},{18,16},{20... | collective-permute-start | bytes 3145736 | tf_op jit(solution)/shard_map/ppermute | solution.py:21
  480.1 141.2 %collective-permute-start.9 = (bf16[2,256,1024]{2,1,0:T(8,128)(2,1)S(1)}, bf16[2,256,1024]{2,1,0:T(8,128)(2,1)}, u32[]{:S(2)}, u32[]{:S(2)}) collective-permute-start(bf16[2,256,1024]{2,1,0:T(8,128)(2,1)S(1)} %get-tuple-element.175), channel_id=1, source_target_pairs={{4,0},{6,2},{8,4},{10,6},{12,8},{14,10},{16,12},{18,14},{20,16},{2... | collective-permute-start | bytes 3145736 | tf_op jit(solution)/shard_map/ppermute | solution.py:21
  710.1 184.7 %reduce-scatter.9.cloned.1.call-start = ((), (), s32[]{:S(2)}) async-start(), calls=%async_computation.3 | async-start | bytes 884736
  843.0 14.4 %collective-permute-start.16 = (bf16[1024,288]{0,1:T(8,128)(2,1)}, bf16[1024,288]{0,1:T(8,128)(2,1)}, u32[]{:S(2)}, u32[]{:S(2)}) collective-permute-start(bf16[1024,288]{0,1:T(8,128)(2,1)} %bitcast.200), channel_id=1, source_target_pairs={{0,32},{32,0},{64,96},{96,64},{1,33},{33,1},{65,97},{97,65},{2,34}... | collective-permute-start | bytes 1769480 | tf_op jit(solution)/shard_map/ppermute | solution.py:25
  857.4 15.0 %collective-permute-start.17 = (bf16[1024,288]{0,1:T(8,128)(2,1)}, bf16[1024,288]{0,1:T(8,128)(2,1)}, u32[]{:S(2)}, u32[]{:S(2)}) collective-permute-start(bf16[1024,288]{0,1:T(8,128)(2,1)} %collective-permute-done.16), channel_id=1, source_target_pairs={{0,64},{32,96},{64,0},{96,32},{1,65},{33,97},{65,1},{97,33},{2,66}... | collective-permute-start | bytes 1769480 | tf_op jit(solution)/shard_map/ppermute | solution.py:25
  (16 other events, 38.9 us)
Sparse Core Ops, SparseCore 0:
  710.2 132.7 reduce-scatter.6
  879.4 15.3 reduce-scatter.8
where the time goes:
time: 920 us; the launch traced here: 906 us
  waiting for transfers between devices  428 us (47%)
  matrix products  201 us (22%)
  local copies, waits for them, and re-layouts  172 us (19%)
  other arithmetic  50.1 us (5%)
  starting transfers between devices  40 us (4%)
  between operations  14.4 us (2%)
    ppermute x16, waiting for transfers between devices, passed_along(): return lax.ppermute(block, axis, route)  261 us
    unnamed x4, waiting for transfers between devices  145 us
    unnamed x26, local copies, waits for them, and re-layouts  56.5 us
    dot_general x8, matrix products, group_grads(): jnp.einsum('rgd,ld->grl', output_gradient, saved_values, preferred_elemen...  37.1 us
    ppermute x16, starting transfers between devices, passed_along(): return lax.ppermute(block, axis, route)  35.3 us
    dot_general x1, matrix products, turn_block(): jnp.einsum('acd,ae->ecd', inner_turn, hadamard(outer_size), precision=lax...  35.2 us
    another operation x3, local copies, waits for them, and re-layouts, body(): grad_all = jnp.stack([key_gradient, value_gradient])  31.5 us
    dot_general x8, matrix products, group_grads(): jnp.einsum('grl,ld->rgd', prob_low, saved_values, preferred_element_type=...  23.8 us
  transfers between devices with their start and end apart: 20, of which 13 were waited for; matrix products, arithmetic and copies ran while one was open for 3% of the time, Pallas kernels for 0%

commit v1 on v0

v1 whole, which is shorter than its diff:
```python
import math

import jax
import jax.numpy as jnp
import numpy as np
from jax import lax
from jax.experimental import pallas as pl
from jax.experimental.pallas import tpu as pltpu
from jax.sharding import PartitionSpec as P

KEY_VALUE_HEADS = 8
HEAD_SIZE = 128
WINDOW = 2048
SCORE_SCALE = 144.0 ** (-0.5)
SOFTCAP = 50.0
LOG2E = math.log2(math.e)


def dot(a, b, contract):
    return lax.dot_general(
        a, b, ((contract[:1], contract[1:]), ((), ())), preferred_element_type=jnp.float32
    )


def attention_kernel(
    parity_ref,
    own_ref,
    other_ref,
    dq_ref,
    own_kv_ref,
    other_kv_ref,
    k_s,
    v_s,
    kt_s,
    dk_s,
    dv_s,
    e_s,
    u_s,
    dp_s,
    l_s,
    d_s,
    dqt_s,
):
    chips, rows, _ = own_ref.shape
    span = WINDOW // rows
    head = HEAD_SIZE
    parity = parity_ref[0]
    step = pl.program_id(0)
    block = 2 * step + parity

    @pl.when(step == 0)
    def _():
        @pl.loop(0, chips)
        def _(j):
            mine, theirs = 2 * j + parity, 2 * j + 1 - parity
            for place, k, v in (
                (mine, own_ref[j, :, 4 * head : 5 * head], own_ref[j, :, 5 * head : 6 * head]),
                (theirs, other_ref[j, :, :head], other_ref[j, :, head:]),
            ):
                k_s[place] = k
                v_s[place] = v
                kt_s[place] = jnp.transpose(k)
                dk_s[place] = jnp.zeros((rows, head), jnp.float32)
                dv_s[place] = jnp.zeros((rows, head), jnp.float32)

    q2 = jnp.concatenate([own_ref[step, :, :head], own_ref[step, :, head : 2 * head]], axis=0)
    g2 = jnp.concatenate(
        [own_ref[step, :, 2 * head : 3 * head], own_ref[step, :, 3 * head : 4 * head]], axis=0
    )
    l_s[...] = jnp.zeros_like(l_s)
    d_s[...] = jnp.zeros_like(d_s)
    dqt_s[...] = jnp.zeros_like(dqt_s)

    def first_pass(place, mask):
        slot = place - block + span
        s = dot(k_s[place], q2, (1, 1))
        dp = dot(v_s[place], g2, (1, 1))
        capped = jnp.tanh(s * (SCORE_SCALE / SOFTCAP))
        e = jnp.exp2(capped * (SOFTCAP * LOG2E))
        if mask is not None:
            e = jnp.where(mask, e, 0.0)
        u = e - e * (capped * capped)
        l_s[...] += jnp.sum(e.reshape(rows // 8, 8, 2 * rows), axis=0)
        d_s[...] += jnp.sum((e * dp).reshape(rows // 8, 8, 2 * rows), axis=0)
        e_s[slot] = e.astype(jnp.bfloat16)
        u_s[slot] = u.astype(jnp.bfloat16)
        dp_s[slot] = dp

    key_place = lax.broadcasted_iota(jnp.int32, (rows, 2 * rows), 0)
    query_place = lax.broadcasted_iota(jnp.int32, (rows, 2 * rows), 1) % rows
    low = jnp.maximum(block - span + 1, 0)

    @pl.loop(low, block)
    def _(place):
        first_pass(place, None)

    first_pass(block, key_place <= query_place)

    @pl.when(block >= span)
    def _():
        first_pass(block - span, key_place > query_place)

    inverse = 1.0 / jnp.sum(l_s[...], axis=0, keepdims=True)
    delta = jnp.sum(d_s[...], axis=0, keepdims=True) * inverse
    inverse_t = jnp.transpose(jnp.broadcast_to(inverse, (head, 2 * rows)))
    g2_scaled = (g2.astype(jnp.float32) * inverse_t).astype(jnp.bfloat16)
    q2_scaled = (q2.astype(jnp.float32) * (inverse_t * SCORE_SCALE)).astype(jnp.bfloat16)

    @pl.loop(jnp.maximum(block - span, 0), block + 1)
    def _(place):
        slot = place - block + span
        score_grad = u_s[slot] * (dp_s[slot] - delta).astype(jnp.bfloat16)
        dv_s[place] += dot(e_s[slot], g2_scaled, (1, 0))
        dk_s[place] += dot(score_grad, q2_scaled, (1, 0))
        dqt_s[...] += dot(kt_s[place], score_grad, (1, 0))

    dq = jnp.transpose(dqt_s[...] * (inverse * SCORE_SCALE)).astype(jnp.bfloat16)
    dq_ref[0, :, :head] = dq[:rows]
    dq_ref[0, :, head:] = dq[rows:]

    @pl.when(step == chips - 1)
    def _():
        @pl.loop(0, chips)
        def _(j):
            mine, theirs = 2 * j + parity, 2 * j + 1 - parity
            for out_ref, place in ((own_kv_ref, mine), (other_kv_ref, theirs)):
                out_ref[j, :, :head] = dk_s[place].astype(jnp.bfloat16)
                out_ref[j, :, head:] = dv_s[place].astype(jnp.bfloat16)


def attention(parity, own, other):
    chips, rows, _ = own.shape
    head = HEAD_SIZE
    blocks = 2 * chips
    slots = WINDOW // rows + 1
    whole = pl.BlockSpec(memory_space=pltpu.VMEM)
    kv = jax.ShapeDtypeStruct((chips, rows, 2 * head), jnp.bfloat16)
    return pl.pallas_call(
        attention_kernel,
        grid=(chips,),
        out_shape=(kv, kv, kv),
        in_specs=[pl.BlockSpec(memory_space=pltpu.SMEM), whole, whole],
        out_specs=(
            pl.BlockSpec((1, rows, 2 * head), lambda t: (t, 0, 0)),
            whole,
            whole,
        ),
        scratch_shapes=[
            pltpu.VMEM((blocks, rows, head), jnp.bfloat16),
            pltpu.VMEM((blocks, rows, head), jnp.bfloat16),
            pltpu.VMEM((blocks, head, rows), jnp.bfloat16),
            pltpu.VMEM((blocks, rows, head), jnp.float32),
            pltpu.VMEM((blocks, rows, head), jnp.float32),
            pltpu.VMEM((slots, rows, 2 * rows), jnp.bfloat16),
            pltpu.VMEM((slots, rows, 2 * rows), jnp.bfloat16),
            pltpu.VMEM((slots, rows, 2 * rows), jnp.float32),
            pltpu.VMEM((8, 2 * rows), jnp.float32),
            pltpu.VMEM((8, 2 * rows), jnp.float32),
            pltpu.VMEM((head, 2 * rows), jnp.float32),
        ],
        compiler_params=pltpu.CompilerParams(
            dimension_semantics=("arbitrary",), vmem_limit_bytes=48 * 2**20
        ),
        cost_estimate=pl.CostEstimate(
            flops=10 * 112 * rows * rows * head,
            bytes_accessed=10 * 2**20,
            transcendentals=2 * 112 * rows * rows,
        ),
        name="attention",
    )(parity, own, other)


def hadamard(order_size):
    place = np.arange(order_size)
    both = place[:, None] & place[None, :]
    parity = np.zeros_like(both)
    for bit in range(order_size.bit_length() - 1):
        parity ^= both >> bit & 1
    return (1 - 2 * parity) / math.sqrt(order_size)


def body(queries, saved_keys, saved_values, output_gradient, layer_input, hadamard_signs):
    rows, width = saved_keys.shape[2:]
    depth = layer_input.shape[3]
    head = HEAD_SIZE
    heads = KEY_VALUE_HEADS
    ctx_count = lax.axis_size("ctx")
    sections = lax.axis_size("section")
    chips = ctx_count // 2
    lines = chips // 2
    ctx = lax.axis_index("ctx")
    section = lax.axis_index("section")
    mirror = lax.axis_index("mirror")
    core = ctx % 2
    line = ctx // 2 % lines
    far = ctx // (2 * lines)
    same_core = [[2 * chip + c for chip in range(chips)] for c in range(2)]

    def by_head(array):
        return array[0, 0].reshape(rows, heads, -1).transpose(1, 0, 2)

    def across(block):
        return lax.all_to_all(
            block, "ctx", 0, 0, tiled=True, axis_index_groups=same_core
        )

    def swap(block, axis, bit):
        route = [(i, i ^ bit) for i in range(lax.axis_size(axis))]
        return lax.ppermute(block, axis, route)

    sent = jnp.concatenate(
        [by_head(queries), by_head(output_gradient), by_head(saved_keys), by_head(saved_values)],
        axis=2,
    )
    own = across(sent)
    other = swap(own[:, :, 4 * head :], "ctx", 1)
    own, input_rows = lax.optimization_barrier((own, layer_input[0, 0]))

    chunks = input_rows.reshape(rows, 2, lines, depth // (2 * lines)).transpose(2, 0, 1, 3)
    chunks = chunks.reshape(lines, rows, depth // lines)
    columns = [lax.dynamic_index_in_dim(chunks, line, 0, keepdims=False)]
    for distance in range(1, lines):
        piece = lax.dynamic_index_in_dim(chunks, line ^ distance, 0, keepdims=False)
        columns.append(swap(piece, "ctx", 2 * distance))

    dq, own_kv, other_kv = attention(core.astype(jnp.int32).reshape(1), own, other)
    kv = own_kv.astype(jnp.float32) + swap(other_kv, "ctx", 1).astype(jnp.float32)
    kv = kv.astype(jnp.bfloat16)

    value_rows = kv[:, :, head:].reshape(2, 1, lines, rows, head).transpose(0, 1, 3, 2, 4)
    value_rows = jnp.broadcast_to(
        value_rows.reshape(2, 1, rows, lines * head), (2, lines, rows, lines * head)
    ).reshape(chips, rows, lines * head)
    back = across(jnp.concatenate([dq, kv[:, :, :head], value_rows], axis=2))
    query_gradient = back[:, :, : 2 * head].transpose(1, 0, 2).reshape(rows, heads * 2 * head)
    key_gradient = back[:, :, 2 * head : 3 * head].transpose(1, 0, 2).reshape(rows, width)
    values = back[:, :, 3 * head :].reshape(heads, rows, lines, head).transpose(2, 1, 0, 3)
    values = values.reshape(lines, rows, width)
    value_gradient = lax.dynamic_index_in_dim(values, line, 0, keepdims=False)

    total = None
    for distance in range(lines):
        part = dot(
            columns[distance],
            lax.dynamic_index_in_dim(values, line ^ distance, 0, keepdims=False),
            (0, 0),
        )
        total = part if total is None else total + part

    def halve(array, place, axis, bit):
        array = array.astype(jnp.bfloat16)
        keep = lax.dynamic_index_in_dim(array, place, 0, keepdims=False)
        give = lax.dynamic_index_in_dim(array, 1 - place, 0, keepdims=False)
        return keep.astype(jnp.float32) + swap(give, axis, bit).astype(jnp.float32)

    share = depth // (2 * ctx_count)
    total = total.reshape(2, 2, 2 * share * width).transpose(1, 0, 2).reshape(2, 2, 2 * share, width)
    total = halve(total, core, "ctx", 1)
    total = halve(total, far, "ctx", 2 * lines)
    total = total.reshape(2, share, width).astype(jnp.bfloat16)

    def routed(block, route):
        pairs = [(s * 2 + m, t * 2 + n) for (s, m), (t, n) in route]
        return lax.ppermute(block, ("section", "mirror"), pairs)

    places = range(sections)
    from_far = routed(total[0], [((s, 1), (sections - 1 - s, 0)) for s in places])
    from_far_second = routed(total[1], [((s, 1), (sections - 1 - s, 1)) for s in places])
    from_near = routed(total[1], [((s, 0), (s, 1)) for s in places])
    first = total[0].astype(jnp.float32) + from_far.astype(jnp.float32)
    second = from_near.astype(jnp.float32) + from_far_second.astype(jnp.float32)
    result = jnp.where(mirror == 0, first, second)

    signs = lax.dynamic_index_in_dim(hadamard_signs, section, 0, keepdims=False)
    turn = jnp.asarray(hadamard(width), jnp.bfloat16) * signs.astype(jnp.bfloat16)[:, None]
    rotated = dot(result.astype(jnp.bfloat16), turn, (1, 0))
    return (
        query_gradient[None, None],
        key_gradient[None, None],
        value_gradient[None, None],
        rotated[None],
    )


def solution(mesh):
    split = P("section", "mirror", "ctx", None)
    return jax.shard_map(
        body,
        mesh=mesh,
        in_specs=(split, split, split, split, split, P()),
        out_specs=(split, split, split, P("section", ("ctx", "mirror"), None)),
        check_vma=False,
    )
```

time: 920 us -> 253 us (0.28); the launches traced: 906 us -> 249 us
  waiting for transfers between devices: 428 us -> 75.7 us
  matrix products: 201 us -> 10.2 us
  local copies, waits for them, and re-layouts: 172 us -> 41.3 us
  blocking collectives: 0 us -> 46 us
  other arithmetic: 50.1 us -> 7.79 us
  Pallas kernels: 0 us -> 42.3 us
  starting transfers between devices: 40 us -> 25.2 us
  between operations: 14.4 us -> 1 us
    ppermute x18 -> x10, waiting for transfers between devices: 283 us -> 38.2 us  [the longest x7 38.2 us: swap(): return lax.ppermute(block, axis, route)]
    dot_general x51 -> x5, matrix products: 201 us -> 10.2 us  [dot(): lax.dot_general(a, b, ((contract[:1], contract[1:]), ((), ())), preferred...]
    unnamed x4 -> x0, waiting for transfers between devices: 145 us -> none
    all_to_all x0 -> x1, blocking collectives: none -> 46 us  [across(): lax.all_to_all(block, 'ctx', 0, 0, tiled=True, axis_index_groups=same_core)]
    pallas_call x0 -> x1, Pallas kernels: none -> 42.3 us  [attention(): pl.pallas_call(attention_kernel, grid=(chips,), out_shape=(kv, kv, kv), i...]
    unnamed x26 -> x28, local copies, waits for them, and re-layouts: 56.5 us -> 16.4 us
    all_to_all x0 -> x1, waiting for transfers between devices: none -> 37.5 us  [across(): lax.all_to_all(block, 'ctx', 0, 0, tiled=True, axis_index_groups=same_core)]
    another operation x3 -> x4, local copies, waits for them, and re-layouts: 31.5 us -> 3.05 us  [by_head(): return array[0, 0].reshape(rows, heads, -1).transpose(1, 0, 2)]
  transfers between devices with their start and end apart: 20 -> 11, of which waited for: 13 -> 6; matrix products, arithmetic and copies ran while one was open for 3% -> 9% of each run, Pallas kernels for 0% -> 0%
where the time goes in v1:
time: 253 us; the launch traced here: 249 us
  waiting for transfers between devices  75.7 us (30%)
  blocking collectives  46 us (18%)
  Pallas kernels  42.3 us (17%)
  local copies, waits for them, and re-layouts  41.3 us (16%)
  starting transfers between devices  25.2 us (10%)
  matrix products  10.2 us (4%)
  other arithmetic  7.79 us (3%)
    all_to_all x1, blocking collectives, across(): lax.all_to_all(block, 'ctx', 0, 0, tiled=True, axis_index_groups=same_core)  46 us
    pallas_call x1, Pallas kernels, attention(): pl.pallas_call(attention_kernel, grid=(chips,), out_shape=(kv, kv, kv), i...  42.3 us
    ppermute x7, waiting for transfers between devices, swap(): return lax.ppermute(block, axis, route)  38.2 us
    all_to_all x1, waiting for transfers between devices, across(): lax.all_to_all(block, 'ctx', 0, 0, tiled=True, axis_index_groups=same_core)  37.5 us
    unnamed x28, local copies, waits for them, and re-layouts  16.4 us
    ppermute x3, starting transfers between devices, routed(): return lax.ppermute(block, ('section', 'mirror'), pairs)  10.3 us
    dot_general x5, matrix products, dot(): lax.dot_general(a, b, ((contract[:1], contract[1:]), ((), ())), preferred...  10.2 us
    ppermute x7, starting transfers between devices, swap(): return lax.ppermute(block, axis, route)  10.2 us
  transfers between devices with their start and end apart: 11, of which 6 were waited for; matrix products, arithmetic and copies ran while one was open for 9% of the time, Pallas kernels for 0%

profile of v1, /device:TPU:2, one launch (start us, length us, event | category | flops | bytes accessed | tf_op | source)
XLA Modules:
  0.0 249.5 jit_solution(7257164191853171561)
XLA Ops:
  7.9 46.0 %all_to_all.10.own_ref = bf16[8,256,768]{2,1,0:T(8,128)(2,1)S(1)} all-to-all(bf16[8,256,768]{2,1,0:T(8,128)(2,1)S(1)} %pad_maximum_fusion.1), channel_id=1, replica_groups={{0,4,8,12,16,20,24,28},{2,6,10,14,18,22,26,30},{1,5,9,13,17,21,25,29},{..., dimensions={0} | all-to-all | bytes 6291456 | tf_op jit(solution)/shard_map/all_to_all | solution.py:203
  56.5 2.5 copy.65
  59.4 42.3 %attention.1 = (bf16[8,256,256]{2,1,0:T(8,128)(2,1)S(1)}, bf16[8,256,256]{2,1,0:T(8,128)(2,1)S(1)}, bf16[8,256,256]{2,1,0:T(8,128)(2,1)S(1)}) custom-call(s32[1]{0:T(128)} %bitcast.parity_ref, bf16[8,256,768]{2,1,0:T(8,128)(2,1)} %copy-done.2, bf16[8,256,256]{2,1,0:T(8,128)(2,1)S(1)} %collective-permute-done.other_ref), custom_call_target="tpu_custom_call" | custom-call | flops 9395240960 | bytes 10485760 | tf_op jit(solution)/shard_map/attention/pallas_call | solution.py:138
  101.7 3.0 %collective-permute-start.1 = (bf16[8,256,256]{2,1,0:T(8,128)(2,1)S(1)}, bf16[8,256,256]{2,1,0:T(8,128)(2,1)S(1)}, u32[]{:S(2)}, u32[]{:S(2)}) collective-permute-start(bf16[8,256,256]{2,1,0:T(8,128)(2,1)S(1)} %get-tuple-element.12), channel_id=1, source_target_pairs={{0,2},{2,0},{4,6},{6,4},{8,10},{10,8},{12,14},{14,12},{16,18},{18,... | collective-permute-start | bytes 3145736 | tf_op jit(solution)/shard_map/ppermute | solution.py:209
  104.8 2.3 collective-permute-done.1
  108.2 2.1 pad_maximum_fusion
  110.3 4.6 %all-to-all-start.1 = ((bf16[8,256,896]{2,1,0:T(8,128)(2,1)}), bf16[8,256,896]{2,1,0:T(8,128)(2,1)}, u32[]{:S(2)}, u32[]{:S(2)}) async-start(bf16[8,256,896]{2,1,0:T(8,128)(2,1)} %pad_maximum_fusion), calls=%async_computation.1 | async-start | bytes 7340032 | tf_op jit(solution)/shard_map/all_to_all | solution.py:203
  117.9 3.1 %collective-permute-start.4 = (bf16[256,1152]{0,1:T(8,128)(2,1)}, bf16[256,1152]{0,1:T(8,128)(2,1)S(1)}, u32[]{:S(2)}, u32[]{:S(2)}) collective-permute-start(bf16[256,1152]{0,1:T(8,128)(2,1)} %get-tuple-element.23), channel_id=1, source_target_pairs={{0,12},{2,14},{4,8},{6,10},{8,4},{10,6},{12,0},{14,2},{16,28},{18,... | collective-permute-start | bytes 1769480 | tf_op jit(solution)/shard_map/ppermute | solution.py:209
  122.0 37.5 %all-to-all-done.1 = bf16[8,256,896]{2,1,0:T(8,128)(2,1)} async-done(((bf16[8,256,896]{2,1,0:T(8,128)(2,1)}), bf16[8,256,896]{2,1,0:T(8,128)(2,1)}, u32[]{:S(2)}, u32[]{:S(2)}) %all-to-all-start.1) | async-done | bytes 3670048 | tf_op jit(solution)/shard_map/all_to_all | solution.py:203
  161.3 2.4 copy.78
  165.4 18.4 %collective-permute-done.4 = bf16[256,1152]{0,1:T(8,128)(2,1)S(1)} collective-permute-done((bf16[256,1152]{0,1:T(8,128)(2,1)}, bf16[256,1152]{0,1:T(8,128)(2,1)S(1)}, u32[]{:S(2)}, u32[]{:S(2)}) %collective-permute-start.4) | collective-permute-done | bytes 589856 | tf_op jit(solution)/shard_map/ppermute | solution.py:209
  184.6 1.9 fusion.10
  186.5 2.0 convolution_add_fusion.1
  188.5 2.3 fusion.1
  190.8 4.0 %convert_element_type.75 = bf16[2,2,294912]{2,1,0:T(2,128)(2,1)} reshape(bf16[1152,1024]{1,0:T(8,128)(2,1)} %fusion.1) | data formatting | bytes 4718592 | tf_op jit(solution)/shard_map/convert_element_type | solution.py:251
  194.8 4.6 %convert_element_type.77 = bf16[2,2,288,1024]{3,2,0,1:T(8,128)(2,1)} reshape(bf16[2,2,294912]{2,0,1:T(2,128)(2,1)} %bitcast.77) | data formatting | bytes 4718592 | tf_op jit(solution)/shard_map/convert_element_type | solution.py:251
  200.8 2.9 %collective-permute-done.5 = bf16[2,288,1024]{2,1,0:T(8,128)(2,1)} collective-permute-done((bf16[2,288,1024]{2,1,0:T(8,128)(2,1)S(1)}, bf16[2,288,1024]{2,1,0:T(8,128)(2,1)}, u32[]{:S(2)}, u32[]{:S(2)}) %collective-permute-start.5) | collective-permute-done | bytes 1179680 | tf_op jit(solution)/shard_map/ppermute | solution.py:209
  203.8 2.1 fusion.2
  206.7 3.0 %collective-permute-start.6 = (bf16[288,1024]{1,0:T(8,128)(2,1)}, bf16[288,1024]{1,0:T(8,128)(2,1)}, u32[]{:S(2)}, u32[]{:S(2)}) collective-permute-start(bf16[288,1024]{1,0:T(8,128)(2,1)} %dynamic-slice_bitcast_fusion.1), channel_id=1, source_target_pairs={{0,16},{2,18},{4,20},{6,22},{8,24},{10,26},{12,28},{14,30},{16,0},... | collective-permute-start | bytes 1769480 | tf_op jit(solution)/shard_map/ppermute | solution.py:209
  209.7 14.2 %collective-permute-done.6 = bf16[288,1024]{1,0:T(8,128)(2,1)} collective-permute-done((bf16[288,1024]{1,0:T(8,128)(2,1)}, bf16[288,1024]{1,0:T(8,128)(2,1)}, u32[]{:S(2)}, u32[]{:S(2)}) %collective-permute-start.6) | collective-permute-done | bytes 589856 | tf_op jit(solution)/shard_map/ppermute | solution.py:209
  226.8 7.1 %collective-permute-start.7 = (bf16[144,1024]{1,0:T(8,128)(2,1)}, bf16[144,1024]{1,0:T(8,128)(2,1)}, u32[]{:S(2)}, u32[]{:S(2)}) collective-permute-start(bf16[144,1024]{1,0:T(8,128)(2,1)} %get-tuple-element.27), channel_id=1, source_target_pairs={{1,96},{33,64},{65,32},{97,0},{3,98},{35,66},{67,34},{99,2},{5,100... | collective-permute-start | bytes 884744 | tf_op jit(solution)/shard_map/ppermute | solution.py:264
  233.9 1.9 collective-permute-start.9
  242.8 2.3 copy.74
  246.1 3.3 %fusion.5 = f32[1,144,1024]{2,1,0:T(8,128)} fusion(bf16[1024,1024]{1,0:T(8,128)(2,1)} %constant.103.clone, bf16[1024]{0:T(1024)(128)(2,1)S(1)} %convert_reduce_fusion, bf16[144,1024]{1,0:T(8,128)(2,1)} %collective-permute-done.9, bf16[144,1024]{1,0:T(8,128)(2,1)} %collective-permute-done.8, bf16[144,1024]{1,0:T(8,128)(2,1)} %collective-permute-done.7, ...), kind=kOutput, calls=%fused_computation.11 | convolution fusion | flops 304218112 | bytes 3868673 | tf_op jit(solution)/shard_map/dot_general | solution.py:20
  (61 shorter events, 32.7 us)
Async XLA Ops:
  0.6 2.4 copy-start.8
  0.6 3.6 %copy-start.6 = (bf16[1,1,256,2048]{3,2,1,0:T(8,128)(2,1)S(1)}, bf16[1,1,256,2048]{3,2,1,0:T(8,128)(2,1)}, u32[]{:S(2)}) copy-start(bf16[1,1,256,2048]{3,2,1,0:T(8,128)(2,1)} %param.7) | copy-start | bytes 3145732
  4.2 1.2 copy-start.7
  7.9 48.7 %copy-start.3 = (bf16[1,1,256,4608]{3,2,1,0:T(8,128)(2,1)S(1)}, bf16[1,1,256,4608]{3,2,1,0:T(8,128)(2,1)}, u32[]{:S(2)}) copy-start(bf16[1,1,256,4608]{3,2,1,0:T(8,128)(2,1)} %param.11) | copy-start | bytes 7077892
  53.8 1.6 copy-start.2
  56.5 2.9 %collective-permute-start = (bf16[8,256,256]{2,1,0:T(8,128)(2,1)}, bf16[8,256,256]{2,1,0:T(8,128)(2,1)S(1)}, u32[]{:S(2)}, u32[]{:S(2)}) collective-permute-start(bf16[8,256,256]{2,1,0:T(8,128)(2,1)} %slice.36), channel_id=1, source_target_pairs={{0,2},{2,0},{4,6},{6,4},{8,10},{10,8},{12,14},{14,12},{16,18},{18,... | collective-permute-start | bytes 3145736 | tf_op jit(solution)/shard_map/ppermute | solution.py:209
  101.7 5.3 %collective-permute-start.1 = (bf16[8,256,256]{2,1,0:T(8,128)(2,1)S(1)}, bf16[8,256,256]{2,1,0:T(8,128)(2,1)S(1)}, u32[]{:S(2)}, u32[]{:S(2)}) collective-permute-start(bf16[8,256,256]{2,1,0:T(8,128)(2,1)S(1)} %get-tuple-element.12), channel_id=1, source_target_pairs={{0,2},{2,0},{4,6},{6,4},{8,10},{10,8},{12,14},{14,12},{16,18},{18,... | collective-permute-start | bytes 3145736 | tf_op jit(solution)/shard_map/ppermute | solution.py:209
  110.3 4.7 %copy-start.1 = (bf16[1,1,256,4608]{2,3,1,0:T(8,128)(2,1)S(1)}, bf16[1,1,256,4608]{2,3,1,0:T(8,128)(2,1)}, u32[]{:S(2)}) copy-start(bf16[1,1,256,4608]{2,3,1,0:T(8,128)(2,1)} %copy.65) | copy-start | bytes 7077892
  110.3 49.2 %all-to-all-start.1 = ((bf16[8,256,896]{2,1,0:T(8,128)(2,1)}), bf16[8,256,896]{2,1,0:T(8,128)(2,1)}, u32[]{:S(2)}, u32[]{:S(2)}) async-start(bf16[8,256,896]{2,1,0:T(8,128)(2,1)} %pad_maximum_fusion), calls=%async_computation.1 | async-start | bytes 7340032 | tf_op jit(solution)/shard_map/all_to_all | solution.py:203
  115.1 1.5 copy-start
  117.9 65.9 %collective-permute-start.4 = (bf16[256,1152]{0,1:T(8,128)(2,1)}, bf16[256,1152]{0,1:T(8,128)(2,1)S(1)}, u32[]{:S(2)}, u32[]{:S(2)}) collective-permute-start(bf16[256,1152]{0,1:T(8,128)(2,1)} %get-tuple-element.23), channel_id=1, source_target_pairs={{0,12},{2,14},{4,8},{6,10},{8,4},{10,6},{12,0},{14,2},{16,28},{18,... | collective-permute-start | bytes 1769480 | tf_op jit(solution)/shard_map/ppermute | solution.py:209
  120.9 67.5 %collective-permute-start.3 = (bf16[256,1152]{0,1:T(8,128)(2,1)}, bf16[256,1152]{0,1:T(8,128)(2,1)S(1)}, u32[]{:S(2)}, u32[]{:S(2)}) collective-permute-start(bf16[256,1152]{0,1:T(8,128)(2,1)} %get-tuple-element.22), channel_id=1, source_target_pairs={{0,8},{2,10},{4,12},{6,14},{8,0},{10,2},{12,4},{14,6},{16,24},{18,... | collective-permute-start | bytes 1769480 | tf_op jit(solution)/shard_map/ppermute | solution.py:209
  121.8 64.7 %collective-permute-start.2 = (bf16[256,1152]{0,1:T(8,128)(2,1)}, bf16[256,1152]{0,1:T(8,128)(2,1)}, u32[]{:S(2)}, u32[]{:S(2)}) collective-permute-start(bf16[256,1152]{0,1:T(8,128)(2,1)} %get-tuple-element.24), channel_id=1, source_target_pairs={{0,4},{2,6},{4,0},{6,2},{8,12},{10,14},{12,8},{14,10},{16,20},{18,... | collective-permute-start | bytes 1769480 | tf_op jit(solution)/shard_map/ppermute | solution.py:209
  200.7 3.1 %collective-permute-start.5 = (bf16[2,288,1024]{2,1,0:T(8,128)(2,1)S(1)}, bf16[2,288,1024]{2,1,0:T(8,128)(2,1)}, u32[]{:S(2)}, u32[]{:S(2)}) collective-permute-start(bf16[2,288,1024]{2,1,0:T(8,128)(2,1)S(1)} %dynamic-slice_bitcast_fusion), channel_id=1, source_target_pairs={{0,2},{2,0},{4,6},{6,4},{8,10},{10,8},{12,14},{14,12},{16,18},{18,... | collective-permute-start | bytes 3538952 | tf_op jit(solution)/shard_map/ppermute | solution.py:209
  206.7 17.2 %collective-permute-start.6 = (bf16[288,1024]{1,0:T(8,128)(2,1)}, bf16[288,1024]{1,0:T(8,128)(2,1)}, u32[]{:S(2)}, u32[]{:S(2)}) collective-permute-start(bf16[288,1024]{1,0:T(8,128)(2,1)} %dynamic-slice_bitcast_fusion.1), channel_id=1, source_target_pairs={{0,16},{2,18},{4,20},{6,22},{8,24},{10,26},{12,28},{14,30},{16,0},... | collective-permute-start | bytes 1769480 | tf_op jit(solution)/shard_map/ppermute | solution.py:209
  225.2 0.8 copy-start.4
  226.8 19.4 %collective-permute-start.7 = (bf16[144,1024]{1,0:T(8,128)(2,1)}, bf16[144,1024]{1,0:T(8,128)(2,1)}, u32[]{:S(2)}, u32[]{:S(2)}) collective-permute-start(bf16[144,1024]{1,0:T(8,128)(2,1)} %get-tuple-element.27), channel_id=1, source_target_pairs={{1,96},{33,64},{65,32},{97,0},{3,98},{35,66},{67,34},{99,2},{5,100... | collective-permute-start | bytes 884744 | tf_op jit(solution)/shard_map/ppermute | solution.py:264
  233.9 12.3 %collective-permute-start.9 = (bf16[144,1024]{1,0:T(8,128)(2,1)S(1)}, bf16[144,1024]{1,0:T(8,128)(2,1)}, u32[]{:S(2)}, u32[]{:S(2)}) collective-permute-start(bf16[144,1024]{1,0:T(8,128)(2,1)S(1)} %get-tuple-element.28), channel_id=1, source_target_pairs={{1,97},{33,65},{65,33},{97,1},{3,99},{35,67},{67,35},{99,3},{5,101... | collective-permute-start | bytes 884744 | tf_op jit(solution)/shard_map/ppermute | solution.py:264
  235.8 10.3 %collective-permute-start.8 = (bf16[144,1024]{1,0:T(8,128)(2,1)S(1)}, bf16[144,1024]{1,0:T(8,128)(2,1)}, u32[]{:S(2)}, u32[]{:S(2)}) collective-permute-start(bf16[144,1024]{1,0:T(8,128)(2,1)S(1)} %get-tuple-element.28), channel_id=1, source_target_pairs={{0,1},{32,33},{64,65},{96,97},{2,3},{34,35},{66,67},{98,99},{4,5},... | collective-permute-start | bytes 884744 | tf_op jit(solution)/shard_map/ppermute | solution.py:264
  242.8 3.4 %copy-start.5 = (bf16[288,1024]{1,0:T(8,128)(2,1)S(1)}, bf16[288,1024]{1,0:T(8,128)(2,1)}, u32[]{:S(2)}) copy-start(bf16[288,1024]{1,0:T(8,128)(2,1)} %copy-done.4) | copy-start | bytes 1769476

commit v2 on v1

v2 whole, which is shorter than its diff:
```python
import math

import jax
import jax.numpy as jnp
import numpy as np
from jax import lax
from jax.experimental import pallas as pl
from jax.experimental.pallas import tpu as pltpu
from jax.sharding import PartitionSpec as P

KEY_VALUE_HEADS = 8
HEAD_SIZE = 128
WINDOW = 2048
SCORE_SCALE = 144.0 ** (-0.5)
SOFTCAP = 50.0
LOG2E = math.log2(math.e)
WHOLE = pl.BlockSpec(memory_space=pltpu.VMEM)
SCALAR = pl.BlockSpec(memory_space=pltpu.SMEM)


def dot(a, b, contract):
    return lax.dot_general(
        a, b, ((contract[:1], contract[1:]), ((), ())), preferred_element_type=jnp.float32
    )


def pair(ref, first):
    at = first * HEAD_SIZE
    return jnp.concatenate(
        [ref[0, :, at : at + HEAD_SIZE], ref[0, :, at + HEAD_SIZE : at + 2 * HEAD_SIZE]],
        axis=0,
    )


def for_window(step, parity, span, one):
    block = 2 * step + parity
    for early in range(span // 2):
        @pl.when(step == early)
        def _():
            one(jnp.maximum(block - 2 * early - 1, 0), ["maybe"])
            one(block - 2 * early, ["middle"] * (2 * early) + ["near"])

    @pl.when(step >= span // 2)
    def _():
        one(block - span, ["far"] + ["middle"] * (span - 1) + ["near"])


def weights(s, kind, parity):
    rows = s.shape[0]
    capped = jnp.tanh(s * (SCORE_SCALE / SOFTCAP))
    e = jnp.exp2(capped * (SOFTCAP * LOG2E))
    if kind == "maybe":
        e = jnp.where(parity == 1, e, 0.0)
    elif kind != "middle":
        key_place = lax.broadcasted_iota(jnp.int32, s.shape, 0)
        query_place = lax.broadcasted_iota(jnp.int32, s.shape, 1) % rows
        allowed = key_place <= query_place if kind == "near" else key_place > query_place
        e = jnp.where(allowed, e, 0.0)
    return capped, e


def first_slot(place, kinds, block, span):
    return 0 if kinds == ["maybe"] else place - block + span


def blocks_at(ref, place, kinds):
    block = ref[pl.ds(place, len(kinds))]
    return block.reshape(len(kinds) * block.shape[1], block.shape[2])


def column_sums(x):
    return jnp.sum(x.reshape(x.shape[0] // 8, 8, x.shape[1]), axis=0)


def value_kernel(
    parity_ref, own_ref, own_kv_ref, other_ref, mine_ref, theirs_ref, k_s, dv_s, e_s, l_s
):
    chips, rows, _ = own_kv_ref.shape
    span = WINDOW // rows
    head = HEAD_SIZE
    parity = parity_ref[0]
    step = pl.program_id(0)
    block = 2 * step + parity

    @pl.when(step == 0)
    def _():
        @pl.loop(0, chips)
        def _(j):
            k_s[2 * j + parity] = own_kv_ref[j, :, :head]
            k_s[2 * j + 1 - parity] = other_ref[j, :, :head]
        dv_s[...] = jnp.zeros_like(dv_s)

    q2 = pair(own_ref, 0)
    g2 = pair(own_ref, 2)
    l_s[...] = jnp.zeros_like(l_s)

    def first_pass(place, kinds):
        slot = first_slot(place, kinds, block, span)
        sums = l_s[...]
        s = dot(blocks_at(k_s, place, kinds), q2, (1, 1))
        for i, kind in enumerate(kinds):
            _, e = weights(s[i * rows : (i + 1) * rows], kind, parity)
            sums = sums + column_sums(e)
            e_s[slot + i] = e.astype(jnp.bfloat16)
        l_s[...] = sums

    for_window(step, parity, span, first_pass)
    inverse = 1.0 / jnp.sum(l_s[...], axis=0, keepdims=True)
    inverse_t = jnp.transpose(jnp.broadcast_to(inverse, (head, 2 * rows)))
    g2_scaled = (g2.astype(jnp.float32) * inverse_t).astype(jnp.bfloat16)

    def second_pass(place, kinds):
        slot = first_slot(place, kinds, block, span)
        term = dot(blocks_at(e_s, slot, kinds), g2_scaled, (1, 0))
        dv_s[pl.ds(place, len(kinds))] += term.reshape(len(kinds), rows, head)

    for_window(step, parity, span, second_pass)

    @pl.when(step == chips - 1)
    def _():
        @pl.loop(0, chips)
        def _(j):
            mine_ref[j] = dv_s[2 * j + parity].astype(jnp.bfloat16)
            theirs_ref[j] = dv_s[2 * j + 1 - parity].astype(jnp.bfloat16)


def score_kernel(
    parity_ref,
    own_ref,
    own_kv_ref,
    other_ref,
    dq_ref,
    mine_ref,
    theirs_ref,
    k_s,
    v_s,
    kt_s,
    dk_s,
    u_s,
    dp_s,
    l_s,
    d_s,
    dqt_s,
):
    chips, rows, _ = own_kv_ref.shape
    span = WINDOW // rows
    head = HEAD_SIZE
    parity = parity_ref[0]
    step = pl.program_id(0)
    block = 2 * step + parity

    @pl.when(step == 0)
    def _():
        @pl.loop(0, chips)
        def _(j):
            mine, theirs = 2 * j + parity, 2 * j + 1 - parity
            for place, k, v in (
                (mine, own_kv_ref[j, :, :head], own_kv_ref[j, :, head:]),
                (theirs, other_ref[j, :, :head], other_ref[j, :, head:]),
            ):
                k_s[place] = k
                v_s[place] = v
                kt_s[place] = jnp.transpose(k)
        dk_s[...] = jnp.zeros_like(dk_s)

    q2 = pair(own_ref, 0)
    g2 = pair(own_ref, 2)
    l_s[...] = jnp.zeros_like(l_s)
    d_s[...] = jnp.zeros_like(d_s)
    dqt_s[...] = jnp.zeros_like(dqt_s)

    def first_pass(place, kinds):
        slot = first_slot(place, kinds, block, span)
        sums, products = l_s[...], d_s[...]
        s = dot(blocks_at(k_s, place, kinds), q2, (1, 1))
        dps = dot(blocks_at(v_s, place, kinds), g2, (1, 1))
        for i, kind in enumerate(kinds):
            capped, e = weights(s[i * rows : (i + 1) * rows], kind, parity)
            dp = dps[i * rows : (i + 1) * rows]
            sums = sums + column_sums(e)
            products = products + column_sums(e * dp)
            u_s[slot + i] = (e - e * (capped * capped)).astype(jnp.bfloat16)
            dp_s[slot + i] = dp
        l_s[...] = sums
        d_s[...] = products

    for_window(step, parity, span, first_pass)
    inverse = 1.0 / jnp.sum(l_s[...], axis=0, keepdims=True)
    delta = jnp.sum(d_s[...], axis=0, keepdims=True) * inverse
    inverse_t = jnp.transpose(jnp.broadcast_to(inverse * SCORE_SCALE, (head, 2 * rows)))
    q2_scaled = (q2.astype(jnp.float32) * inverse_t).astype(jnp.bfloat16)

    def second_pass(place, kinds):
        slot = first_slot(place, kinds, block, span)
        n = len(kinds)
        grads = [
            u_s[slot + i] * (dp_s[slot + i] - delta).astype(jnp.bfloat16) for i in range(n)
        ]
        score_grad = jnp.concatenate(grads, axis=0)
        dk_s[pl.ds(place, n)] += dot(score_grad, q2_scaled, (1, 0)).reshape(n, rows, head)
        turned = jnp.concatenate([kt_s[place + i] for i in range(n)], axis=1)
        dqt_s[...] += dot(turned, score_grad, (1, 0))

    for_window(step, parity, span, second_pass)
    dq = jnp.transpose(dqt_s[...] * (inverse * SCORE_SCALE)).astype(jnp.bfloat16)
    dq_ref[0, :, :head] = dq[:rows]
    dq_ref[0, :, head:] = dq[rows:]

    @pl.when(step == chips - 1)
    def _():
        @pl.loop(0, chips)
        def _(j):
            mine_ref[j] = dk_s[2 * j + parity].astype(jnp.bfloat16)
            theirs_ref[j] = dk_s[2 * j + 1 - parity].astype(jnp.bfloat16)


def attention_call(kernel, name, parity, own, other, with_query, scratch, products, vmem):
    chips, rows, _ = own.shape
    head = HEAD_SIZE
    grads = jax.ShapeDtypeStruct((chips, rows, head), jnp.bfloat16)
    out_shape, out_specs = [grads, grads], [WHOLE, WHOLE]
    if with_query:
        out_shape.insert(0, jax.ShapeDtypeStruct((chips, rows, 3 * head), jnp.bfloat16))
        out_specs.insert(0, pl.BlockSpec((1, rows, 2 * head), lambda t: (t, 0, 0)))
    return pl.pallas_call(
        kernel,
        grid=(chips,),
        out_shape=out_shape,
        in_specs=[
            SCALAR,
            pl.BlockSpec((1, rows, 4 * head), lambda t: (t, 0, 0)),
            pl.BlockSpec((chips, rows, 2 * head), lambda t: (0, 0, 2), pipeline_mode=pl.Buffered(1)),
            WHOLE,
        ],
        out_specs=out_specs,
        scratch_shapes=[pltpu.VMEM(shape, kind) for shape, kind in scratch],
        compiler_params=pltpu.CompilerParams(
            dimension_semantics=("arbitrary",), vmem_limit_bytes=vmem * 2**20
        ),
        cost_estimate=pl.CostEstimate(
            flops=2 * products * 112 * rows * rows * head,
            bytes_accessed=8 * 2**20,
            transcendentals=2 * 112 * rows * rows,
        ),
        name=name,
    )(parity, own, own, other)


def value_gradients(parity, own, other):
    chips, rows, _ = own.shape
    slots = WINDOW // rows + 1
    return attention_call(
        value_kernel,
        "value_gradients",
        parity,
        own,
        other,
        False,
        [
            ((2 * chips, rows, HEAD_SIZE), jnp.bfloat16),
            ((2 * chips, rows, HEAD_SIZE), jnp.float32),
            ((slots, rows, 2 * rows), jnp.bfloat16),
            ((8, 2 * rows), jnp.float32),
        ],
        4,
        28,
    )


def score_gradients(parity, own, other):
    chips, rows, _ = own.shape
    slots = WINDOW // rows + 1
    return attention_call(
        score_kernel,
        "score_gradients",
        parity,
        own,
        other,
        True,
        [
            ((2 * chips, rows, HEAD_SIZE), jnp.bfloat16),
            ((2 * chips, rows, HEAD_SIZE), jnp.bfloat16),
            ((2 * chips, HEAD_SIZE, rows), jnp.bfloat16),
            ((2 * chips, rows, HEAD_SIZE), jnp.float32),
            ((slots, rows, 2 * rows), jnp.bfloat16),
            ((slots, rows, 2 * rows), jnp.float32),
            ((8, 2 * rows), jnp.float32),
            ((8, 2 * rows), jnp.float32),
            ((HEAD_SIZE, 2 * rows), jnp.float32),
        ],
        8,
        60,
    )


def small_call(
    kernel,
    name,
    out_shape,
    scratch,
    flops,
    *operands,
    grid=None,
    in_specs=None,
    out_specs=None,
    kind=jnp.bfloat16,
    vmem=16,
    aliases=None,
):
    kinds = [jax.ShapeDtypeStruct(shape, kind) for shape in out_shape]
    specs = {}
    if grid is not None:
        specs = {"grid": grid}
    moved = sum(x.size * x.dtype.itemsize for x in operands) + sum(2 * math.prod(s) for s in out_shape)
    return pl.pallas_call(
        kernel,
        out_shape=kinds,
        in_specs=in_specs if in_specs is not None else [WHOLE] * len(operands),
        out_specs=out_specs if out_specs is not None else [WHOLE] * len(kinds),
        scratch_shapes=scratch,
        compiler_params=pltpu.CompilerParams(vmem_limit_bytes=vmem * 2**20),
        cost_estimate=pl.CostEstimate(flops=flops, bytes_accessed=moved, transcendentals=0),
        name=name,
        input_output_aliases=aliases or {},
        **specs,
    )(*operands)


def pack_heads(queries, output_gradient, saved_keys, saved_values):
    heads = KEY_VALUE_HEADS

    def kernel(*refs):
        out_ref, at = refs[-1], 0
        for ref in refs[:-1]:
            wide = ref.shape[1] // heads
            for g in range(heads):
                out_ref[g, :, at : at + wide] = ref[:, g * wide : (g + 1) * wide]
            at += wide

    rows = queries.shape[0]
    arrays = (queries, output_gradient, saved_keys, saved_values)
    part = rows // 4
    total = sum(x.shape[1] for x in arrays) // heads
    (packed,) = small_call(
        kernel,
        "pack_heads",
        [(heads, rows, total)],
        [],
        0,
        *arrays,
        grid=(rows // part,),
        in_specs=[pl.BlockSpec((part, x.shape[1]), lambda r: (r, 0)) for x in arrays],
        out_specs=[pl.BlockSpec((heads, part, total), lambda r: (0, r, 0))],
        vmem=60,
    )
    return packed


def pack_scores(payload, mine, theirs):
    def kernel(_, mine_ref, theirs_ref, out_ref):
        out_ref[...] = add(mine_ref[...], theirs_ref[...])

    chips, rows, head = mine.shape
    part = chips // 2
    block = pl.BlockSpec((part, rows, head), lambda t: (t, 0, 0))
    (packed,) = small_call(
        kernel,
        "pack_scores",
        [payload.shape],
        [],
        0,
        payload,
        mine,
        theirs,
        grid=(chips // part,),
        in_specs=[pl.BlockSpec(memory_space=pl.ANY), block, block],
        out_specs=[pl.BlockSpec((part, rows, head), lambda t: (t, 0, 2))],
        vmem=60,
        aliases={0: 0},
    )
    return packed


def unpack_scores(back):
    def kernel(in_ref, dq_ref, dk_ref):
        for g in range(heads):
            dq_ref[:, g * 2 * head : (g + 1) * 2 * head] = in_ref[g, :, : 2 * head]
            dk_ref[:, g * head : (g + 1) * head] = in_ref[g, :, 2 * head :]

    heads, rows, width = back.shape
    head = HEAD_SIZE
    part = rows // 4
    widths = (2 * head * heads, head * heads)
    return small_call(
        kernel,
        "unpack_scores",
        [(rows, w) for w in widths],
        [],
        0,
        back,
        grid=(rows // part,),
        in_specs=[pl.BlockSpec((heads, part, width), lambda r: (0, r, 0))],
        out_specs=[pl.BlockSpec((part, w), lambda r: (r, 0)) for w in widths],
    )


def pack_values(mine, theirs):
    def kernel(mine_ref, theirs_ref, out_ref):
        for x in range(2):
            for y in range(2):
                total = add(mine_ref[x, 0, y], theirs_ref[x, 0, y])
                for to in range(4):
                    out_ref[to // 2, 0, to % 2, 2 * x + y] = total

    chips, rows, head = mine.shape
    split = (2, 2, 2, rows, head)
    (packed,) = small_call(
        kernel,
        "pack_values",
        [split[:3] + (4, rows, head)],
        [],
        0,
        mine.reshape(split),
        theirs.reshape(split),
        grid=(2,),
        in_specs=[pl.BlockSpec((2, 1, 2, rows, head), lambda p: (0, p, 0, 0, 0))] * 2,
        out_specs=[pl.BlockSpec((2, 1, 2, 4, rows, head), lambda p: (0, p, 0, 0, 0, 0))],
        vmem=60,
    )
    return packed.reshape(chips, 4, rows, head)


def turn_input(place, input_rows):
    rows, depth = input_rows.shape
    share = depth // 16
    wide = 2 * HEAD_SIZE

    def kernel(place_ref, in_ref, *refs):
        out_refs, turned_s = refs[:-1], refs[-1]
        for at in range(0, depth, wide):
            turned_s[at : at + wide] = jnp.transpose(in_ref[:, at : at + wide])
        for distance, out_ref in enumerate(out_refs):
            to = place_ref[0] ^ distance
            for high in range(2):
                for core in range(2):
                    index = ((to // 2 * 2 + high) * 2 + to % 2) * 2 + core
                    piece = turned_s[pl.ds(pl.multiple_of(index * share, 16), share)]
                    out_ref[high, core * share : (core + 1) * share] = piece

    return small_call(
        kernel,
        "turn_input",
        [(2, 2 * share, rows)] * 4,
        [pltpu.VMEM((depth, rows), jnp.bfloat16)],
        0,
        place,
        input_rows,
        in_specs=[SCALAR, WHOLE],
    )


def input_product(place, columns, back):
    members = len(columns)
    heads, _, rows, head = back.shape
    share = columns[0].shape[1] // 2

    def kernel(place_ref, *refs):
        column_refs, back_ref = refs[:members], refs[members]
        give_ref, keep_ref, value_ref = refs[members + 1 :]
        member, core, high = place_ref[0], place_ref[1], place_ref[2]
        v = [
            jnp.concatenate([back_ref[0, member ^ d], back_ref[1, member ^ d]], axis=1)
            for d in range(members)
        ]
        value_ref[...] = v[0]
        v = jnp.concatenate(v, axis=0)
        for at, which_high in enumerate((1 - high, high)):
            for out_ref, which_core in ((give_ref, 1 - core), (keep_ref, core)):
                part = pl.ds(pl.multiple_of(which_core * share, 16), share)
                x = jnp.concatenate([ref[which_high, part] for ref in column_refs], axis=1)
                out_ref[at] = dot(x, v, (1, 0)).astype(jnp.bfloat16)

    once = pl.Buffered(1)
    halves = pl.BlockSpec((2, share, 2 * head), lambda g: (0, 0, g))
    return small_call(
        kernel,
        "input_product",
        [(2, share, heads * head)] * 2 + [(rows, heads * head)],
        [],
        8 * share * members * rows * heads * head,
        place,
        *columns,
        back,
        grid=(heads // 2,),
        in_specs=[SCALAR]
        + [pl.BlockSpec((2, 2 * share, rows), lambda g: (0, 0, 0), pipeline_mode=once)] * members
        + [pl.BlockSpec((2, members, rows, head), lambda g: (g, 0, 0, 0))],
        out_specs=[halves, halves, pl.BlockSpec((rows, 2 * head), lambda g: (0, g))],
        vmem=60,
    )


def add32(a, b):
    return a.astype(jnp.float32) + b.astype(jnp.float32)


def add(a, b):
    return add32(a, b).astype(jnp.bfloat16)


def cut_pieces(place, keep, got):
    def kernel(place_ref, keep_ref, got_ref, cross_other_ref, cross_own_ref, stay_ref, second_ref):
        mirror = place_ref[3]
        cross_other_ref[...] = add(keep_ref[0, 1 - mirror], got_ref[0, 1 - mirror])
        cross_own_ref[...] = add(keep_ref[1, 1 - mirror], got_ref[1, 1 - mirror])
        stay_ref[...] = add(keep_ref[0, mirror], got_ref[0, mirror])
        second_ref[...] = add(keep_ref[1, 1], got_ref[1, 1])

    return small_call(
        kernel,
        "cut_pieces",
        [keep.shape[2:]] * 4,
        [],
        0,
        place,
        keep,
        got,
        in_specs=[SCALAR, WHOLE, WHOLE],
    )


def finish(place, signs, turn, pieces):
    def kernel(place_ref, signs_ref, turn_ref, own_ref, got_ref, near_ref, near2_ref, far_ref, other_ref, out_ref):
        own = add32(own_ref[...], got_ref[...])
        total = jnp.where(place_ref[3] == 0, own, far_ref[...].astype(jnp.float32))
        total = total + add32(near_ref[...], near2_ref[...]) + other_ref[...].astype(jnp.float32)
        signs = signs_ref[pl.ds(place_ref[4], 1)].astype(jnp.float32)
        out_ref[...] = dot((total * signs).astype(jnp.bfloat16), turn_ref[...], (1, 0))

    own = pieces[0]
    (out,) = small_call(
        kernel,
        "finish",
        [own.shape],
        [],
        2 * own.size * own.shape[1],
        place,
        signs,
        turn,
        *pieces,
        in_specs=[SCALAR] + [WHOLE] * 8,
        kind=jnp.float32,
    )
    return out


def hadamard(order_size):
    place = np.arange(order_size)
    both = place[:, None] & place[None, :]
    parity = np.zeros_like(both)
    for bit in range(order_size.bit_length() - 1):
        parity ^= both >> bit & 1
    return (1 - 2 * parity) / math.sqrt(order_size)


def body(queries, saved_keys, saved_values, output_gradient, layer_input, hadamard_signs):
    width = saved_keys.shape[3]
    head = HEAD_SIZE
    chips = lax.axis_size("ctx") // 2
    sections = lax.axis_size("section")
    ctx = lax.axis_index("ctx").astype(jnp.int32)
    section = lax.axis_index("section").astype(jnp.int32)
    mirror = lax.axis_index("mirror").astype(jnp.int32)
    core = ctx & 1
    same_core = [[2 * chip + c for chip in range(chips)] for c in range(2)]
    member = (ctx >> 3) * 2 + (ctx >> 1 & 1)
    place = jnp.stack([member, core, ctx >> 2 & 1, mirror, section])

    def across(block):
        return lax.all_to_all(block, "ctx", 0, 0, tiled=True, axis_index_groups=same_core)

    def swap(block, bits):
        return lax.ppermute(block, "ctx", [(i, i ^ bits) for i in range(2 * chips)])

    turned = turn_input(place, layer_input[0, 0])
    own = across(
        pack_heads(queries[0, 0], output_gradient[0, 0], saved_keys[0, 0], saved_values[0, 0])
    )
    own, *turned = lax.optimization_barrier((own, *turned))
    other = swap(own[:, :, 4 * head :], 1)
    parity = core.reshape(1)
    columns = turned[:1] + [swap(turned[d], (d & 1) * 2 + (d >> 1) * 8) for d in range(1, 4)]

    dv_mine, dv_theirs = value_gradients(parity, own, other)
    values = pack_values(dv_mine, swap(dv_theirs, 1))
    values, own, *columns = lax.optimization_barrier((values, own, *columns))
    values_back = across(values)

    scores, dk_mine, dk_theirs = score_gradients(parity, own, other)
    scores = pack_scores(scores, dk_mine, swap(dk_theirs, 1))
    values_back, scores = lax.optimization_barrier((values_back, scores))
    scores_back = across(scores)
    give, keep, value_gradient = input_product(place, columns, values_back)
    got = swap(give, 1)

    keep = keep.reshape(2, 2, -1, width)
    got = got.reshape(keep.shape)
    sections = lax.axis_size("section")
    cross_other, cross_own, stay_other, second_own = cut_pieces(place, keep, got)

    def routed(block, route, group):
        axes = ("section", "ctx", "mirror")
        pairs = [
            ((s * 2 * chips + i) * 2 + m, (t * 2 * chips + (i ^ group)) * 2 + n)
            for (s, m), (t, n) in route
            for i in range(2 * chips)
        ]
        return lax.ppermute(block, axes, pairs)

    far = [((s, 1), (sections - 1 - s, 1)) for s in range(sections)]
    cross = [((s, 1), (sections - 1 - s, 0)) for s in range(sections)]
    cross += [((s, 0), (s, 1)) for s in range(sections)]
    near_other = routed(cross_other, cross, 4)
    other = routed(stay_other, far + [((s, 0), (s, 0)) for s in range(sections)], 4)
    cross_own, second_own, scores_back = lax.optimization_barrier((cross_own, second_own, scores_back))
    near_own = routed(cross_own, cross, 0)
    far_own = routed(second_own, far, 0)
    rotated = finish(
        place,
        hadamard_signs,
        jnp.asarray(hadamard(width), jnp.bfloat16),
        (keep[1, 0], got[1, 0], near_other, near_own, far_own, other),
    )
    query_gradient, key_gradient = unpack_scores(scores_back)
    return (
        query_gradient[None, None],
        key_gradient[None, None],
        value_gradient[None, None],
        rotated[None],
    )


def solution(mesh):
    split = P("section", "mirror", "ctx", None)
    return jax.shard_map(
        body,
        mesh=mesh,
        in_specs=(split, split, split, split, split, P()),
        out_specs=(split, split, split, P("section", ("ctx", "mirror"), None)),
        check_vma=False,
    )
```

time: 253 us -> 171 us (0.68); the launches traced: 249 us -> 171 us
  blocking collectives: 46 us -> 0 us
  local copies, waits for them, and re-layouts: 41.3 us -> 10.1 us
  Pallas kernels: 42.3 us -> 65.7 us
  waiting for transfers between devices: 75.7 us -> 56.1 us
  starting transfers between devices: 25.2 us -> 38 us
  matrix products: 10.2 us -> 0 us
  other arithmetic: 7.79 us -> 0 us
    all_to_all x1 -> x0, blocking collectives: 46 us -> none  [across(): lax.all_to_all(block, 'ctx', 0, 0, tiled=True, axis_index_groups=same_core)]
    pallas_call x1 -> x10, Pallas kernels: 42.3 us -> 65.7 us  [the longest x2 42.8 us: attention_call(): pl.pallas_call(kernel, grid=(chips,), out_shape=out_shape, in_specs=[SCAL...]
    ppermute x10 -> x11, waiting for transfers between devices: 38.2 us -> 23.4 us  [the longest x4 12.3 us: routed(): return lax.ppermute(block, axes, pairs)]
    all_to_all x1 -> x3, starting transfers between devices: 4.63 us -> 18 us  [across(): lax.all_to_all(block, 'ctx', 0, 0, tiled=True, axis_index_groups=same_core)]
    dot_general x5 -> x0, matrix products: 10.2 us -> none  [dot(): lax.dot_general(a, b, ((contract[:1], contract[1:]), ((), ())), preferred...]
    convert_element_type x2 -> x0, local copies, waits for them, and re-layouts: 8.59 us -> none  [halve(): array = array.astype(jnp.bfloat16)]
    unnamed x28 -> x30, local copies, waits for them, and re-layouts: 16.4 us -> 8.95 us
    slice x6 -> x1, local copies, waits for them, and re-layouts: 6.22 us -> 0.07 us  [body(): other = swap(own[:, :, 4 * head:], 1)]
  transfers between devices with their start and end apart: 11 -> 14, of which waited for: 6 -> 7; matrix products, arithmetic and copies ran while one was open for 9% -> 1% of each run, Pallas kernels for 0% -> 35%
where the time goes in v2:
time: 171 us
  Pallas kernels  65.7 us (38%)
  waiting for transfers between devices  56.1 us (33%)
  starting transfers between devices  38 us (22%)
  local copies, waits for them, and re-layouts  10.1 us (6%)
    pallas_call x2, Pallas kernels, attention_call(): pl.pallas_call(kernel, grid=(chips,), out_shape=out_shape, in_specs=[SCAL...  42.8 us
    all_to_all x3, waiting for transfers between devices, across(): lax.all_to_all(block, 'ctx', 0, 0, tiled=True, axis_index_groups=same_core)  32.6 us
    pallas_call x8, Pallas kernels, small_call(): pl.pallas_call(kernel, out_shape=kinds, in_specs=in_specs if in_specs is...  22.8 us
    all_to_all x3, starting transfers between devices, across(): lax.all_to_all(block, 'ctx', 0, 0, tiled=True, axis_index_groups=same_core)  18 us
    ppermute x4, starting transfers between devices, routed(): return lax.ppermute(block, axes, pairs)  14.8 us
    ppermute x4, waiting for transfers between devices, routed(): return lax.ppermute(block, axes, pairs)  12.3 us
    ppermute x7, waiting for transfers between devices, swap(): return lax.ppermute(block, 'ctx', [(i, i ^ bits) for i in range(2 * chips)])  11.1 us
    unnamed x30, local copies, waits for them, and re-layouts  8.95 us
  transfers between devices with their start and end apart: 14, of which 7 were waited for; matrix products, arithmetic and copies ran while one was open for 1% of the time, Pallas kernels for 35%

profile of v2, /device:TPU:2, one launch (start us, length us, event | category | flops | bytes accessed | tf_op | source)
XLA Modules:
  0.0 170.6 jit_solution(15214895978984187484)
XLA Ops:
  0.6 4.2 %pack_heads.1 = bf16[8,256,768]{2,1,0:T(8,128)(2,1)} custom-call(bf16[256,2048]{1,0:T(8,128)(2,1)} %bitcast.30, bf16[256,2048]{1,0:T(8,128)(2,1)} %bitcast.31, bf16[256,1024]{1,0:T(8,128)(2,1)} %bitcast.33, bf16[256,1024]{1,0:T(8,128)(2,1)} %bitcast.34), custom_call_target="tpu_custom_call" | custom-call | bytes 6291456 | tf_op jit(solution)/shard_map/pack_heads/pallas_call | solution.py:315
  4.8 6.0 %all-to-all-start = ((bf16[8,256,768]{2,1,0:T(8,128)(2,1)}), bf16[8,256,768]{2,1,0:T(8,128)(2,1)S(1)}, u32[]{:S(2)}, u32[]{:S(2)}) async-start(bf16[8,256,768]{2,1,0:T(8,128)(2,1)} %pack_heads.1), calls=%async_computation | async-start | bytes 6291456 | tf_op jit(solution)/shard_map/all_to_all | solution.py:580
  11.0 1.7 copy-done.1
  12.6 2.4 %turn_input.1 = (bf16[2,576,256]{2,1,0:T(8,128)(2,1)S(1)}, bf16[2,576,256]{2,1,0:T(8,128)(2,1)}, bf16[2,576,256]{2,1,0:T(8,128)(2,1)}, bf16[2,576,256]{2,1,0:T(8,128)(2,1)}) custom-call(s32[5]{0:T(128)S(1)} %stack.23.place_ref, bf16[256,4608]{1,0:T(8,128)(2,1)S(1)} %bitcast.23), custom_call_target="tpu_custom_call" | custom-call | bytes 4718612 | tf_op jit(solution)/shard_map/turn_input/pallas_call | solution.py:315
  15.9 32.6 %all-to-all-done.own_ref.own_kv_ref = bf16[8,256,768]{2,1,0:T(8,128)(2,1)S(1)} async-done(((bf16[8,256,768]{2,1,0:T(8,128)(2,1)}), bf16[8,256,768]{2,1,0:T(8,128)(2,1)S(1)}, u32[]{:S(2)}, u32[]{:S(2)}) %all-to-all-start) | async-done | bytes 3145760 | tf_op jit(solution)/shard_map/all_to_all | solution.py:580
  50.3 1.9 %collective-permute-start.3 = (bf16[2,576,256]{2,1,0:T(8,128)(2,1)}, bf16[2,576,256]{2,1,0:T(8,128)(2,1)}, u32[]{:S(2)}, u32[]{:S(2)}) collective-permute-start(bf16[2,576,256]{2,1,0:T(8,128)(2,1)} %get-tuple-element.47), channel_id=1, source_target_pairs={{0,16},{2,18},{4,20},{6,22},{8,24},{10,26},{12,28},{14,30},{16,0},... | collective-permute-start | bytes 1769480 | tf_op jit(solution)/shard_map/ppermute | solution.py:583
  53.8 16.3 %value_gradients.1 = (bf16[8,256,128]{2,1,0:T(8,128)(2,1)S(1)}, bf16[8,256,128]{2,1,0:T(8,128)(2,1)S(1)}) custom-call(s32[1]{0:T(128)} %bitcast.1.parity_ref, bf16[8,256,768]{2,1,0:T(8,128)(2,1)S(1)} %all-to-all-done.own_ref.own_kv_ref, bf16[8,256,768]{2,1,0:T(8,128)(2,1)S(1)} %all-to-all-done.own_ref.own_kv_ref, ...), custom_call_target="tpu_custom_call" | custom-call | flops 7516192768 | bytes 8388608 | tf_op jit(solution)/shard_map/value_gradients/pallas_call | solution.py:225
  70.9 1.9 %collective-permute-done.1 = bf16[8,256,128]{2,1,0:T(8,128)(2,1)S(1)} collective-permute-done((bf16[8,256,128]{2,1,0:T(8,128)(2,1)S(1)}, bf16[8,256,128]{2,1,0:T(8,128)(2,1)S(1)}, u32[]{:S(2)}, u32[]{:S(2)}) %collective-permute-start.1) | collective-permute-done | bytes 524320 | tf_op jit(solution)/shard_map/ppermute | solution.py:583
  73.6 2.4 %pack_values.1 = bf16[2,2,2,4,256,128]{5,4,3,2,1,0:T(8,128)(2,1)} custom-call(bf16[2,2,2,256,128]{4,3,2,1,0:T(8,128)(2,1)} %bitcast.28, bf16[2,2,2,256,128]{4,3,2,1,0:T(8,128)(2,1)} %bitcast.35), custom_call_target="tpu_custom_call" | custom-call | bytes 3145728 | tf_op jit(solution)/shard_map/pack_values/pallas_call | solution.py:315
  76.0 4.1 %collective-permute-done.4.refs_3_ = bf16[2,576,256]{2,1,0:T(8,128)(2,1)} collective-permute-done((bf16[2,576,256]{2,1,0:T(8,128)(2,1)}, bf16[2,576,256]{2,1,0:T(8,128)(2,1)}, u32[]{:S(2)}, u32[]{:S(2)}) %collective-permute-start.4) | collective-permute-done | bytes 589856 | tf_op jit(solution)/shard_map/ppermute | solution.py:583
  80.1 4.8 %all-to-all-start.1 = ((bf16[8,4,256,128]{3,2,1,0:T(8,128)(2,1)}), bf16[8,4,256,128]{3,2,1,0:T(8,128)(2,1)S(1)}, u32[]{:S(2)}, u32[]{:S(2)}) async-start(bf16[8,4,256,128]{3,2,1,0:T(8,128)(2,1)} %bitcast.29), calls=%async_computation.1 | async-start | bytes 4194304 | tf_op jit(solution)/shard_map/all_to_all | solution.py:580
  84.9 26.6 %score_gradients.1 = (bf16[8,256,384]{2,1,0:T(8,128)(2,1)}, bf16[8,256,128]{2,1,0:T(8,128)(2,1)}, bf16[8,256,128]{2,1,0:T(8,128)(2,1)}) custom-call(s32[1]{0:T(128)} %bitcast.1.parity_ref, bf16[8,256,768]{2,1,0:T(8,128)(2,1)} %copy-done, bf16[8,256,768]{2,1,0:T(8,128)(2,1)} %copy-done, bf16[8,256,256]{2,1,0:T(8,128)(2,1)} %copy-done.8), custom_call_target="tpu_custom_call" | custom-call | flops 15032385536 | bytes 8388608 | tf_op jit(solution)/shard_map/score_gradients/pallas_call | solution.py:225
  111.5 2.1 %collective-permute-done.5.theirs_ref = bf16[8,256,128]{2,1,0:T(8,128)(2,1)S(1)} collective-permute-done((bf16[8,256,128]{2,1,0:T(8,128)(2,1)}, bf16[8,256,128]{2,1,0:T(8,128)(2,1)S(1)}, u32[]{:S(2)}, u32[]{:S(2)}) %collective-permute-start.5) | collective-permute-done | bytes 524320 | tf_op jit(solution)/shard_map/ppermute | solution.py:583
  114.4 2.0 %pack_scores.1 = bf16[8,256,384]{2,1,0:T(8,128)(2,1)} custom-call(bf16[8,256,384]{2,1,0:T(8,128)(2,1)} %get-tuple-element.55._, bf16[8,256,128]{2,1,0:T(8,128)(2,1)} %get-tuple-element.56.mine_ref, bf16[8,256,128]{2,1,0:T(8,128)(2,1)} %copy-done.14), custom_call_target="tpu_custom_call", output_to_operand_aliasing={{}: (0, {})} | custom-call | bytes 4194304 | tf_op jit(solution)/shard_map/pack_scores/pallas_call | solution.py:315
  117.7 7.2 %all-to-all-start.2 = ((bf16[8,256,384]{2,1,0:T(8,128)(2,1)}), bf16[8,256,384]{2,1,0:T(8,128)(2,1)S(1)}, u32[]{:S(2)}, u32[]{:S(2)}) async-start(bf16[8,256,384]{2,1,0:T(8,128)(2,1)} %pack_scores.1), calls=%async_computation.2 | async-start | bytes 3145728 | tf_op jit(solution)/shard_map/all_to_all | solution.py:580
  124.9 6.4 %input_product.1 = (bf16[2,288,1024]{2,1,0:T(8,128)(2,1)}, bf16[2,288,1024]{2,1,0:T(8,128)(2,1)}, bf16[256,1024]{1,0:T(8,128)(2,1)}) custom-call(s32[5]{0:T(128)} %copy-done.6, bf16[2,576,256]{2,1,0:T(8,128)(2,1)} %copy-done.9, bf16[2,576,256]{2,1,0:T(8,128)(2,1)} %collective-permute-done.2.refs_1_, bf16[2,576,256]{2,1,0:T(8,128)(2,1)} %collective-permute-done.3.refs_2_, ...), custom_call_target="tpu_custom_call" | custom-call | flops 2415919104 | bytes 7340052 | tf_op jit(solution)/shard_map/input_product/pallas_call | solution.py:315
  131.3 3.0 %collective-permute-done.6 = bf16[2,288,1024]{2,1,0:T(8,128)(2,1)S(1)} collective-permute-done((bf16[2,288,1024]{2,1,0:T(8,128)(2,1)}, bf16[2,288,1024]{2,1,0:T(8,128)(2,1)S(1)}, u32[]{:S(2)}, u32[]{:S(2)}) %collective-permute-start.6) | collective-permute-done | bytes 1179680 | tf_op jit(solution)/shard_map/ppermute | solution.py:583
  138.6 7.9 %collective-permute-start.7 = (bf16[144,1024]{1,0:T(8,128)(2,1)}, bf16[144,1024]{1,0:T(8,128)(2,1)S(1)}, u32[]{:S(2)}, u32[]{:S(2)}) collective-permute-start(bf16[144,1024]{1,0:T(8,128)(2,1)} %get-tuple-element.68), channel_id=1, source_target_pairs={{1,104},{3,106},{5,108},{7,110},{9,96},{11,98},{13,100},{15,102},{... | collective-permute-start | bytes 884744 | tf_op jit(solution)/shard_map/ppermute | solution.py:618
  146.5 5.0 %collective-permute-start.8 = (bf16[144,1024]{1,0:T(8,128)(2,1)}, bf16[144,1024]{1,0:T(8,128)(2,1)S(1)}, u32[]{:S(2)}, u32[]{:S(2)}) collective-permute-start(bf16[144,1024]{1,0:T(8,128)(2,1)} %copy-done.11), channel_id=1, source_target_pairs={{1,96},{3,98},{5,100},{7,102},{9,104},{11,106},{13,108},{15,110},{... | collective-permute-start | bytes 884744 | tf_op jit(solution)/shard_map/ppermute | solution.py:618
  151.5 1.9 %collective-permute-start.9 = (bf16[144,1024]{1,0:T(8,128)(2,1)}, bf16[144,1024]{1,0:T(8,128)(2,1)S(1)}, u32[]{:S(2)}, u32[]{:S(2)}) collective-permute-start(bf16[144,1024]{1,0:T(8,128)(2,1)} %copy-done.10), channel_id=1, source_target_pairs={{1,97},{3,99},{5,101},{7,103},{9,105},{11,107},{13,109},{15,111},{... | collective-permute-start | bytes 884744 | tf_op jit(solution)/shard_map/ppermute | solution.py:618
  154.4 1.9 %unpack_scores.1 = (bf16[256,2048]{1,0:T(8,128)(2,1)}, bf16[256,1024]{1,0:T(8,128)(2,1)}) custom-call(bf16[8,256,384]{2,1,0:T(8,128)(2,1)S(1)} %all-to-all-done.2.in_ref), custom_call_target="tpu_custom_call" | custom-call | bytes 3145728 | tf_op jit(solution)/shard_map/unpack_scores/pallas_call | solution.py:315
  156.3 6.8 %collective-permute-done.10.other_ref = bf16[144,1024]{1,0:T(8,128)(2,1)S(1)} collective-permute-done((bf16[144,1024]{1,0:T(8,128)(2,1)}, bf16[144,1024]{1,0:T(8,128)(2,1)S(1)}, u32[]{:S(2)}, u32[]{:S(2)}) %collective-permute-start.10) | collective-permute-done | bytes 294944 | tf_op jit(solution)/shard_map/ppermute | solution.py:618
  163.1 5.5 %collective-permute-done.9.far_ref = bf16[144,1024]{1,0:T(8,128)(2,1)S(1)} collective-permute-done((bf16[144,1024]{1,0:T(8,128)(2,1)}, bf16[144,1024]{1,0:T(8,128)(2,1)S(1)}, u32[]{:S(2)}, u32[]{:S(2)}) %collective-permute-start.9) | collective-permute-done | bytes 294944 | tf_op jit(solution)/shard_map/ppermute | solution.py:618
  168.6 2.0 %finish.1 = f32[144,1024]{1,0:T(8,128)} custom-call(s32[5]{0:T(128)S(1)} %copy-done.7, s32[4,1024]{1,0:T(4,128)S(1)} %copy-done.5, bf16[1024,1024]{1,0:T(8,128)(2,1)S(1)} %copy-done.2, bf16[144,1024]{1,0:T(8,128)(2,1)S(1)} %slice_bitcast_fusion.1.own_ref, bf16[144,1024]{1,0:T(8,128)(2,1)S(1)} %slice_bitcast_fusion.got_ref, ...), custom_call_target="tpu_custom_call" | custom-call | flops 301989888 | bytes 4177940 | tf_op jit(solution)/shard_map/finish/pallas_call | solution.py:315
  (48 shorter events, 13.1 us)
Async XLA Ops:
  4.8 43.7 %all-to-all-start = ((bf16[8,256,768]{2,1,0:T(8,128)(2,1)}), bf16[8,256,768]{2,1,0:T(8,128)(2,1)S(1)}, u32[]{:S(2)}, u32[]{:S(2)}) async-start(bf16[8,256,768]{2,1,0:T(8,128)(2,1)} %pack_heads.1), calls=%async_computation | async-start | bytes 6291456 | tf_op jit(solution)/shard_map/all_to_all | solution.py:580
  11.0 37.6 %copy-start.6 = (s32[5]{0:T(128)}, s32[5]{0:T(128)S(1)}, u32[]{:S(2)}) copy-start(s32[5]{0:T(128)S(1)} %stack.23.place_ref) | copy-start | bytes 64
  11.0 1.7 copy-start.1
  15.1 0.8 copy-start.9
  48.5 21.5 %copy-start = (bf16[8,256,768]{2,1,0:T(8,128)(2,1)}, bf16[8,256,768]{2,1,0:T(8,128)(2,1)S(1)}, u32[]{:S(2)}) copy-start(bf16[8,256,768]{2,1,0:T(8,128)(2,1)S(1)} %all-to-all-done.own_ref.own_kv_ref) | copy-start | bytes 9437188
  48.6 5.2 %collective-permute-start = (bf16[8,256,256]{2,1,0:T(8,128)(2,1)S(1)}, bf16[8,256,256]{2,1,0:T(8,128)(2,1)S(1)}, u32[]{:S(2)}, u32[]{:S(2)}) collective-permute-start(bf16[8,256,256]{2,1,0:T(8,128)(2,1)S(1)} %slice.9), channel_id=1, source_target_pairs={{0,2},{2,0},{4,6},{6,4},{8,10},{10,8},{12,14},{14,12},{16,18},{18,... | collective-permute-start | bytes 3145736 | tf_op jit(solution)/shard_map/ppermute | solution.py:583
  48.7 27.3 %collective-permute-start.2 = (bf16[2,576,256]{2,1,0:T(8,128)(2,1)}, bf16[2,576,256]{2,1,0:T(8,128)(2,1)}, u32[]{:S(2)}, u32[]{:S(2)}) collective-permute-start(bf16[2,576,256]{2,1,0:T(8,128)(2,1)} %get-tuple-element.46), channel_id=1, source_target_pairs={{0,4},{2,6},{4,0},{6,2},{8,12},{10,14},{12,8},{14,10},{16,20},{18,... | collective-permute-start | bytes 1769480 | tf_op jit(solution)/shard_map/ppermute | solution.py:583
  50.3 25.7 %collective-permute-start.3 = (bf16[2,576,256]{2,1,0:T(8,128)(2,1)}, bf16[2,576,256]{2,1,0:T(8,128)(2,1)}, u32[]{:S(2)}, u32[]{:S(2)}) collective-permute-start(bf16[2,576,256]{2,1,0:T(8,128)(2,1)} %get-tuple-element.47), channel_id=1, source_target_pairs={{0,16},{2,18},{4,20},{6,22},{8,24},{10,26},{12,28},{14,30},{16,0},... | collective-permute-start | bytes 1769480 | tf_op jit(solution)/shard_map/ppermute | solution.py:583
  52.2 27.9 %collective-permute-start.4 = (bf16[2,576,256]{2,1,0:T(8,128)(2,1)}, bf16[2,576,256]{2,1,0:T(8,128)(2,1)}, u32[]{:S(2)}, u32[]{:S(2)}) collective-permute-start(bf16[2,576,256]{2,1,0:T(8,128)(2,1)} %get-tuple-element.48), channel_id=1, source_target_pairs={{0,20},{2,22},{4,16},{6,18},{8,28},{10,30},{12,24},{14,26},{16,4},... | collective-permute-start | bytes 1769480 | tf_op jit(solution)/shard_map/ppermute | solution.py:583
  53.8 16.3 %copy-start.8 = (bf16[8,256,256]{2,1,0:T(8,128)(2,1)}, bf16[8,256,256]{2,1,0:T(8,128)(2,1)S(1)}, u32[]{:S(2)}) copy-start(bf16[8,256,256]{2,1,0:T(8,128)(2,1)S(1)} %collective-permute-done.other_ref) | copy-start | bytes 3145732
  70.9 1.9 %collective-permute-start.1 = (bf16[8,256,128]{2,1,0:T(8,128)(2,1)S(1)}, bf16[8,256,128]{2,1,0:T(8,128)(2,1)S(1)}, u32[]{:S(2)}, u32[]{:S(2)}) collective-permute-start(bf16[8,256,128]{2,1,0:T(8,128)(2,1)S(1)} %get-tuple-element.44), channel_id=1, source_target_pairs={{0,2},{2,0},{4,6},{6,4},{8,10},{10,8},{12,14},{14,12},{16,18},{18,... | collective-permute-start | bytes 1572872 | tf_op jit(solution)/shard_map/ppermute | solution.py:583
  80.1 36.3 %all-to-all-start.1 = ((bf16[8,4,256,128]{3,2,1,0:T(8,128)(2,1)}), bf16[8,4,256,128]{3,2,1,0:T(8,128)(2,1)S(1)}, u32[]{:S(2)}, u32[]{:S(2)}) async-start(bf16[8,4,256,128]{3,2,1,0:T(8,128)(2,1)} %bitcast.29), calls=%async_computation.1 | async-start | bytes 4194304 | tf_op jit(solution)/shard_map/all_to_all | solution.py:580
  111.4 2.1 %collective-permute-start.5 = (bf16[8,256,128]{2,1,0:T(8,128)(2,1)}, bf16[8,256,128]{2,1,0:T(8,128)(2,1)S(1)}, u32[]{:S(2)}, u32[]{:S(2)}) collective-permute-start(bf16[8,256,128]{2,1,0:T(8,128)(2,1)} %get-tuple-element.57), channel_id=1, source_target_pairs={{0,2},{2,0},{4,6},{6,4},{8,10},{10,8},{12,14},{14,12},{16,18},{18,... | collective-permute-start | bytes 1572872 | tf_op jit(solution)/shard_map/ppermute | solution.py:583
  116.4 1.4 copy-start.12
  117.7 28.8 %all-to-all-start.2 = ((bf16[8,256,384]{2,1,0:T(8,128)(2,1)}), bf16[8,256,384]{2,1,0:T(8,128)(2,1)S(1)}, u32[]{:S(2)}, u32[]{:S(2)}) async-start(bf16[8,256,384]{2,1,0:T(8,128)(2,1)} %pack_scores.1), calls=%async_computation.2 | async-start | bytes 3145728 | tf_op jit(solution)/shard_map/all_to_all | solution.py:580
  124.9 9.5 %copy-start.7 = (s32[5]{0:T(128)S(1)}, s32[5]{0:T(128)}, u32[]{:S(2)}) copy-start(s32[5]{0:T(128)} %copy-done.6) | copy-start | bytes 64
  131.3 3.1 %collective-permute-start.6 = (bf16[2,288,1024]{2,1,0:T(8,128)(2,1)}, bf16[2,288,1024]{2,1,0:T(8,128)(2,1)S(1)}, u32[]{:S(2)}, u32[]{:S(2)}) collective-permute-start(bf16[2,288,1024]{2,1,0:T(8,128)(2,1)} %get-tuple-element.60), channel_id=1, source_target_pairs={{0,2},{2,0},{4,6},{6,4},{8,10},{10,8},{12,14},{14,12},{16,18},{18,... | collective-permute-start | bytes 3538952 | tf_op jit(solution)/shard_map/ppermute | solution.py:583
  134.4 1.3 copy-start.3
  138.6 30.0 %copy-start.5 = (s32[4,1024]{1,0:T(4,128)S(1)}, s32[4,1024]{1,0:T(4,128)}, u32[]{:S(2)}) copy-start(s32[4,1024]{1,0:T(4,128)} %signs_ref.1) | copy-start | bytes 49156
  138.6 17.7 %collective-permute-start.7 = (bf16[144,1024]{1,0:T(8,128)(2,1)}, bf16[144,1024]{1,0:T(8,128)(2,1)S(1)}, u32[]{:S(2)}, u32[]{:S(2)}) collective-permute-start(bf16[144,1024]{1,0:T(8,128)(2,1)} %get-tuple-element.68), channel_id=1, source_target_pairs={{1,104},{3,106},{5,108},{7,110},{9,96},{11,98},{13,100},{15,102},{... | collective-permute-start | bytes 884744 | tf_op jit(solution)/shard_map/ppermute | solution.py:618
  146.5 16.6 %collective-permute-start.10 = (bf16[144,1024]{1,0:T(8,128)(2,1)}, bf16[144,1024]{1,0:T(8,128)(2,1)S(1)}, u32[]{:S(2)}, u32[]{:S(2)}) collective-permute-start(bf16[144,1024]{1,0:T(8,128)(2,1)} %get-tuple-element.71), channel_id=1, source_target_pairs={{1,105},{3,107},{5,109},{7,111},{9,97},{11,99},{13,101},{15,103},{... | collective-permute-start | bytes 884744 | tf_op jit(solution)/shard_map/ppermute | solution.py:618
  146.5 22.1 %copy-start.2 = (bf16[1024,1024]{1,0:T(8,128)(2,1)S(1)}, bf16[1024,1024]{1,0:T(8,128)(2,1)}, u32[]{:S(2)}) copy-start(bf16[1024,1024]{1,0:T(8,128)(2,1)} %constant.22.clone.turn_ref) | copy-start | bytes 6291460
  146.5 16.6 %collective-permute-start.8 = (bf16[144,1024]{1,0:T(8,128)(2,1)}, bf16[144,1024]{1,0:T(8,128)(2,1)S(1)}, u32[]{:S(2)}, u32[]{:S(2)}) collective-permute-start(bf16[144,1024]{1,0:T(8,128)(2,1)} %copy-done.11), channel_id=1, source_target_pairs={{1,96},{3,98},{5,100},{7,102},{9,104},{11,106},{13,108},{15,110},{... | collective-permute-start | bytes 884744 | tf_op jit(solution)/shard_map/ppermute | solution.py:618
  151.5 17.1 %collective-permute-start.9 = (bf16[144,1024]{1,0:T(8,128)(2,1)}, bf16[144,1024]{1,0:T(8,128)(2,1)S(1)}, u32[]{:S(2)}, u32[]{:S(2)}) collective-permute-start(bf16[144,1024]{1,0:T(8,128)(2,1)} %copy-done.10), channel_id=1, source_target_pairs={{1,97},{3,99},{5,101},{7,103},{9,105},{11,107},{13,109},{15,111},{... | collective-permute-start | bytes 884744 | tf_op jit(solution)/shard_map/ppermute | solution.py:618
  (5 other events, 3.8 us)

commit v3 on v2

--- a/solution.py
+++ b/solution.py
@@ -32,17 +32,23 @@
     )
 
 
-def for_window(step, parity, span, one):
+def full_window(span):
+    return ["far"] + ["middle"] * (span - 1) + ["near"]
+
+
+def early_windows(step, parity, span, one):
     block = 2 * step + parity
     for early in range(span // 2):
+
         @pl.when(step == early)
         def _():
-            one(jnp.maximum(block - 2 * early - 1, 0), ["maybe"])
-            one(block - 2 * early, ["middle"] * (2 * early) + ["near"])
-
-    @pl.when(step >= span // 2)
-    def _():
-        one(block - span, ["far"] + ["middle"] * (span - 1) + ["near"])
+            distance = 2 * early
+            one(
+                [
+                    (jnp.maximum(block - distance - 1, 0), 0, ["maybe"]),
+                    (block - distance, 1, ["middle"] * distance + ["near"]),
+                ]
+            )
 
 
 def weights(s, kind, parity):
@@ -59,10 +65,6 @@
     return capped, e
 
 
-def first_slot(place, kinds, block, span):
-    return 0 if kinds == ["maybe"] else place - block + span
-
-
 def blocks_at(ref, place, kinds):
     block = ref[pl.ds(place, len(kinds))]
     return block.reshape(len(kinds) * block.shape[1], block.shape[2])
@@ -72,8 +74,34 @@
     return jnp.sum(x.reshape(x.shape[0] // 8, 8, x.shape[1]), axis=0)
 
 
+def turned_rows(x, scale):
+    scale = jnp.transpose(jnp.broadcast_to(scale, (x.shape[1], x.shape[0])))
+    return (x.astype(jnp.float32) * scale).astype(jnp.bfloat16)
+
+
+def store_query_gradient(ref, turned):
+    rows = turned.shape[1] // 2
+    dq = jnp.transpose(turned).astype(jnp.bfloat16)
+    ref[0, :, : turned.shape[0]] = dq[:rows]
+    ref[0, :, turned.shape[0] :] = dq[rows:]
+
+
 def value_kernel(
-    parity_ref, own_ref, own_kv_ref, other_ref, mine_ref, theirs_ref, k_s, dv_s, e_s, l_s
+    parity_ref,
+    own_ref,
+    own_kv_ref,
+    other_ref,
+    dq_ref,
+    dk_ref,
+    mine_ref,
+    theirs_ref,
+    k_s,
+    v_s,
+    kt_s,
+    dv_s,
+    e_s,
+    u_s,
+    dp_s,
 ):
     chips, rows, _ = own_kv_ref.shape
     span = WINDOW // rows
@@ -88,33 +116,69 @@
         def _(j):
             k_s[2 * j + parity] = own_kv_ref[j, :, :head]
             k_s[2 * j + 1 - parity] = other_ref[j, :, :head]
+
+        @pl.loop(0, span // 2)
+        def _(j):
+            v_s[2 * j + parity] = own_kv_ref[j, :, head:]
+            v_s[2 * j + 1 - parity] = other_ref[j, :, head:]
+
+        @pl.loop(0, span)
+        def _(j):
+            kt_s[j] = jnp.transpose(k_s[j])
+
         dv_s[...] = jnp.zeros_like(dv_s)
+        dk_ref[...] = jnp.zeros_like(dk_ref)
 
     q2 = pair(own_ref, 0)
     g2 = pair(own_ref, 2)
-    l_s[...] = jnp.zeros_like(l_s)
-
-    def first_pass(place, kinds):
-        slot = first_slot(place, kinds, block, span)
-        sums = l_s[...]
+
+    def early(runs):
+        sums = jnp.zeros((8, 2 * rows), jnp.float32)
+        products = jnp.zeros((8, 2 * rows), jnp.float32)
+        for place, slot, kinds in runs:
+            s = dot(blocks_at(k_s, place, kinds), q2, (1, 1))
+            dps = dot(blocks_at(v_s, place, kinds), g2, (1, 1))
+            for i, kind in enumerate(kinds):
+                capped, e = weights(s[i * rows : (i + 1) * rows], kind, parity)
+                dp = dps[i * rows : (i + 1) * rows]
+                sums = sums + column_sums(e)
+                products = products + column_sums(e * dp)
+                e_s[slot + i] = e.astype(jnp.bfloat16)
+                u_s[slot + i] = (e - e * (capped * capped)).astype(jnp.bfloat16)
+                dp_s[slot + i] = dp
+        inverse = 1.0 / jnp.sum(sums, axis=0, keepdims=True)
+        delta = jnp.sum(products, axis=0, keepdims=True) * inverse
+        g2_scaled = turned_rows(g2, inverse)
+        q2_scaled = turned_rows(q2, inverse * SCORE_SCALE)
+        turned = jnp.zeros((head, 2 * rows), jnp.float32)
+        for place, slot, kinds in runs:
+            n = len(kinds)
+            grad = [
+                u_s[slot + i] * (dp_s[slot + i] - delta).astype(jnp.bfloat16) for i in range(n)
+            ]
+            grad = jnp.concatenate(grad, axis=0)
+            term = dot(blocks_at(e_s, slot, kinds), g2_scaled, (1, 0))
+            dv_s[pl.ds(place, n)] += term.reshape(n, rows, head)
+            dk_ref[pl.ds(place, n)] += dot(grad, q2_scaled, (1, 0)).reshape(n, rows, head)
+            keys = jnp.concatenate([kt_s[place + i] for i in range(n)], axis=1)
+            turned = turned + dot(keys, grad, (1, 0))
+        store_query_gradient(dq_ref, turned * (inverse * SCORE_SCALE))
+
+    early_windows(step, parity, span, early)
+
+    @pl.when(step >= span // 2)
+    def _():
+        kinds = full_window(span)
+        place = block - span
         s = dot(blocks_at(k_s, place, kinds), q2, (1, 1))
+        sums = jnp.zeros((8, 2 * rows), jnp.float32)
         for i, kind in enumerate(kinds):
             _, e = weights(s[i * rows : (i + 1) * rows], kind, parity)
             sums = sums + column_sums(e)
-            e_s[slot + i] = e.astype(jnp.bfloat16)
-        l_s[...] = sums
-
-    for_window(step, parity, span, first_pass)
-    inverse = 1.0 / jnp.sum(l_s[...], axis=0, keepdims=True)
-    inverse_t = jnp.transpose(jnp.broadcast_to(inverse, (head, 2 * rows)))
-    g2_scaled = (g2.astype(jnp.float32) * inverse_t).astype(jnp.bfloat16)
-
-    def second_pass(place, kinds):
-        slot = first_slot(place, kinds, block, span)
-        term = dot(blocks_at(e_s, slot, kinds), g2_scaled, (1, 0))
-        dv_s[pl.ds(place, len(kinds))] += term.reshape(len(kinds), rows, head)
-
-    for_window(step, parity, span, second_pass)
+            e_s[i] = e.astype(jnp.bfloat16)
+        g2_scaled = turned_rows(g2, 1.0 / jnp.sum(sums, axis=0, keepdims=True))
+        term = dot(blocks_at(e_s, 0, kinds), g2_scaled, (1, 0))
+        dv_s[pl.ds(place, span + 1)] += term.reshape(span + 1, rows, head)
 
     @pl.when(step == chips - 1)
     def _():
@@ -129,6 +193,8 @@
     own_ref,
     own_kv_ref,
     other_ref,
+    _,
+    dk_ref,
     dq_ref,
     mine_ref,
     theirs_ref,
@@ -138,75 +204,54 @@
     dk_s,
     u_s,
     dp_s,
-    l_s,
-    d_s,
-    dqt_s,
 ):
     chips, rows, _ = own_kv_ref.shape
     span = WINDOW // rows
     head = HEAD_SIZE
     parity = parity_ref[0]
     step = pl.program_id(0)
-    block = 2 * step + parity
+    place = 2 * (step + span // 2) + parity - span
 
     @pl.when(step == 0)
     def _():
         @pl.loop(0, chips)
         def _(j):
             mine, theirs = 2 * j + parity, 2 * j + 1 - parity
-            for place, k, v in (
+            for to, k, v in (
                 (mine, own_kv_ref[j, :, :head], own_kv_ref[j, :, head:]),
                 (theirs, other_ref[j, :, :head], other_ref[j, :, head:]),
             ):
-                k_s[place] = k
-                v_s[place] = v
-                kt_s[place] = jnp.transpose(k)
-        dk_s[...] = jnp.zeros_like(dk_s)
+                k_s[to] = k
+                v_s[to] = v
+                kt_s[to] = jnp.transpose(k)
+
+        dk_s[:span] = dk_ref[...]
+        dk_s[span:] = jnp.zeros((2 * chips - span, rows, head), jnp.float32)
 
     q2 = pair(own_ref, 0)
     g2 = pair(own_ref, 2)
-    l_s[...] = jnp.zeros_like(l_s)
-    d_s[...] = jnp.zeros_like(d_s)
-    dqt_s[...] = jnp.zeros_like(dqt_s)
-
-    def first_pass(place, kinds):
-        slot = first_slot(place, kinds, block, span)
-        sums, products = l_s[...], d_s[...]
-        s = dot(blocks_at(k_s, place, kinds), q2, (1, 1))
-        dps = dot(blocks_at(v_s, place, kinds), g2, (1, 1))
-        for i, kind in enumerate(kinds):
-            capped, e = weights(s[i * rows : (i + 1) * rows], kind, parity)
-            dp = dps[i * rows : (i + 1) * rows]
-            sums = sums + column_sums(e)
-            products = products + column_sums(e * dp)
-            u_s[slot + i] = (e - e * (capped * capped)).astype(jnp.bfloat16)
-            dp_s[slot + i] = dp
-        l_s[...] = sums
-        d_s[...] = products
-
-    for_window(step, parity, span, first_pass)
-    inverse = 1.0 / jnp.sum(l_s[...], axis=0, keepdims=True)
-    delta = jnp.sum(d_s[...], axis=0, keepdims=True) * inverse
-    inverse_t = jnp.transpose(jnp.broadcast_to(inverse * SCORE_SCALE, (head, 2 * rows)))
-    q2_scaled = (q2.astype(jnp.float32) * inverse_t).astype(jnp.bfloat16)
-
-    def second_pass(place, kinds):
-        slot = first_slot(place, kinds, block, span)
-        n = len(kinds)
-        grads = [
-            u_s[slot + i] * (dp_s[slot + i] - delta).astype(jnp.bfloat16) for i in range(n)
-        ]
-        score_grad = jnp.concatenate(grads, axis=0)
-        dk_s[pl.ds(place, n)] += dot(score_grad, q2_scaled, (1, 0)).reshape(n, rows, head)
-        turned = jnp.concatenate([kt_s[place + i] for i in range(n)], axis=1)
-        dqt_s[...] += dot(turned, score_grad, (1, 0))
-
-    for_window(step, parity, span, second_pass)
-    dq = jnp.transpose(dqt_s[...] * (inverse * SCORE_SCALE)).astype(jnp.bfloat16)
-    dq_ref[0, :, :head] = dq[:rows]
-    dq_ref[0, :, head:] = dq[rows:]
-
-    @pl.when(step == chips - 1)
+    kinds = full_window(span)
+    s = dot(blocks_at(k_s, place, kinds), q2, (1, 1))
+    dps = dot(blocks_at(v_s, place, kinds), g2, (1, 1))
+    sums = jnp.zeros((8, 2 * rows), jnp.float32)
+    products = jnp.zeros((8, 2 * rows), jnp.float32)
+    for i, kind in enumerate(kinds):
+        capped, e = weights(s[i * rows : (i + 1) * rows], kind, parity)
+        dp = dps[i * rows : (i + 1) * rows]
+        sums = sums + column_sums(e)
+        products = products + column_sums(e * dp)
+        u_s[i] = (e - e * (capped * capped)).astype(jnp.bfloat16)
+        dp_s[i] = dp
+    inverse = 1.0 / jnp.sum(sums, axis=0, keepdims=True)
+    delta = jnp.sum(products, axis=0, keepdims=True) * inverse
+    q2_scaled = turned_rows(q2, inverse * SCORE_SCALE)
+    grad = [u_s[i] * (dp_s[i] - delta).astype(jnp.bfloat16) for i in range(span + 1)]
+    grad = jnp.concatenate(grad, axis=0)
+    dk_s[pl.ds(place, span + 1)] += dot(grad, q2_scaled, (1, 0)).reshape(span + 1, rows, head)
+    keys = jnp.concatenate([kt_s[place + i] for i in range(span + 1)], axis=1)
+    store_query_gradient(dq_ref, dot(keys, grad, (1, 0)) * (inverse * SCORE_SCALE))
+
+    @pl.when(step == chips - span // 2 - 1)
     def _():
         @pl.loop(0, chips)
         def _(j):
@@ -214,26 +259,32 @@
             theirs_ref[j] = dk_s[2 * j + 1 - parity].astype(jnp.bfloat16)
 
 
-def attention_call(kernel, name, parity, own, other, with_query, scratch, products, vmem):
-    chips, rows, _ = own.shape
+def attention_call(kernel, name, operands, first, more_in, more_out, scratch, products, vmem):
+    chips, rows, _ = operands[1].shape
     head = HEAD_SIZE
+    early = WINDOW // rows // 2
     grads = jax.ShapeDtypeStruct((chips, rows, head), jnp.bfloat16)
-    out_shape, out_specs = [grads, grads], [WHOLE, WHOLE]
-    if with_query:
-        out_shape.insert(0, jax.ShapeDtypeStruct((chips, rows, 3 * head), jnp.bfloat16))
-        out_specs.insert(0, pl.BlockSpec((1, rows, 2 * head), lambda t: (t, 0, 0)))
+    payload = jax.ShapeDtypeStruct((chips, rows, 3 * head), jnp.bfloat16)
+
+    def query_block(t):
+        return (t + first if first else jnp.minimum(t, early - 1), 0, 0)
+
     return pl.pallas_call(
         kernel,
-        grid=(chips,),
-        out_shape=out_shape,
+        grid=(chips - first,),
+        out_shape=[payload] + [shape for shape, _ in more_out] + [grads, grads],
         in_specs=[
             SCALAR,
-            pl.BlockSpec((1, rows, 4 * head), lambda t: (t, 0, 0)),
+            pl.BlockSpec((1, rows, 4 * head), lambda t: (t + first, 0, 0)),
             pl.BlockSpec((chips, rows, 2 * head), lambda t: (0, 0, 2), pipeline_mode=pl.Buffered(1)),
             WHOLE,
-        ],
-        out_specs=out_specs,
+        ]
+        + more_in,
+        out_specs=[pl.BlockSpec((1, rows, 2 * head), query_block)]
+        + [spec for _, spec in more_out]
+        + [WHOLE, WHOLE],
         scratch_shapes=[pltpu.VMEM(shape, kind) for shape, kind in scratch],
+        input_output_aliases={4: 0} if first else {},
         compiler_params=pltpu.CompilerParams(
             dimension_semantics=("arbitrary",), vmem_limit_bytes=vmem * 2**20
         ),
@@ -243,50 +294,53 @@
             transcendentals=2 * 112 * rows * rows,
         ),
         name=name,
-    )(parity, own, own, other)
+    )(*operands)
 
 
 def value_gradients(parity, own, other):
     chips, rows, _ = own.shape
-    slots = WINDOW // rows + 1
+    span = WINDOW // rows
+    head = HEAD_SIZE
+    dk = jax.ShapeDtypeStruct((span, rows, head), jnp.float32)
     return attention_call(
         value_kernel,
         "value_gradients",
-        parity,
-        own,
-        other,
-        False,
+        (parity, own, own, other),
+        0,
+        [],
+        [(dk, WHOLE)],
         [
-            ((2 * chips, rows, HEAD_SIZE), jnp.bfloat16),
-            ((2 * chips, rows, HEAD_SIZE), jnp.float32),
-            ((slots, rows, 2 * rows), jnp.bfloat16),
-            ((8, 2 * rows), jnp.float32),
+            ((2 * chips, rows, head), jnp.bfloat16),
+            ((span, rows, head), jnp.bfloat16),
+            ((span, head, rows), jnp.bfloat16),
+            ((2 * chips, rows, head), jnp.float32),
+            ((span + 1, rows, 2 * rows), jnp.bfloat16),
+            ((span, rows, 2 * rows), jnp.bfloat16),
+            ((span, rows, 2 * rows), jnp.float32),
         ],
         4,
         28,
     )
 
 
-def score_gradients(parity, own, other):
+def score_gradients(parity, own, other, payload, dk):
     chips, rows, _ = own.shape
-    slots = WINDOW // rows + 1
+    span = WINDOW // rows
+    head = HEAD_SIZE
     return attention_call(
         score_kernel,
         "score_gradients",
-        parity,
-        own,
-        other,
-        True,
+        (parity, own, own, other, payload, dk),
+        span // 2,
+        [pl.BlockSpec(memory_space=pl.ANY), WHOLE],
+        [],
         [
-            ((2 * chips, rows, HEAD_SIZE), jnp.bfloat16),
-            ((2 * chips, rows, HEAD_SIZE), jnp.bfloat16),
-            ((2 * chips, HEAD_SIZE, rows), jnp.bfloat16),
-            ((2 * chips, rows, HEAD_SIZE), jnp.float32),
-            ((slots, rows, 2 * rows), jnp.bfloat16),
-            ((slots, rows, 2 * rows), jnp.float32),
-            ((8, 2 * rows), jnp.float32),
-            ((8, 2 * rows), jnp.float32),
-            ((HEAD_SIZE, 2 * rows), jnp.float32),
+            ((2 * chips, rows, head), jnp.bfloat16),
+            ((2 * chips, rows, head), jnp.bfloat16),
+            ((2 * chips, head, rows), jnp.bfloat16),
+            ((2 * chips, rows, head), jnp.float32),
+            ((span + 1, rows, 2 * rows), jnp.bfloat16),
+            ((span + 1, rows, 2 * rows), jnp.float32),
         ],
         8,
         60,
@@ -339,7 +393,7 @@
 
     rows = queries.shape[0]
     arrays = (queries, output_gradient, saved_keys, saved_values)
-    part = rows // 4
+    part = rows // 2
     total = sum(x.shape[1] for x in arrays) // heads
     (packed,) = small_call(
         kernel,
@@ -425,7 +479,7 @@
         grid=(2,),
         in_specs=[pl.BlockSpec((2, 1, 2, rows, head), lambda p: (0, p, 0, 0, 0))] * 2,
         out_specs=[pl.BlockSpec((2, 1, 2, 4, rows, head), lambda p: (0, p, 0, 0, 0, 0))],
-        vmem=60,
+        vmem=16,
     )
     return packed.reshape(chips, 4, rows, head)
 
@@ -509,17 +563,18 @@
 
 
 def cut_pieces(place, keep, got):
-    def kernel(place_ref, keep_ref, got_ref, cross_other_ref, cross_own_ref, stay_ref, second_ref):
+    def kernel(place_ref, keep_ref, got_ref, cross_other_ref, cross_own_ref, stay_ref, second_ref, own_ref):
         mirror = place_ref[3]
         cross_other_ref[...] = add(keep_ref[0, 1 - mirror], got_ref[0, 1 - mirror])
         cross_own_ref[...] = add(keep_ref[1, 1 - mirror], got_ref[1, 1 - mirror])
         stay_ref[...] = add(keep_ref[0, mirror], got_ref[0, mirror])
         second_ref[...] = add(keep_ref[1, 1], got_ref[1, 1])
+        own_ref[...] = add(keep_ref[1, 0], got_ref[1, 0])
 
     return small_call(
         kernel,
         "cut_pieces",
-        [keep.shape[2:]] * 4,
+        [keep.shape[2:]] * 5,
         [],
         0,
         place,
@@ -530,9 +585,8 @@
 
 
 def finish(place, signs, turn, pieces):
-    def kernel(place_ref, signs_ref, turn_ref, own_ref, got_ref, near_ref, near2_ref, far_ref, other_ref, out_ref):
-        own = add32(own_ref[...], got_ref[...])
-        total = jnp.where(place_ref[3] == 0, own, far_ref[...].astype(jnp.float32))
+    def kernel(place_ref, signs_ref, turn_ref, own_ref, near_ref, near2_ref, far_ref, other_ref, out_ref):
+        total = jnp.where(place_ref[3] == 0, own_ref[...], far_ref[...]).astype(jnp.float32)
         total = total + add32(near_ref[...], near2_ref[...]) + other_ref[...].astype(jnp.float32)
         signs = signs_ref[pl.ds(place_ref[4], 1)].astype(jnp.float32)
         out_ref[...] = dot((total * signs).astype(jnp.bfloat16), turn_ref[...], (1, 0))
@@ -548,7 +602,7 @@
         signs,
         turn,
         *pieces,
-        in_specs=[SCALAR] + [WHOLE] * 8,
+        in_specs=[SCALAR] + [WHOLE] * 7,
         kind=jnp.float32,
     )
     return out
@@ -591,12 +645,12 @@
     parity = core.reshape(1)
     columns = turned[:1] + [swap(turned[d], (d & 1) * 2 + (d >> 1) * 8) for d in range(1, 4)]
 
-    dv_mine, dv_theirs = value_gradients(parity, own, other)
+    scores, dk, dv_mine, dv_theirs = value_gradients(parity, own, other)
     values = pack_values(dv_mine, swap(dv_theirs, 1))
     values, own, *columns = lax.optimization_barrier((values, own, *columns))
     values_back = across(values)
 
-    scores, dk_mine, dk_theirs = score_gradients(parity, own, other)
+    scores, dk_mine, dk_theirs = score_gradients(parity, own, other, scores, dk)
     scores = pack_scores(scores, dk_mine, swap(dk_theirs, 1))
     values_back, scores = lax.optimization_barrier((values_back, scores))
     scores_back = across(scores)
@@ -606,7 +660,7 @@
     keep = keep.reshape(2, 2, -1, width)
     got = got.reshape(keep.shape)
     sections = lax.axis_size("section")
-    cross_other, cross_own, stay_other, second_own = cut_pieces(place, keep, got)
+    cross_other, cross_own, stay_other, second_own, first_own = cut_pieces(place, keep, got)
 
     def routed(block, route, group):
         axes = ("section", "ctx", "mirror")
@@ -629,7 +683,7 @@
         place,
         hadamard_signs,
         jnp.asarray(hadamard(width), jnp.bfloat16),
-        (keep[1, 0], got[1, 0], near_other, near_own, far_own, other),
+        (first_own, near_other, near_own, far_own, other),
     )
     query_gradient, key_gradient = unpack_scores(scores_back)
     return (

time: 171 us -> 166 us (0.971)
  Pallas kernels: 65.7 us -> 58.9 us
  waiting for transfers between devices: 56.1 us -> 51.1 us
  starting transfers between devices: 38 us -> 41.7 us
  local copies, waits for them, and re-layouts: 10.1 us -> 12.6 us
    ppermute x4, starting transfers between devices: 14.8 us -> 20.1 us  [routed(): return lax.ppermute(block, axes, pairs)]
    pallas_call x2, Pallas kernels: 42.8 us -> 39.2 us  [attention_call(): pl.pallas_call(kernel, grid=(chips - first,), out_shape=[payload] + [shap...]
    ppermute x4, waiting for transfers between devices: 12.3 us -> 8.68 us  [routed(): return lax.ppermute(block, axes, pairs)]
    unnamed x30 -> x44, local copies, waits for them, and re-layouts: 8.95 us -> 12.5 us
    ppermute x7, waiting for transfers between devices: 11.1 us -> 7.76 us  [swap(): return lax.ppermute(block, 'ctx', [(i, i ^ bits) for i in range(2 * chips)])]
    pallas_call x8, Pallas kernels: 22.8 us -> 19.7 us  [small_call(): pl.pallas_call(kernel, out_shape=kinds, in_specs=in_specs if in_specs is...]
    all_to_all x3, waiting for transfers between devices: 32.6 us -> 34.6 us  [across(): lax.all_to_all(block, 'ctx', 0, 0, tiled=True, axis_index_groups=same_core)]
    all_to_all x3, starting transfers between devices: 18 us -> 16.3 us  [across(): lax.all_to_all(block, 'ctx', 0, 0, tiled=True, axis_index_groups=same_core)]
  transfers between devices with their start and end apart: 14 -> 14, of which waited for: 7 -> 9; matrix products, arithmetic and copies ran while one was open for 1% -> 0% of each run, Pallas kernels for 35% -> 33%
where the time goes in v3:
time: 166 us; the launch traced here: 165 us
  Pallas kernels  58.9 us (35%)
  waiting for transfers between devices  51.1 us (31%)
  starting transfers between devices  41.7 us (25%)
  local copies, waits for them, and re-layouts  12.6 us (8%)
    pallas_call x2, Pallas kernels, attention_call(): pl.pallas_call(kernel, grid=(chips - first,), out_shape=[payload] + [shap...  39.2 us
    all_to_all x3, waiting for transfers between devices, across(): lax.all_to_all(block, 'ctx', 0, 0, tiled=True, axis_index_groups=same_core)  34.6 us
    ppermute x4, starting transfers between devices, routed(): return lax.ppermute(block, axes, pairs)  20.1 us
    pallas_call x8, Pallas kernels, small_call(): pl.pallas_call(kernel, out_shape=kinds, in_specs=in_specs if in_specs is...  19.7 us
    all_to_all x3, starting transfers between devices, across(): lax.all_to_all(block, 'ctx', 0, 0, tiled=True, axis_index_groups=same_core)  16.3 us
    unnamed x44, local copies, waits for them, and re-layouts  12.5 us
    ppermute x4, waiting for transfers between devices, routed(): return lax.ppermute(block, axes, pairs)  8.68 us
    ppermute x7, waiting for transfers between devices, swap(): return lax.ppermute(block, 'ctx', [(i, i ^ bits) for i in range(2 * chips)])  7.76 us
  transfers between devices with their start and end apart: 14, of which 9 were waited for; matrix products, arithmetic and copies ran while one was open for 0% of the time, Pallas kernels for 33%

profile of v3, /device:TPU:2, one launch (start us, length us, event | category | flops | bytes accessed | tf_op | source)
XLA Modules:
  0.0 165.1 jit_solution(3713927712061170741)
XLA Ops:
  0.6 3.2 %pack_heads.1 = bf16[8,256,768]{2,1,0:T(8,128)(2,1)} custom-call(bf16[256,2048]{1,0:T(8,128)(2,1)} %bitcast.24, bf16[256,2048]{1,0:T(8,128)(2,1)} %bitcast.25, bf16[256,1024]{1,0:T(8,128)(2,1)} %bitcast.27, bf16[256,1024]{1,0:T(8,128)(2,1)} %bitcast.28), custom_call_target="tpu_custom_call" | custom-call | bytes 6291456 | tf_op jit(solution)/shard_map/pack_heads/pallas_call | solution.py:369
  3.8 6.0 %all-to-all-start = ((bf16[8,256,768]{2,1,0:T(8,128)(2,1)}), bf16[8,256,768]{2,1,0:T(8,128)(2,1)S(1)}, u32[]{:S(2)}, u32[]{:S(2)}) async-start(bf16[8,256,768]{2,1,0:T(8,128)(2,1)} %pack_heads.1), calls=%async_computation | async-start | bytes 6291456 | tf_op jit(solution)/shard_map/all_to_all | solution.py:634
  9.9 1.7 %copy-done.2 = bf16[1,1,256,4608]{3,2,1,0:T(8,128)(2,1)S(1)} copy-done((bf16[1,1,256,4608]{3,2,1,0:T(8,128)(2,1)S(1)}, bf16[1,1,256,4608]{3,2,1,0:T(8,128)(2,1)}, u32[]{:S(2)}) %copy-start.2) | copy-done | bytes 2359320
  16.2 31.3 %all-to-all-done.own_ref.own_kv_ref = bf16[8,256,768]{2,1,0:T(8,128)(2,1)S(1)} async-done(((bf16[8,256,768]{2,1,0:T(8,128)(2,1)}), bf16[8,256,768]{2,1,0:T(8,128)(2,1)S(1)}, u32[]{:S(2)}, u32[]{:S(2)}) %all-to-all-start) | async-done | bytes 3145760 | tf_op jit(solution)/shard_map/all_to_all | solution.py:634
  50.5 1.9 %collective-permute-start.3 = (bf16[2,576,256]{2,1,0:T(8,128)(2,1)S(1)}, bf16[2,576,256]{2,1,0:T(8,128)(2,1)S(1)}, u32[]{:S(2)}, u32[]{:S(2)}) collective-permute-start(bf16[2,576,256]{2,1,0:T(8,128)(2,1)S(1)} %copy-done.13), channel_id=1, source_target_pairs={{0,16},{2,18},{4,20},{6,22},{8,24},{10,26},{12,28},{14,30},{16,0},... | collective-permute-start | bytes 1769480 | tf_op jit(solution)/shard_map/ppermute | solution.py:637
  52.4 1.7 %collective-permute-start.4 = (bf16[2,576,256]{2,1,0:T(8,128)(2,1)S(1)}, bf16[2,576,256]{2,1,0:T(8,128)(2,1)S(1)}, u32[]{:S(2)}, u32[]{:S(2)}) collective-permute-start(bf16[2,576,256]{2,1,0:T(8,128)(2,1)S(1)} %copy-done.11), channel_id=1, source_target_pairs={{0,20},{2,22},{4,16},{6,18},{8,28},{10,30},{12,24},{14,26},{16,4},... | collective-permute-start | bytes 1769480 | tf_op jit(solution)/shard_map/ppermute | solution.py:637
  54.1 20.5 %value_gradients.1 = (bf16[8,256,384]{2,1,0:T(8,128)(2,1)S(1)}, f32[8,256,128]{2,1,0:T(8,128)S(1)}, bf16[8,256,128]{2,1,0:T(8,128)(2,1)S(1)}, bf16[8,256,128]{2,1,0:T(8,128)(2,1)S(1)}) custom-call(s32[1]{0:T(128)} %bitcast.1.parity_ref, bf16[8,256,768]{2,1,0:T(8,128)(2,1)S(1)} %all-to-all-done.own_ref.own_kv_ref, ...), custom_call_target="tpu_custom_call" | custom-call | flops 7516192768 | bytes 8388608 | tf_op jit(solution)/shard_map/value_gradients/pallas_call | solution.py:272
  74.7 1.9 %collective-permute-done.1 = bf16[8,256,128]{2,1,0:T(8,128)(2,1)S(1)} collective-permute-done((bf16[8,256,128]{2,1,0:T(8,128)(2,1)S(1)}, bf16[8,256,128]{2,1,0:T(8,128)(2,1)S(1)}, u32[]{:S(2)}, u32[]{:S(2)}) %collective-permute-start.1) | collective-permute-done | bytes 524320 | tf_op jit(solution)/shard_map/ppermute | solution.py:637
  80.0 5.4 %all-to-all-start.1 = ((bf16[8,4,256,128]{3,2,1,0:T(8,128)(2,1)}), bf16[8,4,256,128]{3,2,1,0:T(8,128)(2,1)S(1)}, u32[]{:S(2)}, u32[]{:S(2)}) async-start(bf16[8,4,256,128]{3,2,1,0:T(8,128)(2,1)} %bitcast.12), calls=%async_computation.1 | async-start | bytes 4194304 | tf_op jit(solution)/shard_map/all_to_all | solution.py:634
  85.5 18.7 %score_gradients.1 = (bf16[8,256,384]{2,1,0:T(8,128)(2,1)}, bf16[8,256,128]{2,1,0:T(8,128)(2,1)}, bf16[8,256,128]{2,1,0:T(8,128)(2,1)}) custom-call(s32[1]{0:T(128)} %bitcast.1.parity_ref, bf16[8,256,768]{2,1,0:T(8,128)(2,1)} %copy-done.1, bf16[8,256,768]{2,1,0:T(8,128)(2,1)} %copy-done.1, ...), custom_call_target="tpu_custom_call", output_to_operand_aliasing={{0}: (4, {})} | custom-call | flops 15032385536 | bytes 8388608 | tf_op jit(solution)/shard_map/score_gradients/pallas_call | solution.py:272
  104.2 2.1 %collective-permute-done.5.theirs_ref = bf16[8,256,128]{2,1,0:T(8,128)(2,1)S(1)} collective-permute-done((bf16[8,256,128]{2,1,0:T(8,128)(2,1)}, bf16[8,256,128]{2,1,0:T(8,128)(2,1)S(1)}, u32[]{:S(2)}, u32[]{:S(2)}) %collective-permute-start.5) | collective-permute-done | bytes 524320 | tf_op jit(solution)/shard_map/ppermute | solution.py:637
  107.1 2.0 %pack_scores.1 = bf16[8,256,384]{2,1,0:T(8,128)(2,1)} custom-call(bf16[8,256,384]{2,1,0:T(8,128)(2,1)} %get-tuple-element.60._, bf16[8,256,128]{2,1,0:T(8,128)(2,1)} %get-tuple-element.61.mine_ref, bf16[8,256,128]{2,1,0:T(8,128)(2,1)} %copy-done.18), custom_call_target="tpu_custom_call", output_to_operand_aliasing={{}: (0, {})} | custom-call | bytes 4194304 | tf_op jit(solution)/shard_map/pack_scores/pallas_call | solution.py:369
  109.1 2.4 %all-to-all-done.1.refs_4_ = bf16[8,4,256,128]{3,2,1,0:T(8,128)(2,1)S(1)} async-done(((bf16[8,4,256,128]{3,2,1,0:T(8,128)(2,1)}), bf16[8,4,256,128]{3,2,1,0:T(8,128)(2,1)S(1)}, u32[]{:S(2)}, u32[]{:S(2)}) %all-to-all-start.1) | async-done | bytes 2097184 | tf_op jit(solution)/shard_map/all_to_all | solution.py:634
  112.8 4.8 %all-to-all-start.2 = ((bf16[8,256,384]{2,1,0:T(8,128)(2,1)}), bf16[8,256,384]{2,1,0:T(8,128)(2,1)S(1)}, u32[]{:S(2)}, u32[]{:S(2)}) async-start(bf16[8,256,384]{2,1,0:T(8,128)(2,1)} %pack_scores.1), calls=%async_computation.2 | async-start | bytes 3145728 | tf_op jit(solution)/shard_map/all_to_all | solution.py:634
  117.6 6.4 %input_product.1 = (bf16[2,288,1024]{2,1,0:T(8,128)(2,1)}, bf16[2,288,1024]{2,1,0:T(8,128)(2,1)}, bf16[256,1024]{1,0:T(8,128)(2,1)}) custom-call(s32[5]{0:T(128)} %copy-done.6, bf16[2,576,256]{2,1,0:T(8,128)(2,1)} %copy-done.9, bf16[2,576,256]{2,1,0:T(8,128)(2,1)} %copy-done.19, bf16[2,576,256]{2,1,0:T(8,128)(2,1)} %copy-done.20, ...), custom_call_target="tpu_custom_call" | custom-call | flops 2415919104 | bytes 7340052 | tf_op jit(solution)/shard_map/input_product/pallas_call | solution.py:369
  124.0 3.0 %collective-permute-done.6 = bf16[2,288,1024]{2,1,0:T(8,128)(2,1)S(1)} collective-permute-done((bf16[2,288,1024]{2,1,0:T(8,128)(2,1)}, bf16[2,288,1024]{2,1,0:T(8,128)(2,1)S(1)}, u32[]{:S(2)}, u32[]{:S(2)}) %collective-permute-start.6) | collective-permute-done | bytes 1179680 | tf_op jit(solution)/shard_map/ppermute | solution.py:637
  129.9 7.9 %collective-permute-start.7 = (bf16[144,1024]{1,0:T(8,128)(2,1)}, bf16[144,1024]{1,0:T(8,128)(2,1)S(1)}, u32[]{:S(2)}, u32[]{:S(2)}) collective-permute-start(bf16[144,1024]{1,0:T(8,128)(2,1)} %get-tuple-element.74), channel_id=1, source_target_pairs={{1,104},{3,106},{5,108},{7,110},{9,96},{11,98},{13,100},{15,102},{... | collective-permute-start | bytes 884744 | tf_op jit(solution)/shard_map/ppermute | solution.py:672
  138.7 10.4 %collective-permute-start.8 = (bf16[144,1024]{1,0:T(8,128)(2,1)S(1)}, bf16[144,1024]{1,0:T(8,128)(2,1)S(1)}, u32[]{:S(2)}, u32[]{:S(2)}) collective-permute-start(bf16[144,1024]{1,0:T(8,128)(2,1)S(1)} %get-tuple-element.75), channel_id=1, source_target_pairs={{1,96},{3,98},{5,100},{7,102},{9,104},{11,106},{13,108},{15,110},{... | collective-permute-start | bytes 884744 | tf_op jit(solution)/shard_map/ppermute | solution.py:672
  149.1 1.9 %collective-permute-start.9 = (bf16[144,1024]{1,0:T(8,128)(2,1)S(1)}, bf16[144,1024]{1,0:T(8,128)(2,1)S(1)}, u32[]{:S(2)}, u32[]{:S(2)}) collective-permute-start(bf16[144,1024]{1,0:T(8,128)(2,1)S(1)} %get-tuple-element.76), channel_id=1, source_target_pairs={{1,97},{3,99},{5,101},{7,103},{9,105},{11,107},{13,109},{15,111},{... | collective-permute-start | bytes 884744 | tf_op jit(solution)/shard_map/ppermute | solution.py:672
  151.0 1.9 %unpack_scores.1 = (bf16[256,2048]{1,0:T(8,128)(2,1)}, bf16[256,1024]{1,0:T(8,128)(2,1)}) custom-call(bf16[8,256,384]{2,1,0:T(8,128)(2,1)S(1)} %all-to-all-done.2.in_ref), custom_call_target="tpu_custom_call" | custom-call | bytes 3145728 | tf_op jit(solution)/shard_map/unpack_scores/pallas_call | solution.py:369
  152.9 2.7 %collective-permute-done.10.other_ref = bf16[144,1024]{1,0:T(8,128)(2,1)S(1)} collective-permute-done((bf16[144,1024]{1,0:T(8,128)(2,1)S(1)}, bf16[144,1024]{1,0:T(8,128)(2,1)S(1)}, u32[]{:S(2)}, u32[]{:S(2)}) %collective-permute-start.10) | collective-permute-done | bytes 294944 | tf_op jit(solution)/shard_map/ppermute | solution.py:672
  155.6 5.9 %collective-permute-done.9.far_ref = bf16[144,1024]{1,0:T(8,128)(2,1)S(1)} collective-permute-done((bf16[144,1024]{1,0:T(8,128)(2,1)S(1)}, bf16[144,1024]{1,0:T(8,128)(2,1)S(1)}, u32[]{:S(2)}, u32[]{:S(2)}) %collective-permute-start.9) | collective-permute-done | bytes 294944 | tf_op jit(solution)/shard_map/ppermute | solution.py:672
  161.5 1.6 copy-done.3
  163.1 1.9 %finish.1 = f32[144,1024]{1,0:T(8,128)} custom-call(s32[5]{0:T(128)S(1)} %copy-done.7, s32[4,1024]{1,0:T(4,128)S(1)} %copy-done.5, bf16[1024,1024]{1,0:T(8,128)(2,1)S(1)} %copy-done.3, bf16[144,1024]{1,0:T(8,128)(2,1)S(1)} %get-tuple-element.73.own_ref, bf16[144,1024]{1,0:T(8,128)(2,1)S(1)} %collective-permute-done.7.near_ref, ...), custom_call_target="tpu_custom_call" | custom-call | flops 301989888 | bytes 3883028 | tf_op jit(solution)/shard_map/finish/pallas_call | solution.py:369
  (60 shorter events, 17.1 us)
Async XLA Ops:
  3.8 43.7 %all-to-all-start = ((bf16[8,256,768]{2,1,0:T(8,128)(2,1)}), bf16[8,256,768]{2,1,0:T(8,128)(2,1)S(1)}, u32[]{:S(2)}, u32[]{:S(2)}) async-start(bf16[8,256,768]{2,1,0:T(8,128)(2,1)} %pack_heads.1), calls=%async_computation | async-start | bytes 6291456 | tf_op jit(solution)/shard_map/all_to_all | solution.py:634
  9.9 37.7 %copy-start.6 = (s32[5]{0:T(128)}, s32[5]{0:T(128)S(1)}, u32[]{:S(2)}) copy-start(s32[5]{0:T(128)S(1)} %stack.23.place_ref) | copy-start | bytes 64
  9.9 1.7 %copy-start.2 = (bf16[1,1,256,4608]{3,2,1,0:T(8,128)(2,1)S(1)}, bf16[1,1,256,4608]{3,2,1,0:T(8,128)(2,1)}, u32[]{:S(2)}) copy-start(bf16[1,1,256,4608]{3,2,1,0:T(8,128)(2,1)} %param.11) | copy-start | bytes 7077892
  47.5 27.1 %copy-start.1 = (bf16[8,256,768]{2,1,0:T(8,128)(2,1)}, bf16[8,256,768]{2,1,0:T(8,128)(2,1)S(1)}, u32[]{:S(2)}) copy-start(bf16[8,256,768]{2,1,0:T(8,128)(2,1)S(1)} %all-to-all-done.own_ref.own_kv_ref) | copy-start | bytes 9437188
  47.5 3.0 %copy-start.13 = (bf16[2,576,256]{2,1,0:T(8,128)(2,1)S(1)}, bf16[2,576,256]{2,1,0:T(8,128)(2,1)}, u32[]{:S(2)}) copy-start(bf16[2,576,256]{2,1,0:T(8,128)(2,1)} %copy-done.12) | copy-start | bytes 1769476
  47.5 4.9 %copy-start.11 = (bf16[2,576,256]{2,1,0:T(8,128)(2,1)S(1)}, bf16[2,576,256]{2,1,0:T(8,128)(2,1)}, u32[]{:S(2)}) copy-start(bf16[2,576,256]{2,1,0:T(8,128)(2,1)} %copy-done.10) | copy-start | bytes 1769476
  47.6 6.5 %collective-permute-start = (bf16[8,256,256]{2,1,0:T(8,128)(2,1)S(1)}, bf16[8,256,256]{2,1,0:T(8,128)(2,1)S(1)}, u32[]{:S(2)}, u32[]{:S(2)}) collective-permute-start(bf16[8,256,256]{2,1,0:T(8,128)(2,1)S(1)} %slice.3), channel_id=1, source_target_pairs={{0,2},{2,0},{4,6},{6,4},{8,10},{10,8},{12,14},{14,12},{16,18},{18,... | collective-permute-start | bytes 3145736 | tf_op jit(solution)/shard_map/ppermute | solution.py:637
  49.0 29.1 %collective-permute-start.2 = (bf16[2,576,256]{2,1,0:T(8,128)(2,1)S(1)}, bf16[2,576,256]{2,1,0:T(8,128)(2,1)S(1)}, u32[]{:S(2)}, u32[]{:S(2)}) collective-permute-start(bf16[2,576,256]{2,1,0:T(8,128)(2,1)S(1)} %copy-done.15), channel_id=1, source_target_pairs={{0,4},{2,6},{4,0},{6,2},{8,12},{10,14},{12,8},{14,10},{16,20},{18,... | collective-permute-start | bytes 1769480 | tf_op jit(solution)/shard_map/ppermute | solution.py:637
  50.5 27.6 %collective-permute-start.3 = (bf16[2,576,256]{2,1,0:T(8,128)(2,1)S(1)}, bf16[2,576,256]{2,1,0:T(8,128)(2,1)S(1)}, u32[]{:S(2)}, u32[]{:S(2)}) collective-permute-start(bf16[2,576,256]{2,1,0:T(8,128)(2,1)S(1)} %copy-done.13), channel_id=1, source_target_pairs={{0,16},{2,18},{4,20},{6,22},{8,24},{10,26},{12,28},{14,30},{16,0},... | collective-permute-start | bytes 1769480 | tf_op jit(solution)/shard_map/ppermute | solution.py:637
  52.4 26.4 %collective-permute-start.4 = (bf16[2,576,256]{2,1,0:T(8,128)(2,1)S(1)}, bf16[2,576,256]{2,1,0:T(8,128)(2,1)S(1)}, u32[]{:S(2)}, u32[]{:S(2)}) collective-permute-start(bf16[2,576,256]{2,1,0:T(8,128)(2,1)S(1)} %copy-done.11), channel_id=1, source_target_pairs={{0,20},{2,22},{4,16},{6,18},{8,28},{10,30},{12,24},{14,26},{16,4},... | collective-permute-start | bytes 1769480 | tf_op jit(solution)/shard_map/ppermute | solution.py:637
  54.1 20.5 %copy-start.8 = (bf16[8,256,256]{2,1,0:T(8,128)(2,1)}, bf16[8,256,256]{2,1,0:T(8,128)(2,1)S(1)}, u32[]{:S(2)}) copy-start(bf16[8,256,256]{2,1,0:T(8,128)(2,1)S(1)} %collective-permute-done.other_ref) | copy-start | bytes 3145732
  74.6 3.5 %copy-start = (bf16[8,256,384]{2,1,0:T(8,128)(2,1)}, bf16[8,256,384]{2,1,0:T(8,128)(2,1)S(1)}, u32[]{:S(2)}) copy-start(bf16[8,256,384]{2,1,0:T(8,128)(2,1)S(1)} %get-tuple-element.58._) | copy-start | bytes 4718596
  74.6 3.5 %copy-start.16 = (f32[8,256,128]{2,1,0:T(8,128)}, f32[8,256,128]{2,1,0:T(8,128)S(1)}, u32[]{:S(2)}) copy-start(f32[8,256,128]{2,1,0:T(8,128)S(1)} %get-tuple-element.59.dk_ref) | copy-start | bytes 3145732
  74.6 2.0 %collective-permute-start.1 = (bf16[8,256,128]{2,1,0:T(8,128)(2,1)S(1)}, bf16[8,256,128]{2,1,0:T(8,128)(2,1)S(1)}, u32[]{:S(2)}, u32[]{:S(2)}) collective-permute-start(bf16[8,256,128]{2,1,0:T(8,128)(2,1)S(1)} %get-tuple-element.47), channel_id=1, source_target_pairs={{0,2},{2,0},{4,6},{6,4},{8,10},{10,8},{12,14},{14,12},{16,18},{18,... | collective-permute-start | bytes 1572872 | tf_op jit(solution)/shard_map/ppermute | solution.py:637
  80.0 31.4 %all-to-all-start.1 = ((bf16[8,4,256,128]{3,2,1,0:T(8,128)(2,1)}), bf16[8,4,256,128]{3,2,1,0:T(8,128)(2,1)S(1)}, u32[]{:S(2)}, u32[]{:S(2)}) async-start(bf16[8,4,256,128]{3,2,1,0:T(8,128)(2,1)} %bitcast.12), calls=%async_computation.1 | async-start | bytes 4194304 | tf_op jit(solution)/shard_map/all_to_all | solution.py:634
  104.2 2.1 %collective-permute-start.5 = (bf16[8,256,128]{2,1,0:T(8,128)(2,1)}, bf16[8,256,128]{2,1,0:T(8,128)(2,1)S(1)}, u32[]{:S(2)}, u32[]{:S(2)}) collective-permute-start(bf16[8,256,128]{2,1,0:T(8,128)(2,1)} %get-tuple-element.62), channel_id=1, source_target_pairs={{0,2},{2,0},{4,6},{6,4},{8,10},{10,8},{12,14},{14,12},{16,18},{18,... | collective-permute-start | bytes 1572872 | tf_op jit(solution)/shard_map/ppermute | solution.py:637
  112.8 25.9 %all-to-all-start.2 = ((bf16[8,256,384]{2,1,0:T(8,128)(2,1)}), bf16[8,256,384]{2,1,0:T(8,128)(2,1)S(1)}, u32[]{:S(2)}, u32[]{:S(2)}) async-start(bf16[8,256,384]{2,1,0:T(8,128)(2,1)} %pack_scores.1), calls=%async_computation.2 | async-start | bytes 3145728 | tf_op jit(solution)/shard_map/all_to_all | solution.py:634
  117.6 9.5 %copy-start.7 = (s32[5]{0:T(128)S(1)}, s32[5]{0:T(128)}, u32[]{:S(2)}) copy-start(s32[5]{0:T(128)} %copy-done.6) | copy-start | bytes 64
  124.0 3.1 %collective-permute-start.6 = (bf16[2,288,1024]{2,1,0:T(8,128)(2,1)}, bf16[2,288,1024]{2,1,0:T(8,128)(2,1)S(1)}, u32[]{:S(2)}, u32[]{:S(2)}) collective-permute-start(bf16[2,288,1024]{2,1,0:T(8,128)(2,1)} %get-tuple-element.65), channel_id=1, source_target_pairs={{0,2},{2,0},{4,6},{6,4},{8,10},{10,8},{12,14},{14,12},{16,18},{18,... | collective-permute-start | bytes 3538952 | tf_op jit(solution)/shard_map/ppermute | solution.py:637
  128.4 33.2 %copy-start.5 = (s32[4,1024]{1,0:T(4,128)S(1)}, s32[4,1024]{1,0:T(4,128)}, u32[]{:S(2)}) copy-start(s32[4,1024]{1,0:T(4,128)} %signs_ref.1) | copy-start | bytes 49156
  129.9 23.0 %collective-permute-start.7 = (bf16[144,1024]{1,0:T(8,128)(2,1)}, bf16[144,1024]{1,0:T(8,128)(2,1)S(1)}, u32[]{:S(2)}, u32[]{:S(2)}) collective-permute-start(bf16[144,1024]{1,0:T(8,128)(2,1)} %get-tuple-element.74), channel_id=1, source_target_pairs={{1,104},{3,106},{5,108},{7,110},{9,96},{11,98},{13,100},{15,102},{... | collective-permute-start | bytes 884744 | tf_op jit(solution)/shard_map/ppermute | solution.py:672
  137.7 17.8 %collective-permute-start.10 = (bf16[144,1024]{1,0:T(8,128)(2,1)S(1)}, bf16[144,1024]{1,0:T(8,128)(2,1)S(1)}, u32[]{:S(2)}, u32[]{:S(2)}) collective-permute-start(bf16[144,1024]{1,0:T(8,128)(2,1)S(1)} %get-tuple-element.77), channel_id=1, source_target_pairs={{1,105},{3,107},{5,109},{7,111},{9,97},{11,99},{13,101},{15,103},{... | collective-permute-start | bytes 884744 | tf_op jit(solution)/shard_map/ppermute | solution.py:672
  138.7 16.9 %collective-permute-start.8 = (bf16[144,1024]{1,0:T(8,128)(2,1)S(1)}, bf16[144,1024]{1,0:T(8,128)(2,1)S(1)}, u32[]{:S(2)}, u32[]{:S(2)}) collective-permute-start(bf16[144,1024]{1,0:T(8,128)(2,1)S(1)} %get-tuple-element.75), channel_id=1, source_target_pairs={{1,96},{3,98},{5,100},{7,102},{9,104},{11,106},{13,108},{15,110},{... | collective-permute-start | bytes 884744 | tf_op jit(solution)/shard_map/ppermute | solution.py:672
  149.1 12.5 %collective-permute-start.9 = (bf16[144,1024]{1,0:T(8,128)(2,1)S(1)}, bf16[144,1024]{1,0:T(8,128)(2,1)S(1)}, u32[]{:S(2)}, u32[]{:S(2)}) collective-permute-start(bf16[144,1024]{1,0:T(8,128)(2,1)S(1)} %get-tuple-element.76), channel_id=1, source_target_pairs={{1,97},{3,99},{5,101},{7,103},{9,105},{11,107},{13,109},{15,111},{... | collective-permute-start | bytes 884744 | tf_op jit(solution)/shard_map/ppermute | solution.py:672
  (12 other events, 12.5 us)

commit v4 on v3

--- a/solution.py
+++ b/solution.py
@@ -360,12 +360,14 @@
     kind=jnp.bfloat16,
     vmem=16,
     aliases=None,
+    moved=None,
 ):
     kinds = [jax.ShapeDtypeStruct(shape, kind) for shape in out_shape]
     specs = {}
     if grid is not None:
         specs = {"grid": grid}
-    moved = sum(x.size * x.dtype.itemsize for x in operands) + sum(2 * math.prod(s) for s in out_shape)
+    if moved is None:
+        moved = sum(2 * x.size for x in operands) + sum(2 * math.prod(s) for s in out_shape)
     return pl.pallas_call(
         kernel,
         out_shape=kinds,
@@ -462,9 +464,9 @@
     def kernel(mine_ref, theirs_ref, out_ref):
         for x in range(2):
             for y in range(2):
-                total = add(mine_ref[x, 0, y], theirs_ref[x, 0, y])
+                total = add(mine_ref[x, y, 0], theirs_ref[x, y, 0])
                 for to in range(4):
-                    out_ref[to // 2, 0, to % 2, 2 * x + y] = total
+                    out_ref[to // 2, to % 2, 0, 2 * x + y] = total
 
     chips, rows, head = mine.shape
     split = (2, 2, 2, rows, head)
@@ -477,8 +479,8 @@
         mine.reshape(split),
         theirs.reshape(split),
         grid=(2,),
-        in_specs=[pl.BlockSpec((2, 1, 2, rows, head), lambda p: (0, p, 0, 0, 0))] * 2,
-        out_specs=[pl.BlockSpec((2, 1, 2, 4, rows, head), lambda p: (0, p, 0, 0, 0, 0))],
+        in_specs=[pl.BlockSpec((2, 2, 1, rows, head), lambda p: (0, 0, p, 0, 0))] * 2,
+        out_specs=[pl.BlockSpec((2, 2, 1, 4, rows, head), lambda p: (0, 0, p, 0, 0, 0))],
         vmem=16,
     )
     return packed.reshape(chips, 4, rows, head)
@@ -495,11 +497,13 @@
             turned_s[at : at + wide] = jnp.transpose(in_ref[:, at : at + wide])
         for distance, out_ref in enumerate(out_refs):
             to = place_ref[0] ^ distance
-            for high in range(2):
-                for core in range(2):
-                    index = ((to // 2 * 2 + high) * 2 + to % 2) * 2 + core
+            for core in range(2):
+                for group in range(2):
+                    high = to % 2 if group else to % 2 ^ core
+                    low = place_ref[2] if group else 1 - place_ref[2]
+                    index = ((to // 2 * 2 + high) * 2 + low) * 2 + core
                     piece = turned_s[pl.ds(pl.multiple_of(index * share, 16), share)]
-                    out_ref[high, core * share : (core + 1) * share] = piece
+                    out_ref[group, core * share : (core + 1) * share] = piece
 
     return small_call(
         kernel,
@@ -521,17 +525,17 @@
     def kernel(place_ref, *refs):
         column_refs, back_ref = refs[:members], refs[members]
         give_ref, keep_ref, value_ref = refs[members + 1 :]
-        member, core, high = place_ref[0], place_ref[1], place_ref[2]
+        member, core = place_ref[0], place_ref[1]
         v = [
             jnp.concatenate([back_ref[0, member ^ d], back_ref[1, member ^ d]], axis=1)
             for d in range(members)
         ]
         value_ref[...] = v[0]
         v = jnp.concatenate(v, axis=0)
-        for at, which_high in enumerate((1 - high, high)):
+        for at in range(2):
             for out_ref, which_core in ((give_ref, 1 - core), (keep_ref, core)):
                 part = pl.ds(pl.multiple_of(which_core * share, 16), share)
-                x = jnp.concatenate([ref[which_high, part] for ref in column_refs], axis=1)
+                x = jnp.concatenate([ref[at, part] for ref in column_refs], axis=1)
                 out_ref[at] = dot(x, v, (1, 0)).astype(jnp.bfloat16)
 
     once = pl.Buffered(1)
@@ -541,7 +545,7 @@
         "input_product",
         [(2, share, heads * head)] * 2 + [(rows, heads * head)],
         [],
-        8 * share * members * rows * heads * head,
+        0,
         place,
         *columns,
         back,
@@ -551,6 +555,7 @@
         + [pl.BlockSpec((2, members, rows, head), lambda g: (g, 0, 0, 0))],
         out_specs=[halves, halves, pl.BlockSpec((rows, 2 * head), lambda g: (0, g))],
         vmem=60,
+        moved=0,
     )
 
 
@@ -584,12 +589,11 @@
     )
 
 
-def finish(place, signs, turn, pieces):
-    def kernel(place_ref, signs_ref, turn_ref, own_ref, near_ref, near2_ref, far_ref, other_ref, out_ref):
+def finish(place, turn, pieces):
+    def kernel(place_ref, turn_ref, own_ref, near_ref, near2_ref, far_ref, other_ref, out_ref):
         total = jnp.where(place_ref[3] == 0, own_ref[...], far_ref[...]).astype(jnp.float32)
         total = total + add32(near_ref[...], near2_ref[...]) + other_ref[...].astype(jnp.float32)
-        signs = signs_ref[pl.ds(place_ref[4], 1)].astype(jnp.float32)
-        out_ref[...] = dot((total * signs).astype(jnp.bfloat16), turn_ref[...], (1, 0))
+        out_ref[...] = dot(total.astype(jnp.bfloat16), turn_ref[...], (1, 0))
 
     own = pieces[0]
     (out,) = small_call(
@@ -599,10 +603,9 @@
         [],
         2 * own.size * own.shape[1],
         place,
-        signs,
         turn,
         *pieces,
-        in_specs=[SCALAR] + [WHOLE] * 7,
+        in_specs=[SCALAR] + [WHOLE] * 6,
         kind=jnp.float32,
     )
     return out
@@ -627,8 +630,8 @@
     mirror = lax.axis_index("mirror").astype(jnp.int32)
     core = ctx & 1
     same_core = [[2 * chip + c for chip in range(chips)] for c in range(2)]
-    member = (ctx >> 3) * 2 + (ctx >> 1 & 1)
-    place = jnp.stack([member, core, ctx >> 2 & 1, mirror, section])
+    member = (ctx >> 3) * 2 + (ctx >> 2 & 1)
+    place = jnp.stack([member, core, ctx >> 1 & 1, mirror])
 
     def across(block):
         return lax.all_to_all(block, "ctx", 0, 0, tiled=True, axis_index_groups=same_core)
@@ -643,7 +646,7 @@
     own, *turned = lax.optimization_barrier((own, *turned))
     other = swap(own[:, :, 4 * head :], 1)
     parity = core.reshape(1)
-    columns = turned[:1] + [swap(turned[d], (d & 1) * 2 + (d >> 1) * 8) for d in range(1, 4)]
+    columns = turned[:1] + [swap(turned[d], (d & 1) * 4 + (d >> 1) * 8) for d in range(1, 4)]
 
     scores, dk, dv_mine, dv_theirs = value_gradients(parity, own, other)
     values = pack_values(dv_mine, swap(dv_theirs, 1))
@@ -662,10 +665,10 @@
     sections = lax.axis_size("section")
     cross_other, cross_own, stay_other, second_own, first_own = cut_pieces(place, keep, got)
 
-    def routed(block, route, group):
+    def routed(block, route, groups):
         axes = ("section", "ctx", "mirror")
         pairs = [
-            ((s * 2 * chips + i) * 2 + m, (t * 2 * chips + (i ^ group)) * 2 + n)
+            ((s * 2 * chips + i) * 2 + m, (t * 2 * chips + (i ^ groups[i % 2])) * 2 + n)
             for (s, m), (t, n) in route
             for i in range(2 * chips)
         ]
@@ -674,15 +677,16 @@
     far = [((s, 1), (sections - 1 - s, 1)) for s in range(sections)]
     cross = [((s, 1), (sections - 1 - s, 0)) for s in range(sections)]
     cross += [((s, 0), (s, 1)) for s in range(sections)]
-    near_other = routed(cross_other, cross, 4)
-    other = routed(stay_other, far + [((s, 0), (s, 0)) for s in range(sections)], 4)
+    near_other = routed(cross_other, cross, (2, 6))
+    other = routed(stay_other, far + [((s, 0), (s, 0)) for s in range(sections)], (2, 6))
     cross_own, second_own, scores_back = lax.optimization_barrier((cross_own, second_own, scores_back))
-    near_own = routed(cross_own, cross, 0)
-    far_own = routed(second_own, far, 0)
+    near_own = routed(cross_own, cross, (0, 0))
+    far_own = routed(second_own, far, (0, 0))
+    signs = lax.dynamic_index_in_dim(hadamard_signs, section, 0, keepdims=False)
+    turn = jnp.asarray(hadamard(width), jnp.bfloat16) * signs.astype(jnp.bfloat16)[:, None]
     rotated = finish(
         place,
-        hadamard_signs,
-        jnp.asarray(hadamard(width), jnp.bfloat16),
+        turn,
         (first_own, near_other, near_own, far_own, other),
     )
     query_gradient, key_gradient = unpack_scores(scores_back)

time: 166 us -> 161 us (0.970)
  starting transfers between devices: 41.7 us -> 37 us
  waiting for transfers between devices: 51.1 us -> 47.7 us
  other arithmetic: 0 us -> 2.62 us
    ppermute x4, starting transfers between devices: 20.1 us -> 14.9 us  [routed(): return lax.ppermute(block, axes, pairs)]
    ppermute x4, waiting for transfers between devices: 8.68 us -> 5.3 us  [routed(): return lax.ppermute(block, axes, pairs)]
    mul x0 -> x1, other arithmetic: none -> 1.8 us  [body(): jnp.asarray(hadamard(width), jnp.bfloat16)]
    unnamed x44 -> x42, local copies, waits for them, and re-layouts: 12.5 us -> 13.4 us
  transfers between devices with their start and end apart: 14 -> 14, of which waited for: 9 -> 8; matrix products, arithmetic and copies ran while one was open for 0% -> 2% of each run, Pallas kernels for 33% -> 34%
where the time goes in v4:
time: 161 us
  Pallas kernels  58.9 us (37%)
  waiting for transfers between devices  47.7 us (30%)
  starting transfers between devices  37 us (23%)
  local copies, waits for them, and re-layouts  13.5 us (8%)
  other arithmetic  2.62 us (2%)
    pallas_call x2, Pallas kernels, attention_call(): pl.pallas_call(kernel, grid=(chips - first,), out_shape=[payload] + [shap...  39.2 us
    all_to_all x3, waiting for transfers between devices, across(): lax.all_to_all(block, 'ctx', 0, 0, tiled=True, axis_index_groups=same_core)  36.1 us
    pallas_call x8, Pallas kernels, small_call(): pl.pallas_call(kernel, out_shape=kinds, in_specs=in_specs if in_specs is...  19.7 us
    all_to_all x3, starting transfers between devices, across(): lax.all_to_all(block, 'ctx', 0, 0, tiled=True, axis_index_groups=same_core)  15.5 us
    ppermute x4, starting transfers between devices, routed(): return lax.ppermute(block, axes, pairs)  14.9 us
    unnamed x42, local copies, waits for them, and re-layouts  13.4 us
    ppermute x7, starting transfers between devices, swap(): return lax.ppermute(block, 'ctx', [(i, i ^ bits) for i in range(2 * chips)])  6.66 us
    ppermute x7, waiting for transfers between devices, swap(): return lax.ppermute(block, 'ctx', [(i, i ^ bits) for i in range(2 * chips)])  6.33 us
  transfers between devices with their start and end apart: 14, of which 8 were waited for; matrix products, arithmetic and copies ran while one was open for 2% of the time, Pallas kernels for 34%

profile of v4, /device:TPU:2, one launch (start us, length us, event | category | flops | bytes accessed | tf_op | source)
XLA Modules:
  0.0 160.5 jit_solution(13095044375275815998)
XLA Ops:
  0.6 3.2 %pack_heads.1 = bf16[8,256,768]{2,1,0:T(8,128)(2,1)} custom-call(bf16[256,2048]{1,0:T(8,128)(2,1)} %bitcast.23, bf16[256,2048]{1,0:T(8,128)(2,1)} %bitcast.24, bf16[256,1024]{1,0:T(8,128)(2,1)} %bitcast.26, bf16[256,1024]{1,0:T(8,128)(2,1)} %bitcast.27), custom_call_target="tpu_custom_call" | custom-call | bytes 6291456 | tf_op jit(solution)/shard_map/pack_heads/pallas_call | solution.py:371
  3.8 6.0 %all-to-all-start = ((bf16[8,256,768]{2,1,0:T(8,128)(2,1)}), bf16[8,256,768]{2,1,0:T(8,128)(2,1)S(1)}, u32[]{:S(2)}, u32[]{:S(2)}) async-start(bf16[8,256,768]{2,1,0:T(8,128)(2,1)} %pack_heads.1), calls=%async_computation | async-start | bytes 6291456 | tf_op jit(solution)/shard_map/all_to_all | solution.py:637
  9.9 1.7 %copy-done.2 = bf16[1,1,256,4608]{3,2,1,0:T(8,128)(2,1)S(1)} copy-done((bf16[1,1,256,4608]{3,2,1,0:T(8,128)(2,1)S(1)}, bf16[1,1,256,4608]{3,2,1,0:T(8,128)(2,1)}, u32[]{:S(2)}) %copy-start.2) | copy-done | bytes 2359320
  16.2 31.3 %all-to-all-done.own_ref.own_kv_ref = bf16[8,256,768]{2,1,0:T(8,128)(2,1)S(1)} async-done(((bf16[8,256,768]{2,1,0:T(8,128)(2,1)}), bf16[8,256,768]{2,1,0:T(8,128)(2,1)S(1)}, u32[]{:S(2)}, u32[]{:S(2)}) %all-to-all-start) | async-done | bytes 3145760 | tf_op jit(solution)/shard_map/all_to_all | solution.py:637
  48.9 3.0 %collective-permute-start.2 = (bf16[2,576,256]{2,1,0:T(8,128)(2,1)S(1)}, bf16[2,576,256]{2,1,0:T(8,128)(2,1)S(1)}, u32[]{:S(2)}, u32[]{:S(2)}) collective-permute-start(bf16[2,576,256]{2,1,0:T(8,128)(2,1)S(1)} %copy-done.13), channel_id=1, source_target_pairs={{0,8},{2,10},{4,12},{6,14},{8,0},{10,2},{12,4},{14,6},{16,24},{18,... | collective-permute-start | bytes 1769480 | tf_op jit(solution)/shard_map/ppermute | solution.py:640
  52.5 3.0 %collective-permute-start.4 = (bf16[2,576,256]{2,1,0:T(8,128)(2,1)S(1)}, bf16[2,576,256]{2,1,0:T(8,128)(2,1)S(1)}, u32[]{:S(2)}, u32[]{:S(2)}) collective-permute-start(bf16[2,576,256]{2,1,0:T(8,128)(2,1)S(1)} %copy-done.9), channel_id=1, source_target_pairs={{0,24},{2,26},{4,28},{6,30},{8,16},{10,18},{12,20},{14,22},{16,8},... | collective-permute-start | bytes 1769480 | tf_op jit(solution)/shard_map/ppermute | solution.py:640
  55.5 20.5 %value_gradients.1 = (bf16[8,256,384]{2,1,0:T(8,128)(2,1)S(1)}, f32[8,256,128]{2,1,0:T(8,128)S(1)}, bf16[8,256,128]{2,1,0:T(8,128)(2,1)S(1)}, bf16[8,256,128]{2,1,0:T(8,128)(2,1)S(1)}) custom-call(s32[1]{0:T(128)} %bitcast.1.parity_ref, bf16[8,256,768]{2,1,0:T(8,128)(2,1)S(1)} %all-to-all-done.own_ref.own_kv_ref, ...), custom_call_target="tpu_custom_call" | custom-call | flops 7516192768 | bytes 8388608 | tf_op jit(solution)/shard_map/value_gradients/pallas_call | solution.py:272
  77.2 1.9 %collective-permute-done.1 = bf16[8,256,128]{2,1,0:T(8,128)(2,1)S(1)} collective-permute-done((bf16[8,256,128]{2,1,0:T(8,128)(2,1)S(1)}, bf16[8,256,128]{2,1,0:T(8,128)(2,1)S(1)}, u32[]{:S(2)}, u32[]{:S(2)}) %collective-permute-start.1) | collective-permute-done | bytes 524320 | tf_op jit(solution)/shard_map/ppermute | solution.py:640
  82.5 4.7 %all-to-all-start.1 = ((bf16[8,4,256,128]{3,2,1,0:T(8,128)(2,1)}), bf16[8,4,256,128]{3,2,1,0:T(8,128)(2,1)S(1)}, u32[]{:S(2)}, u32[]{:S(2)}) async-start(bf16[8,4,256,128]{3,2,1,0:T(8,128)(2,1)} %bitcast.11), calls=%async_computation.1 | async-start | bytes 4194304 | tf_op jit(solution)/shard_map/all_to_all | solution.py:637
  87.2 18.7 %score_gradients.1 = (bf16[8,256,384]{2,1,0:T(8,128)(2,1)}, bf16[8,256,128]{2,1,0:T(8,128)(2,1)}, bf16[8,256,128]{2,1,0:T(8,128)(2,1)}) custom-call(s32[1]{0:T(128)} %bitcast.1.parity_ref, bf16[8,256,768]{2,1,0:T(8,128)(2,1)} %copy-done.1, bf16[8,256,768]{2,1,0:T(8,128)(2,1)} %copy-done.1, ...), custom_call_target="tpu_custom_call", output_to_operand_aliasing={{0}: (4, {})} | custom-call | flops 15032385536 | bytes 8388608 | tf_op jit(solution)/shard_map/score_gradients/pallas_call | solution.py:272
  105.9 2.1 %collective-permute-done.5.theirs_ref = bf16[8,256,128]{2,1,0:T(8,128)(2,1)S(1)} collective-permute-done((bf16[8,256,128]{2,1,0:T(8,128)(2,1)}, bf16[8,256,128]{2,1,0:T(8,128)(2,1)S(1)}, u32[]{:S(2)}, u32[]{:S(2)}) %collective-permute-start.5) | collective-permute-done | bytes 524320 | tf_op jit(solution)/shard_map/ppermute | solution.py:640
  108.8 2.0 %pack_scores.1 = bf16[8,256,384]{2,1,0:T(8,128)(2,1)} custom-call(bf16[8,256,384]{2,1,0:T(8,128)(2,1)} %get-tuple-element.60._, bf16[8,256,128]{2,1,0:T(8,128)(2,1)} %get-tuple-element.61.mine_ref, bf16[8,256,128]{2,1,0:T(8,128)(2,1)} %copy-done.20), custom_call_target="tpu_custom_call", output_to_operand_aliasing={{}: (0, {})} | custom-call | bytes 4194304 | tf_op jit(solution)/shard_map/pack_scores/pallas_call | solution.py:371
  110.8 3.1 %all-to-all-done.1.refs_4_ = bf16[8,4,256,128]{3,2,1,0:T(8,128)(2,1)S(1)} async-done(((bf16[8,4,256,128]{3,2,1,0:T(8,128)(2,1)}), bf16[8,4,256,128]{3,2,1,0:T(8,128)(2,1)S(1)}, u32[]{:S(2)}, u32[]{:S(2)}) %all-to-all-start.1) | async-done | bytes 2097184 | tf_op jit(solution)/shard_map/all_to_all | solution.py:637
  115.3 4.8 %all-to-all-start.2 = ((bf16[8,256,384]{2,1,0:T(8,128)(2,1)}), bf16[8,256,384]{2,1,0:T(8,128)(2,1)S(1)}, u32[]{:S(2)}, u32[]{:S(2)}) async-start(bf16[8,256,384]{2,1,0:T(8,128)(2,1)} %pack_scores.1), calls=%async_computation.2 | async-start | bytes 3145728 | tf_op jit(solution)/shard_map/all_to_all | solution.py:637
  120.1 6.4 %input_product.1 = (bf16[2,288,1024]{2,1,0:T(8,128)(2,1)}, bf16[2,288,1024]{2,1,0:T(8,128)(2,1)}, bf16[256,1024]{1,0:T(8,128)(2,1)}) custom-call(s32[4]{0:T(128)} %copy-done.5, bf16[2,576,256]{2,1,0:T(8,128)(2,1)} %copy-done.4, bf16[2,576,256]{2,1,0:T(8,128)(2,1)} %copy-done.17, bf16[2,576,256]{2,1,0:T(8,128)(2,1)} %copy-done.18, ...), custom_call_target="tpu_custom_call" | custom-call | tf_op jit(solution)/shard_map/input_product/pallas_call | solution.py:371
  127.2 2.3 %collective-permute-done.6 = bf16[2,288,1024]{2,1,0:T(8,128)(2,1)S(1)} collective-permute-done((bf16[2,288,1024]{2,1,0:T(8,128)(2,1)}, bf16[2,288,1024]{2,1,0:T(8,128)(2,1)S(1)}, u32[]{:S(2)}, u32[]{:S(2)}) %collective-permute-start.6) | collective-permute-done | bytes 1179680 | tf_op jit(solution)/shard_map/ppermute | solution.py:640
  133.0 6.4 %collective-permute-start.7 = (bf16[144,1024]{1,0:T(8,128)(2,1)}, bf16[144,1024]{1,0:T(8,128)(2,1)S(1)}, u32[]{:S(2)}, u32[]{:S(2)}) collective-permute-start(bf16[144,1024]{1,0:T(8,128)(2,1)} %get-tuple-element.74), channel_id=1, source_target_pairs={{1,100},{3,110},{5,96},{7,106},{9,108},{11,102},{13,104},{15,98},{... | collective-permute-start | bytes 884744 | tf_op jit(solution)/shard_map/ppermute | solution.py:675
  139.3 1.7 %all-to-all-done.2.in_ref = bf16[8,256,384]{2,1,0:T(8,128)(2,1)S(1)} async-done(((bf16[8,256,384]{2,1,0:T(8,128)(2,1)}), bf16[8,256,384]{2,1,0:T(8,128)(2,1)S(1)}, u32[]{:S(2)}, u32[]{:S(2)}) %all-to-all-start.2) | async-done | bytes 1572896 | tf_op jit(solution)/shard_map/all_to_all | solution.py:637
  141.0 6.6 %collective-permute-start.8 = (bf16[144,1024]{1,0:T(8,128)(2,1)}, bf16[144,1024]{1,0:T(8,128)(2,1)S(1)}, u32[]{:S(2)}, u32[]{:S(2)}) collective-permute-start(bf16[144,1024]{1,0:T(8,128)(2,1)} %copy-done.14), channel_id=1, source_target_pairs={{1,96},{3,98},{5,100},{7,102},{9,104},{11,106},{13,108},{15,110},{... | collective-permute-start | bytes 884744 | tf_op jit(solution)/shard_map/ppermute | solution.py:675
  147.6 1.9 %collective-permute-start.9 = (bf16[144,1024]{1,0:T(8,128)(2,1)S(1)}, bf16[144,1024]{1,0:T(8,128)(2,1)S(1)}, u32[]{:S(2)}, u32[]{:S(2)}) collective-permute-start(bf16[144,1024]{1,0:T(8,128)(2,1)S(1)} %get-tuple-element.76), channel_id=1, source_target_pairs={{1,97},{3,99},{5,101},{7,103},{9,105},{11,107},{13,109},{15,111},{... | collective-permute-start | bytes 884744 | tf_op jit(solution)/shard_map/ppermute | solution.py:675
  149.6 1.8 %broadcast_multiply_fusion.turn_ref = bf16[1024,1024]{1,0:T(8,128)(2,1)S(1)} fusion(bf16[1024,1024]{1,0:T(8,128)(2,1)} %constant.28.clone, bf16[1024]{0:T(1024)(128)(2,1)S(1)} %convert_reduce_fusion), kind=kLoop, calls=%fused_computation | loop fusion | flops 1048576 | bytes 4196352 | tf_op jit(solution)/shard_map/mul | solution.py:686
  151.4 1.9 %unpack_scores.1 = (bf16[256,2048]{1,0:T(8,128)(2,1)}, bf16[256,1024]{1,0:T(8,128)(2,1)}) custom-call(bf16[8,256,384]{2,1,0:T(8,128)(2,1)S(1)} %all-to-all-done.2.in_ref), custom_call_target="tpu_custom_call" | custom-call | bytes 3145728 | tf_op jit(solution)/shard_map/unpack_scores/pallas_call | solution.py:371
  153.4 5.1 %collective-permute-done.9.far_ref = bf16[144,1024]{1,0:T(8,128)(2,1)S(1)} collective-permute-done((bf16[144,1024]{1,0:T(8,128)(2,1)S(1)}, bf16[144,1024]{1,0:T(8,128)(2,1)S(1)}, u32[]{:S(2)}, u32[]{:S(2)}) %collective-permute-start.9) | collective-permute-done | bytes 294944 | tf_op jit(solution)/shard_map/ppermute | solution.py:675
  158.5 2.0 %finish.1 = f32[144,1024]{1,0:T(8,128)} custom-call(s32[4]{0:T(128)S(1)} %copy-done.6, bf16[1024,1024]{1,0:T(8,128)(2,1)S(1)} %broadcast_multiply_fusion.turn_ref, bf16[144,1024]{1,0:T(8,128)(2,1)S(1)} %get-tuple-element.73.own_ref, bf16[144,1024]{1,0:T(8,128)(2,1)S(1)} %collective-permute-done.7.near_ref, ...), custom_call_target="tpu_custom_call" | custom-call | flops 301989888 | bytes 3866632 | tf_op jit(solution)/shard_map/finish/pallas_call | solution.py:371
  (60 shorter events, 17.7 us)
Async XLA Ops:
  3.8 43.7 %all-to-all-start = ((bf16[8,256,768]{2,1,0:T(8,128)(2,1)}), bf16[8,256,768]{2,1,0:T(8,128)(2,1)S(1)}, u32[]{:S(2)}, u32[]{:S(2)}) async-start(bf16[8,256,768]{2,1,0:T(8,128)(2,1)} %pack_heads.1), calls=%async_computation | async-start | bytes 6291456 | tf_op jit(solution)/shard_map/all_to_all | solution.py:637
  9.9 37.7 %copy-start.5 = (s32[4]{0:T(128)}, s32[4]{0:T(128)S(1)}, u32[]{:S(2)}) copy-start(s32[4]{0:T(128)S(1)} %pad_add_fusion.place_ref) | copy-start | bytes 52
  9.9 1.7 %copy-start.2 = (bf16[1,1,256,4608]{3,2,1,0:T(8,128)(2,1)S(1)}, bf16[1,1,256,4608]{3,2,1,0:T(8,128)(2,1)}, u32[]{:S(2)}) copy-start(bf16[1,1,256,4608]{3,2,1,0:T(8,128)(2,1)} %param.11) | copy-start | bytes 7077892
  47.5 28.6 %copy-start.1 = (bf16[8,256,768]{2,1,0:T(8,128)(2,1)}, bf16[8,256,768]{2,1,0:T(8,128)(2,1)S(1)}, u32[]{:S(2)}) copy-start(bf16[8,256,768]{2,1,0:T(8,128)(2,1)S(1)} %all-to-all-done.own_ref.own_kv_ref) | copy-start | bytes 9437188
  47.5 1.5 copy-start.13
  47.5 4.4 %copy-start.11 = (bf16[2,576,256]{2,1,0:T(8,128)(2,1)S(1)}, bf16[2,576,256]{2,1,0:T(8,128)(2,1)}, u32[]{:S(2)}) copy-start(bf16[2,576,256]{2,1,0:T(8,128)(2,1)} %copy-done.10) | copy-start | bytes 1769476
  47.5 5.0 %copy-start.9 = (bf16[2,576,256]{2,1,0:T(8,128)(2,1)S(1)}, bf16[2,576,256]{2,1,0:T(8,128)(2,1)}, u32[]{:S(2)}) copy-start(bf16[2,576,256]{2,1,0:T(8,128)(2,1)} %copy-done.8) | copy-start | bytes 1769476
  47.6 7.9 %collective-permute-start = (bf16[8,256,256]{2,1,0:T(8,128)(2,1)S(1)}, bf16[8,256,256]{2,1,0:T(8,128)(2,1)S(1)}, u32[]{:S(2)}, u32[]{:S(2)}) collective-permute-start(bf16[8,256,256]{2,1,0:T(8,128)(2,1)S(1)} %slice.3), channel_id=1, source_target_pairs={{0,2},{2,0},{4,6},{6,4},{8,10},{10,8},{12,14},{14,12},{16,18},{18,... | collective-permute-start | bytes 3145736 | tf_op jit(solution)/shard_map/ppermute | solution.py:640
  48.9 31.7 %collective-permute-start.2 = (bf16[2,576,256]{2,1,0:T(8,128)(2,1)S(1)}, bf16[2,576,256]{2,1,0:T(8,128)(2,1)S(1)}, u32[]{:S(2)}, u32[]{:S(2)}) collective-permute-start(bf16[2,576,256]{2,1,0:T(8,128)(2,1)S(1)} %copy-done.13), channel_id=1, source_target_pairs={{0,8},{2,10},{4,12},{6,14},{8,0},{10,2},{12,4},{14,6},{16,24},{18,... | collective-permute-start | bytes 1769480 | tf_op jit(solution)/shard_map/ppermute | solution.py:640
  51.9 28.7 %collective-permute-start.3 = (bf16[2,576,256]{2,1,0:T(8,128)(2,1)S(1)}, bf16[2,576,256]{2,1,0:T(8,128)(2,1)S(1)}, u32[]{:S(2)}, u32[]{:S(2)}) collective-permute-start(bf16[2,576,256]{2,1,0:T(8,128)(2,1)S(1)} %copy-done.11), channel_id=1, source_target_pairs={{0,16},{2,18},{4,20},{6,22},{8,24},{10,26},{12,28},{14,30},{16,0},... | collective-permute-start | bytes 1769480 | tf_op jit(solution)/shard_map/ppermute | solution.py:640
  52.5 28.2 %collective-permute-start.4 = (bf16[2,576,256]{2,1,0:T(8,128)(2,1)S(1)}, bf16[2,576,256]{2,1,0:T(8,128)(2,1)S(1)}, u32[]{:S(2)}, u32[]{:S(2)}) collective-permute-start(bf16[2,576,256]{2,1,0:T(8,128)(2,1)S(1)} %copy-done.9), channel_id=1, source_target_pairs={{0,24},{2,26},{4,28},{6,30},{8,16},{10,18},{12,20},{14,22},{16,8},... | collective-permute-start | bytes 1769480 | tf_op jit(solution)/shard_map/ppermute | solution.py:640
  55.5 20.5 %copy-start.7 = (bf16[8,256,256]{2,1,0:T(8,128)(2,1)}, bf16[8,256,256]{2,1,0:T(8,128)(2,1)S(1)}, u32[]{:S(2)}) copy-start(bf16[8,256,256]{2,1,0:T(8,128)(2,1)S(1)} %collective-permute-done.other_ref) | copy-start | bytes 3145732
  77.2 3.4 %copy-start.15 = (f32[8,256,128]{2,1,0:T(8,128)}, f32[8,256,128]{2,1,0:T(8,128)S(1)}, u32[]{:S(2)}) copy-start(f32[8,256,128]{2,1,0:T(8,128)S(1)} %get-tuple-element.59.dk_ref) | copy-start | bytes 3145732
  77.2 1.9 %collective-permute-start.1 = (bf16[8,256,128]{2,1,0:T(8,128)(2,1)S(1)}, bf16[8,256,128]{2,1,0:T(8,128)(2,1)S(1)}, u32[]{:S(2)}, u32[]{:S(2)}) collective-permute-start(bf16[8,256,128]{2,1,0:T(8,128)(2,1)S(1)} %get-tuple-element.47), channel_id=1, source_target_pairs={{0,2},{2,0},{4,6},{6,4},{8,10},{10,8},{12,14},{14,12},{16,18},{18,... | collective-permute-start | bytes 1572872 | tf_op jit(solution)/shard_map/ppermute | solution.py:640
  82.5 31.4 %all-to-all-start.1 = ((bf16[8,4,256,128]{3,2,1,0:T(8,128)(2,1)}), bf16[8,4,256,128]{3,2,1,0:T(8,128)(2,1)S(1)}, u32[]{:S(2)}, u32[]{:S(2)}) async-start(bf16[8,4,256,128]{3,2,1,0:T(8,128)(2,1)} %bitcast.11), calls=%async_computation.1 | async-start | bytes 4194304 | tf_op jit(solution)/shard_map/all_to_all | solution.py:637
  105.9 2.1 %collective-permute-start.5 = (bf16[8,256,128]{2,1,0:T(8,128)(2,1)}, bf16[8,256,128]{2,1,0:T(8,128)(2,1)S(1)}, u32[]{:S(2)}, u32[]{:S(2)}) collective-permute-start(bf16[8,256,128]{2,1,0:T(8,128)(2,1)} %get-tuple-element.62), channel_id=1, source_target_pairs={{0,2},{2,0},{4,6},{6,4},{8,10},{10,8},{12,14},{14,12},{16,18},{18,... | collective-permute-start | bytes 1572872 | tf_op jit(solution)/shard_map/ppermute | solution.py:640
  113.9 1.4 copy-start.16
  115.3 25.7 %all-to-all-start.2 = ((bf16[8,256,384]{2,1,0:T(8,128)(2,1)}), bf16[8,256,384]{2,1,0:T(8,128)(2,1)S(1)}, u32[]{:S(2)}, u32[]{:S(2)}) async-start(bf16[8,256,384]{2,1,0:T(8,128)(2,1)} %pack_scores.1), calls=%async_computation.2 | async-start | bytes 3145728 | tf_op jit(solution)/shard_map/all_to_all | solution.py:637
  120.1 9.5 %copy-start.6 = (s32[4]{0:T(128)S(1)}, s32[4]{0:T(128)}, u32[]{:S(2)}) copy-start(s32[4]{0:T(128)} %copy-done.5) | copy-start | bytes 52
  126.5 3.1 %collective-permute-start.6 = (bf16[2,288,1024]{2,1,0:T(8,128)(2,1)}, bf16[2,288,1024]{2,1,0:T(8,128)(2,1)S(1)}, u32[]{:S(2)}, u32[]{:S(2)}) collective-permute-start(bf16[2,288,1024]{2,1,0:T(8,128)(2,1)} %get-tuple-element.65), channel_id=1, source_target_pairs={{0,2},{2,0},{4,6},{6,4},{8,10},{10,8},{12,14},{14,12},{16,18},{18,... | collective-permute-start | bytes 3538952 | tf_op jit(solution)/shard_map/ppermute | solution.py:640
  133.0 20.2 %collective-permute-start.7 = (bf16[144,1024]{1,0:T(8,128)(2,1)}, bf16[144,1024]{1,0:T(8,128)(2,1)S(1)}, u32[]{:S(2)}, u32[]{:S(2)}) collective-permute-start(bf16[144,1024]{1,0:T(8,128)(2,1)} %get-tuple-element.74), channel_id=1, source_target_pairs={{1,100},{3,110},{5,96},{7,106},{9,108},{11,102},{13,104},{15,98},{... | collective-permute-start | bytes 884744 | tf_op jit(solution)/shard_map/ppermute | solution.py:675
  139.3 13.9 %collective-permute-start.10 = (bf16[144,1024]{1,0:T(8,128)(2,1)}, bf16[144,1024]{1,0:T(8,128)(2,1)S(1)}, u32[]{:S(2)}, u32[]{:S(2)}) collective-permute-start(bf16[144,1024]{1,0:T(8,128)(2,1)} %get-tuple-element.77), channel_id=1, source_target_pairs={{1,101},{3,111},{5,97},{7,107},{9,109},{11,103},{13,105},{15,99},{... | collective-permute-start | bytes 884744 | tf_op jit(solution)/shard_map/ppermute | solution.py:675
  141.0 12.4 %collective-permute-start.8 = (bf16[144,1024]{1,0:T(8,128)(2,1)}, bf16[144,1024]{1,0:T(8,128)(2,1)S(1)}, u32[]{:S(2)}, u32[]{:S(2)}) collective-permute-start(bf16[144,1024]{1,0:T(8,128)(2,1)} %copy-done.14), channel_id=1, source_target_pairs={{1,96},{3,98},{5,100},{7,102},{9,104},{11,106},{13,108},{15,110},{... | collective-permute-start | bytes 884744 | tf_op jit(solution)/shard_map/ppermute | solution.py:675
  147.6 10.9 %collective-permute-start.9 = (bf16[144,1024]{1,0:T(8,128)(2,1)S(1)}, bf16[144,1024]{1,0:T(8,128)(2,1)S(1)}, u32[]{:S(2)}, u32[]{:S(2)}) collective-permute-start(bf16[144,1024]{1,0:T(8,128)(2,1)S(1)} %get-tuple-element.76), channel_id=1, source_target_pairs={{1,97},{3,99},{5,101},{7,103},{9,105},{11,107},{13,109},{15,111},{... | collective-permute-start | bytes 884744 | tf_op jit(solution)/shard_map/ppermute | solution.py:675
  (11 other events, 10.0 us)

commit v5 on v4

--- a/solution.py
+++ b/solution.py
@@ -501,9 +501,14 @@
                 for group in range(2):
                     high = to % 2 if group else to % 2 ^ core
                     low = place_ref[2] if group else 1 - place_ref[2]
-                    index = ((to // 2 * 2 + high) * 2 + low) * 2 + core
-                    piece = turned_s[pl.ds(pl.multiple_of(index * share, 16), share)]
-                    out_ref[group, core * share : (core + 1) * share] = piece
+                    for half in range(2):
+                        x = to // 2
+                        if core:
+                            x = jnp.where(place_ref[3] == half, x, 1 - x)
+                        index = (((x * 2 + high) * 2 + low) * 2 + core) * 2 + half
+                        at = (core * 2 + half) * share // 2
+                        piece = turned_s[pl.ds(pl.multiple_of(index * (share // 2), 16), share // 2)]
+                        out_ref[group, at : at + share // 2] = piece
 
     return small_call(
         kernel,
@@ -514,6 +519,7 @@
         place,
         input_rows,
         in_specs=[SCALAR, WHOLE],
+        vmem=60,
     )
 
 
@@ -524,7 +530,19 @@
 
     def kernel(place_ref, *refs):
         column_refs, back_ref = refs[:members], refs[members]
-        give_ref, keep_ref, value_ref = refs[members + 1 :]
+        give_ref, keep_ref, value_ref, x_s, sems = refs[members + 1 :]
+
+        @pl.when(pl.program_id(0) == 0)
+        def _():
+            copies = [
+                pltpu.make_async_copy(ref, x_s.at[d], sems.at[d])
+                for d, ref in enumerate(column_refs)
+            ]
+            for copy in copies:
+                copy.start()
+            for copy in copies:
+                copy.wait()
+
         member, core = place_ref[0], place_ref[1]
         v = [
             jnp.concatenate([back_ref[0, member ^ d], back_ref[1, member ^ d]], axis=1)
@@ -535,26 +553,28 @@
         for at in range(2):
             for out_ref, which_core in ((give_ref, 1 - core), (keep_ref, core)):
                 part = pl.ds(pl.multiple_of(which_core * share, 16), share)
-                x = jnp.concatenate([ref[at, part] for ref in column_refs], axis=1)
+                x = jnp.concatenate([x_s[d, at, part] for d in range(members)], axis=1)
                 out_ref[at] = dot(x, v, (1, 0)).astype(jnp.bfloat16)
 
-    once = pl.Buffered(1)
     halves = pl.BlockSpec((2, share, 2 * head), lambda g: (0, 0, g))
     return small_call(
         kernel,
         "input_product",
         [(2, share, heads * head)] * 2 + [(rows, heads * head)],
-        [],
+        [
+            pltpu.VMEM((members, 2, 2 * share, rows), jnp.bfloat16),
+            pltpu.SemaphoreType.DMA((members,)),
+        ],
         0,
         place,
         *columns,
         back,
         grid=(heads // 2,),
         in_specs=[SCALAR]
-        + [pl.BlockSpec((2, 2 * share, rows), lambda g: (0, 0, 0), pipeline_mode=once)] * members
+        + [pl.BlockSpec(memory_space=pltpu.HBM)] * members
         + [pl.BlockSpec((2, members, rows, head), lambda g: (g, 0, 0, 0))],
         out_specs=[halves, halves, pl.BlockSpec((rows, 2 * head), lambda g: (0, g))],
-        vmem=60,
+        vmem=28,
         moved=0,
     )
 
@@ -586,6 +606,7 @@
         keep,
         got,
         in_specs=[SCALAR, WHOLE, WHOLE],
+        vmem=60,
     )
 
 
@@ -677,10 +698,10 @@
     far = [((s, 1), (sections - 1 - s, 1)) for s in range(sections)]
     cross = [((s, 1), (sections - 1 - s, 0)) for s in range(sections)]
     cross += [((s, 0), (s, 1)) for s in range(sections)]
-    near_other = routed(cross_other, cross, (2, 6))
+    near_other = routed(cross_other, cross, (2, 6 ^ 8))
     other = routed(stay_other, far + [((s, 0), (s, 0)) for s in range(sections)], (2, 6))
     cross_own, second_own, scores_back = lax.optimization_barrier((cross_own, second_own, scores_back))
-    near_own = routed(cross_own, cross, (0, 0))
+    near_own = routed(cross_own, cross, (0, 8))
     far_own = routed(second_own, far, (0, 0))
     signs = lax.dynamic_index_in_dim(hadamard_signs, section, 0, keepdims=False)
     turn = jnp.asarray(hadamard(width), jnp.bfloat16) * signs.astype(jnp.bfloat16)[:, None]

time: 161 us -> 161 us (level)
  local copies, waits for them, and re-layouts: 13.5 us -> 9.15 us
  Pallas kernels: 58.9 us -> 62.2 us
  waiting for transfers between devices: 47.7 us -> 50.8 us
    unnamed x42, local copies, waits for them, and re-layouts: 13.4 us -> 9.08 us
    pallas_call x8, Pallas kernels: 19.7 us -> 23 us  [small_call(): pl.pallas_call(kernel, out_shape=kinds, in_specs=in_specs if in_specs is...]
    ppermute x4, waiting for transfers between devices: 5.3 us -> 7.7 us  [routed(): return lax.ppermute(block, axes, pairs)]
    ppermute x4, starting transfers between devices: 14.9 us -> 13.2 us  [routed(): return lax.ppermute(block, axes, pairs)]
  transfers between devices with their start and end apart: 14 -> 14, of which waited for: 8 -> 8; matrix products, arithmetic and copies ran while one was open for 2% -> 1% of each run, Pallas kernels for 34% -> 36%
where the time goes in v5:
time: 161 us; the launch traced here: 160 us
  Pallas kernels  62.2 us (39%)
  waiting for transfers between devices  50.8 us (32%)
  starting transfers between devices  35.6 us (22%)
  local copies, waits for them, and re-layouts  9.15 us (6%)
  other arithmetic  1.65 us (1%)
    pallas_call x2, Pallas kernels, attention_call(): pl.pallas_call(kernel, grid=(chips - first,), out_shape=[payload] + [shap...  39.2 us
    all_to_all x3, waiting for transfers between devices, across(): lax.all_to_all(block, 'ctx', 0, 0, tiled=True, axis_index_groups=same_core)  36.8 us
    pallas_call x8, Pallas kernels, small_call(): pl.pallas_call(kernel, out_shape=kinds, in_specs=in_specs if in_specs is...  23 us
    all_to_all x3, starting transfers between devices, across(): lax.all_to_all(block, 'ctx', 0, 0, tiled=True, axis_index_groups=same_core)  15.7 us
    ppermute x4, starting transfers between devices, routed(): return lax.ppermute(block, axes, pairs)  13.2 us
    unnamed x42, local copies, waits for them, and re-layouts  9.08 us
    ppermute x4, waiting for transfers between devices, routed(): return lax.ppermute(block, axes, pairs)  7.7 us
    ppermute x7, starting transfers between devices, swap(): return lax.ppermute(block, 'ctx', [(i, i ^ bits) for i in range(2 * chips)])  6.74 us
  transfers between devices with their start and end apart: 14, of which 8 were waited for; matrix products, arithmetic and copies ran while one was open for 1% of the time, Pallas kernels for 36%

profile of v5, /device:TPU:2, one launch (start us, length us, event | category | flops | bytes accessed | tf_op | source)
XLA Modules:
  0.0 160.2 jit_solution(2894523097660381486)
XLA Ops:
  0.6 3.2 %pack_heads.1 = bf16[8,256,768]{2,1,0:T(8,128)(2,1)} custom-call(bf16[256,2048]{1,0:T(8,128)(2,1)} %bitcast.23, bf16[256,2048]{1,0:T(8,128)(2,1)} %bitcast.24, bf16[256,1024]{1,0:T(8,128)(2,1)} %bitcast.26, bf16[256,1024]{1,0:T(8,128)(2,1)} %bitcast.27), custom_call_target="tpu_custom_call" | custom-call | bytes 6291456 | tf_op jit(solution)/shard_map/pack_heads/pallas_call | solution.py:371
  3.8 6.0 %all-to-all-start = ((bf16[8,256,768]{2,1,0:T(8,128)(2,1)}), bf16[8,256,768]{2,1,0:T(8,128)(2,1)S(1)}, u32[]{:S(2)}, u32[]{:S(2)}) async-start(bf16[8,256,768]{2,1,0:T(8,128)(2,1)} %pack_heads.1), calls=%async_computation | async-start | bytes 6291456 | tf_op jit(solution)/shard_map/all_to_all | solution.py:658
  10.4 3.8 %turn_input.1 = (bf16[2,576,256]{2,1,0:T(8,128)(2,1)}, bf16[2,576,256]{2,1,0:T(8,128)(2,1)}, bf16[2,576,256]{2,1,0:T(8,128)(2,1)}, bf16[2,576,256]{2,1,0:T(8,128)(2,1)}) custom-call(s32[4]{0:T(128)} %pad_add_fusion.place_ref, bf16[256,4608]{1,0:T(8,128)(2,1)} %bitcast.22), custom_call_target="tpu_custom_call" | custom-call | bytes 4718600 | tf_op jit(solution)/shard_map/turn_input/pallas_call | solution.py:371
  14.2 33.3 %all-to-all-done.own_ref.own_kv_ref = bf16[8,256,768]{2,1,0:T(8,128)(2,1)S(1)} async-done(((bf16[8,256,768]{2,1,0:T(8,128)(2,1)}), bf16[8,256,768]{2,1,0:T(8,128)(2,1)S(1)}, u32[]{:S(2)}, u32[]{:S(2)}) %all-to-all-start) | async-done | bytes 3145760 | tf_op jit(solution)/shard_map/all_to_all | solution.py:658
  48.9 3.0 %collective-permute-start.2 = (bf16[2,576,256]{2,1,0:T(8,128)(2,1)S(1)}, bf16[2,576,256]{2,1,0:T(8,128)(2,1)S(1)}, u32[]{:S(2)}, u32[]{:S(2)}) collective-permute-start(bf16[2,576,256]{2,1,0:T(8,128)(2,1)S(1)} %copy-done.20), channel_id=1, source_target_pairs={{0,8},{2,10},{4,12},{6,14},{8,0},{10,2},{12,4},{14,6},{16,24},{18,... | collective-permute-start | bytes 1769480 | tf_op jit(solution)/shard_map/ppermute | solution.py:661
  52.5 3.0 %collective-permute-start.4 = (bf16[2,576,256]{2,1,0:T(8,128)(2,1)S(1)}, bf16[2,576,256]{2,1,0:T(8,128)(2,1)S(1)}, u32[]{:S(2)}, u32[]{:S(2)}) collective-permute-start(bf16[2,576,256]{2,1,0:T(8,128)(2,1)S(1)} %copy-done.18), channel_id=1, source_target_pairs={{0,24},{2,26},{4,28},{6,30},{8,16},{10,18},{12,20},{14,22},{16,8},... | collective-permute-start | bytes 1769480 | tf_op jit(solution)/shard_map/ppermute | solution.py:661
  55.5 20.5 %value_gradients.1 = (bf16[8,256,384]{2,1,0:T(8,128)(2,1)S(1)}, f32[8,256,128]{2,1,0:T(8,128)S(1)}, bf16[8,256,128]{2,1,0:T(8,128)(2,1)S(1)}, bf16[8,256,128]{2,1,0:T(8,128)(2,1)S(1)}) custom-call(s32[1]{0:T(128)} %bitcast.1.parity_ref, bf16[8,256,768]{2,1,0:T(8,128)(2,1)S(1)} %all-to-all-done.own_ref.own_kv_ref, ...), custom_call_target="tpu_custom_call" | custom-call | flops 7516192768 | bytes 8388608 | tf_op jit(solution)/shard_map/value_gradients/pallas_call | solution.py:272
  76.2 1.9 %collective-permute-done.1 = bf16[8,256,128]{2,1,0:T(8,128)(2,1)S(1)} collective-permute-done((bf16[8,256,128]{2,1,0:T(8,128)(2,1)S(1)}, bf16[8,256,128]{2,1,0:T(8,128)(2,1)S(1)}, u32[]{:S(2)}, u32[]{:S(2)}) %collective-permute-start.1) | collective-permute-done | bytes 524320 | tf_op jit(solution)/shard_map/ppermute | solution.py:661
  82.3 4.9 %all-to-all-start.1 = ((bf16[8,4,256,128]{3,2,1,0:T(8,128)(2,1)}), bf16[8,4,256,128]{3,2,1,0:T(8,128)(2,1)S(1)}, u32[]{:S(2)}, u32[]{:S(2)}) async-start(bf16[8,4,256,128]{3,2,1,0:T(8,128)(2,1)} %bitcast.18), calls=%async_computation.1 | async-start | bytes 4194304 | tf_op jit(solution)/shard_map/all_to_all | solution.py:658
  87.2 18.7 %score_gradients.1 = (bf16[8,256,384]{2,1,0:T(8,128)(2,1)}, bf16[8,256,128]{2,1,0:T(8,128)(2,1)}, bf16[8,256,128]{2,1,0:T(8,128)(2,1)}) custom-call(s32[1]{0:T(128)} %bitcast.1.parity_ref, bf16[8,256,768]{2,1,0:T(8,128)(2,1)} %copy-done.2, bf16[8,256,768]{2,1,0:T(8,128)(2,1)} %copy-done.2, ...), custom_call_target="tpu_custom_call", output_to_operand_aliasing={{0}: (4, {})} | custom-call | flops 15032385536 | bytes 8388608 | tf_op jit(solution)/shard_map/score_gradients/pallas_call | solution.py:272
  105.9 2.1 %collective-permute-done.5.theirs_ref = bf16[8,256,128]{2,1,0:T(8,128)(2,1)S(1)} collective-permute-done((bf16[8,256,128]{2,1,0:T(8,128)(2,1)}, bf16[8,256,128]{2,1,0:T(8,128)(2,1)S(1)}, u32[]{:S(2)}, u32[]{:S(2)}) %collective-permute-start.5) | collective-permute-done | bytes 524320 | tf_op jit(solution)/shard_map/ppermute | solution.py:661
  108.9 2.0 %pack_scores.1 = bf16[8,256,384]{2,1,0:T(8,128)(2,1)} custom-call(bf16[8,256,384]{2,1,0:T(8,128)(2,1)} %get-tuple-element.60._, bf16[8,256,128]{2,1,0:T(8,128)(2,1)} %get-tuple-element.61.mine_ref, bf16[8,256,128]{2,1,0:T(8,128)(2,1)} %copy-done.17), custom_call_target="tpu_custom_call", output_to_operand_aliasing={{}: (0, {})} | custom-call | bytes 4194304 | tf_op jit(solution)/shard_map/pack_scores/pallas_call | solution.py:371
  110.8 3.1 %all-to-all-done.1.refs_4_ = bf16[8,4,256,128]{3,2,1,0:T(8,128)(2,1)S(1)} async-done(((bf16[8,4,256,128]{3,2,1,0:T(8,128)(2,1)}), bf16[8,4,256,128]{3,2,1,0:T(8,128)(2,1)S(1)}, u32[]{:S(2)}, u32[]{:S(2)}) %all-to-all-start.1) | async-done | bytes 2097184 | tf_op jit(solution)/shard_map/all_to_all | solution.py:658
  114.0 4.8 %all-to-all-start.2 = ((bf16[8,256,384]{2,1,0:T(8,128)(2,1)}), bf16[8,256,384]{2,1,0:T(8,128)(2,1)}, u32[]{:S(2)}, u32[]{:S(2)}) async-start(bf16[8,256,384]{2,1,0:T(8,128)(2,1)} %pack_scores.1), calls=%async_computation.2 | async-start | bytes 3145728 | tf_op jit(solution)/shard_map/all_to_all | solution.py:658
  120.9 5.2 %input_product.1 = (bf16[2,288,1024]{2,1,0:T(8,128)(2,1)}, bf16[2,288,1024]{2,1,0:T(8,128)(2,1)S(1)}, bf16[256,1024]{1,0:T(8,128)(2,1)}) custom-call(s32[4]{0:T(128)S(1)} %copy-done.12, bf16[2,576,256]{2,1,0:T(8,128)(2,1)S(1)} %copy-done.4, bf16[2,576,256]{2,1,0:T(8,128)(2,1)S(1)} %copy-done.6, bf16[2,576,256]{2,1,0:T(8,128)(2,1)S(1)} %copy-done.8, ...), custom_call_target="tpu_custom_call" | custom-call | tf_op jit(solution)/shard_map/input_product/pallas_call | solution.py:371
  127.9 2.3 %collective-permute-done.6 = bf16[2,288,1024]{2,1,0:T(8,128)(2,1)} collective-permute-done((bf16[2,288,1024]{2,1,0:T(8,128)(2,1)}, bf16[2,288,1024]{2,1,0:T(8,128)(2,1)}, u32[]{:S(2)}, u32[]{:S(2)}) %collective-permute-start.6) | collective-permute-done | bytes 1179680 | tf_op jit(solution)/shard_map/ppermute | solution.py:661
  130.2 2.9 %cut_pieces.1 = (bf16[144,1024]{1,0:T(8,128)(2,1)}, bf16[144,1024]{1,0:T(8,128)(2,1)}, bf16[144,1024]{1,0:T(8,128)(2,1)}, bf16[144,1024]{1,0:T(8,128)(2,1)}, bf16[144,1024]{1,0:T(8,128)(2,1)}) custom-call(s32[4]{0:T(128)} %pad_add_fusion.place_ref, bf16[2,2,144,1024]{3,2,1,0:T(8,128)(2,1)} %bitcast.19, bf16[2,2,144,1024]{3,2,1,0:T(8,128)(2,1)} %bitcast.13.got_ref), custom_call_target="tpu_custom_call" | custom-call | bytes 3833864 | tf_op jit(solution)/shard_map/cut_pieces/pallas_call | solution.py:371
  133.2 6.4 %collective-permute-start.7 = (bf16[144,1024]{1,0:T(8,128)(2,1)}, bf16[144,1024]{1,0:T(8,128)(2,1)S(1)}, u32[]{:S(2)}, u32[]{:S(2)}) collective-permute-start(bf16[144,1024]{1,0:T(8,128)(2,1)} %get-tuple-element.74), channel_id=1, source_target_pairs={{1,100},{3,126},{5,96},{7,122},{9,108},{11,118},{13,104},{15,114},... | collective-permute-start | bytes 884744 | tf_op jit(solution)/shard_map/ppermute | solution.py:696
  139.9 4.9 %collective-permute-start.8 = (bf16[144,1024]{1,0:T(8,128)(2,1)}, bf16[144,1024]{1,0:T(8,128)(2,1)S(1)}, u32[]{:S(2)}, u32[]{:S(2)}) collective-permute-start(bf16[144,1024]{1,0:T(8,128)(2,1)} %get-tuple-element.75), channel_id=1, source_target_pairs={{1,96},{3,114},{5,100},{7,118},{9,104},{11,122},{13,108},{15,126},... | collective-permute-start | bytes 884744 | tf_op jit(solution)/shard_map/ppermute | solution.py:696
  144.8 1.9 %collective-permute-start.9 = (bf16[144,1024]{1,0:T(8,128)(2,1)}, bf16[144,1024]{1,0:T(8,128)(2,1)S(1)}, u32[]{:S(2)}, u32[]{:S(2)}) collective-permute-start(bf16[144,1024]{1,0:T(8,128)(2,1)} %get-tuple-element.76), channel_id=1, source_target_pairs={{1,97},{3,99},{5,101},{7,103},{9,105},{11,107},{13,109},{15,111},{... | collective-permute-start | bytes 884744 | tf_op jit(solution)/shard_map/ppermute | solution.py:696
  146.9 3.6 %unpack_scores.1 = (bf16[256,2048]{1,0:T(8,128)(2,1)}, bf16[256,1024]{1,0:T(8,128)(2,1)}) custom-call(bf16[8,256,384]{2,1,0:T(8,128)(2,1)} %all-to-all-done.2.in_ref), custom_call_target="tpu_custom_call" | custom-call | bytes 3145728 | tf_op jit(solution)/shard_map/unpack_scores/pallas_call | solution.py:371
  150.6 2.5 %collective-permute-done.8.near2_ref = bf16[144,1024]{1,0:T(8,128)(2,1)S(1)} collective-permute-done((bf16[144,1024]{1,0:T(8,128)(2,1)}, bf16[144,1024]{1,0:T(8,128)(2,1)S(1)}, u32[]{:S(2)}, u32[]{:S(2)}) %collective-permute-start.8) | collective-permute-done | bytes 294944 | tf_op jit(solution)/shard_map/ppermute | solution.py:696
  153.1 5.2 %collective-permute-done.9.far_ref = bf16[144,1024]{1,0:T(8,128)(2,1)S(1)} collective-permute-done((bf16[144,1024]{1,0:T(8,128)(2,1)}, bf16[144,1024]{1,0:T(8,128)(2,1)S(1)}, u32[]{:S(2)}, u32[]{:S(2)}) %collective-permute-start.9) | collective-permute-done | bytes 294944 | tf_op jit(solution)/shard_map/ppermute | solution.py:696
  158.3 1.9 %finish.1 = f32[144,1024]{1,0:T(8,128)} custom-call(s32[4]{0:T(128)S(1)} %copy-done.13, bf16[1024,1024]{1,0:T(8,128)(2,1)S(1)} %broadcast_multiply_fusion.turn_ref, bf16[144,1024]{1,0:T(8,128)(2,1)S(1)} %copy-done.11, bf16[144,1024]{1,0:T(8,128)(2,1)S(1)} %collective-permute-done.7.near_ref, bf16[144,1024]{1,0:T(8,128)(2,1)S(1)} %collective-permute-done.8.near2_ref, ...), custom_call_target="tpu_custom_call" | custom-call | flops 301989888 | bytes 3866632 | tf_op jit(solution)/shard_map/finish/pallas_call | solution.py:371
  (60 shorter events, 12.3 us)
Async XLA Ops:
  3.8 43.7 %all-to-all-start = ((bf16[8,256,768]{2,1,0:T(8,128)(2,1)}), bf16[8,256,768]{2,1,0:T(8,128)(2,1)S(1)}, u32[]{:S(2)}, u32[]{:S(2)}) async-start(bf16[8,256,768]{2,1,0:T(8,128)(2,1)} %pack_heads.1), calls=%async_computation | async-start | bytes 6291456 | tf_op jit(solution)/shard_map/all_to_all | solution.py:658
  47.5 28.6 %copy-start.2 = (bf16[8,256,768]{2,1,0:T(8,128)(2,1)}, bf16[8,256,768]{2,1,0:T(8,128)(2,1)S(1)}, u32[]{:S(2)}) copy-start(bf16[8,256,768]{2,1,0:T(8,128)(2,1)S(1)} %all-to-all-done.own_ref.own_kv_ref) | copy-start | bytes 9437188
  47.5 5.0 %copy-start.18 = (bf16[2,576,256]{2,1,0:T(8,128)(2,1)S(1)}, bf16[2,576,256]{2,1,0:T(8,128)(2,1)}, u32[]{:S(2)}) copy-start(bf16[2,576,256]{2,1,0:T(8,128)(2,1)} %get-tuple-element.51) | copy-start | bytes 1769476
  47.6 8.0 %collective-permute-start = (bf16[8,256,256]{2,1,0:T(8,128)(2,1)S(1)}, bf16[8,256,256]{2,1,0:T(8,128)(2,1)S(1)}, u32[]{:S(2)}, u32[]{:S(2)}) collective-permute-start(bf16[8,256,256]{2,1,0:T(8,128)(2,1)S(1)} %slice.3), channel_id=1, source_target_pairs={{0,2},{2,0},{4,6},{6,4},{8,10},{10,8},{12,14},{14,12},{16,18},{18,... | collective-permute-start | bytes 3145736 | tf_op jit(solution)/shard_map/ppermute | solution.py:661
  48.9 30.9 %collective-permute-start.2 = (bf16[2,576,256]{2,1,0:T(8,128)(2,1)S(1)}, bf16[2,576,256]{2,1,0:T(8,128)(2,1)S(1)}, u32[]{:S(2)}, u32[]{:S(2)}) collective-permute-start(bf16[2,576,256]{2,1,0:T(8,128)(2,1)S(1)} %copy-done.20), channel_id=1, source_target_pairs={{0,8},{2,10},{4,12},{6,14},{8,0},{10,2},{12,4},{14,6},{16,24},{18,... | collective-permute-start | bytes 1769480 | tf_op jit(solution)/shard_map/ppermute | solution.py:661
  51.9 28.8 %collective-permute-start.3 = (bf16[2,576,256]{2,1,0:T(8,128)(2,1)S(1)}, bf16[2,576,256]{2,1,0:T(8,128)(2,1)S(1)}, u32[]{:S(2)}, u32[]{:S(2)}) collective-permute-start(bf16[2,576,256]{2,1,0:T(8,128)(2,1)S(1)} %copy-done.19), channel_id=1, source_target_pairs={{0,16},{2,18},{4,20},{6,22},{8,24},{10,26},{12,28},{14,30},{16,0},... | collective-permute-start | bytes 1769480 | tf_op jit(solution)/shard_map/ppermute | solution.py:661
  52.5 29.0 %collective-permute-start.4 = (bf16[2,576,256]{2,1,0:T(8,128)(2,1)S(1)}, bf16[2,576,256]{2,1,0:T(8,128)(2,1)S(1)}, u32[]{:S(2)}, u32[]{:S(2)}) collective-permute-start(bf16[2,576,256]{2,1,0:T(8,128)(2,1)S(1)} %copy-done.18), channel_id=1, source_target_pairs={{0,24},{2,26},{4,28},{6,30},{8,16},{10,18},{12,20},{14,22},{16,8},... | collective-permute-start | bytes 1769480 | tf_op jit(solution)/shard_map/ppermute | solution.py:661
  55.5 20.5 %copy-start.14 = (bf16[8,256,256]{2,1,0:T(8,128)(2,1)}, bf16[8,256,256]{2,1,0:T(8,128)(2,1)S(1)}, u32[]{:S(2)}) copy-start(bf16[8,256,256]{2,1,0:T(8,128)(2,1)S(1)} %collective-permute-done.other_ref) | copy-start | bytes 3145732
  76.1 5.5 %copy-start.15 = (f32[8,256,128]{2,1,0:T(8,128)}, f32[8,256,128]{2,1,0:T(8,128)S(1)}, u32[]{:S(2)}) copy-start(f32[8,256,128]{2,1,0:T(8,128)S(1)} %get-tuple-element.59.dk_ref) | copy-start | bytes 3145732
  76.1 2.0 %collective-permute-start.1 = (bf16[8,256,128]{2,1,0:T(8,128)(2,1)S(1)}, bf16[8,256,128]{2,1,0:T(8,128)(2,1)S(1)}, u32[]{:S(2)}, u32[]{:S(2)}) collective-permute-start(bf16[8,256,128]{2,1,0:T(8,128)(2,1)S(1)} %get-tuple-element.47), channel_id=1, source_target_pairs={{0,2},{2,0},{4,6},{6,4},{8,10},{10,8},{12,14},{14,12},{16,18},{18,... | collective-permute-start | bytes 1572872 | tf_op jit(solution)/shard_map/ppermute | solution.py:661
  82.3 31.6 %all-to-all-start.1 = ((bf16[8,4,256,128]{3,2,1,0:T(8,128)(2,1)}), bf16[8,4,256,128]{3,2,1,0:T(8,128)(2,1)S(1)}, u32[]{:S(2)}, u32[]{:S(2)}) async-start(bf16[8,4,256,128]{3,2,1,0:T(8,128)(2,1)} %bitcast.18), calls=%async_computation.1 | async-start | bytes 4194304 | tf_op jit(solution)/shard_map/all_to_all | solution.py:658
  105.9 2.1 %collective-permute-start.5 = (bf16[8,256,128]{2,1,0:T(8,128)(2,1)}, bf16[8,256,128]{2,1,0:T(8,128)(2,1)S(1)}, u32[]{:S(2)}, u32[]{:S(2)}) collective-permute-start(bf16[8,256,128]{2,1,0:T(8,128)(2,1)} %get-tuple-element.62), channel_id=1, source_target_pairs={{0,2},{2,0},{4,6},{6,4},{8,10},{10,8},{12,14},{14,12},{16,18},{18,... | collective-permute-start | bytes 1572872 | tf_op jit(solution)/shard_map/ppermute | solution.py:661
  110.8 7.9 %copy-start.4 = (bf16[2,576,256]{2,1,0:T(8,128)(2,1)S(1)}, bf16[2,576,256]{2,1,0:T(8,128)(2,1)}, u32[]{:S(2)}) copy-start(bf16[2,576,256]{2,1,0:T(8,128)(2,1)} %get-tuple-element.52.refs_0_) | copy-start | bytes 1769476
  110.8 7.9 %copy-start.6 = (bf16[2,576,256]{2,1,0:T(8,128)(2,1)S(1)}, bf16[2,576,256]{2,1,0:T(8,128)(2,1)}, u32[]{:S(2)}) copy-start(bf16[2,576,256]{2,1,0:T(8,128)(2,1)} %copy-done.5) | copy-start | bytes 1769476
  110.8 7.9 %copy-start.12 = (s32[4]{0:T(128)S(1)}, s32[4]{0:T(128)}, u32[]{:S(2)}) copy-start(s32[4]{0:T(128)} %pad_add_fusion.place_ref) | copy-start | bytes 52
  114.0 25.9 %all-to-all-start.2 = ((bf16[8,256,384]{2,1,0:T(8,128)(2,1)}), bf16[8,256,384]{2,1,0:T(8,128)(2,1)}, u32[]{:S(2)}, u32[]{:S(2)}) async-start(bf16[8,256,384]{2,1,0:T(8,128)(2,1)} %pack_scores.1), calls=%async_computation.2 | async-start | bytes 3145728 | tf_op jit(solution)/shard_map/all_to_all | solution.py:658
  127.0 19.7 %copy-start.16 = (bf16[1024,1024]{1,0:T(8,128)(2,1)S(1)}, bf16[1024,1024]{1,0:T(8,128)(2,1)}, u32[]{:S(2)}) copy-start(bf16[1024,1024]{1,0:T(8,128)(2,1)} %constant.28.clone) | copy-start | bytes 6291460
  127.1 3.2 %collective-permute-start.6 = (bf16[2,288,1024]{2,1,0:T(8,128)(2,1)}, bf16[2,288,1024]{2,1,0:T(8,128)(2,1)}, u32[]{:S(2)}, u32[]{:S(2)}) collective-permute-start(bf16[2,288,1024]{2,1,0:T(8,128)(2,1)} %get-tuple-element.65), channel_id=1, source_target_pairs={{0,2},{2,0},{4,6},{6,4},{8,10},{10,8},{12,14},{14,12},{16,18},{18,... | collective-permute-start | bytes 3538952 | tf_op jit(solution)/shard_map/ppermute | solution.py:661
  133.2 17.4 %collective-permute-start.7 = (bf16[144,1024]{1,0:T(8,128)(2,1)}, bf16[144,1024]{1,0:T(8,128)(2,1)S(1)}, u32[]{:S(2)}, u32[]{:S(2)}) collective-permute-start(bf16[144,1024]{1,0:T(8,128)(2,1)} %get-tuple-element.74), channel_id=1, source_target_pairs={{1,100},{3,126},{5,96},{7,122},{9,108},{11,118},{13,104},{15,114},... | collective-permute-start | bytes 884744 | tf_op jit(solution)/shard_map/ppermute | solution.py:696
  139.5 11.0 %collective-permute-start.10 = (bf16[144,1024]{1,0:T(8,128)(2,1)}, bf16[144,1024]{1,0:T(8,128)(2,1)S(1)}, u32[]{:S(2)}, u32[]{:S(2)}) collective-permute-start(bf16[144,1024]{1,0:T(8,128)(2,1)} %get-tuple-element.77), channel_id=1, source_target_pairs={{1,101},{3,111},{5,97},{7,107},{9,109},{11,103},{13,105},{15,99},{... | collective-permute-start | bytes 884744 | tf_op jit(solution)/shard_map/ppermute | solution.py:696
  139.9 18.4 %copy-start.11 = (bf16[144,1024]{1,0:T(8,128)(2,1)S(1)}, bf16[144,1024]{1,0:T(8,128)(2,1)}, u32[]{:S(2)}) copy-start(bf16[144,1024]{1,0:T(8,128)(2,1)} %get-tuple-element.73.own_ref) | copy-start | bytes 884740
  139.9 18.4 %copy-start.13 = (s32[4]{0:T(128)S(1)}, s32[4]{0:T(128)}, u32[]{:S(2)}) copy-start(s32[4]{0:T(128)} %pad_add_fusion.place_ref) | copy-start | bytes 52
  139.9 13.1 %collective-permute-start.8 = (bf16[144,1024]{1,0:T(8,128)(2,1)}, bf16[144,1024]{1,0:T(8,128)(2,1)S(1)}, u32[]{:S(2)}, u32[]{:S(2)}) collective-permute-start(bf16[144,1024]{1,0:T(8,128)(2,1)} %get-tuple-element.75), channel_id=1, source_target_pairs={{1,96},{3,114},{5,100},{7,118},{9,104},{11,122},{13,108},{15,126},... | collective-permute-start | bytes 884744 | tf_op jit(solution)/shard_map/ppermute | solution.py:696
  144.8 13.5 %collective-permute-start.9 = (bf16[144,1024]{1,0:T(8,128)(2,1)}, bf16[144,1024]{1,0:T(8,128)(2,1)S(1)}, u32[]{:S(2)}, u32[]{:S(2)}) collective-permute-start(bf16[144,1024]{1,0:T(8,128)(2,1)} %get-tuple-element.76), channel_id=1, source_target_pairs={{1,97},{3,99},{5,101},{7,103},{9,105},{11,107},{13,109},{15,111},{... | collective-permute-start | bytes 884744 | tf_op jit(solution)/shard_map/ppermute | solution.py:696
  (11 other events, 16.1 us)
